TPU v7x, 32 devices: a whole 2x2x4 slice. The times are simulated.
32 devices in a mesh: wide: 32 (over z, y, x, core), narrow: 1.
Axes of the slice: x: 2, y: 2, z: 4, core: 2. Of those that a mesh axis runs over, the one named last changes fastest.
Arguments:
- tokens: bfloat16 [768, 4096], P('wide', 'narrow'), may hold values from -6 to 6
- grad_out: bfloat16 [768, 4096], P('wide', 'narrow'), may hold values from -1.1953125 to 1.1953125
- expert_ids: int32 [768, 8], P('wide'), may hold values from 0 to 31, all different within a row; in each aligned block of 24 rows (0 to 23, 24 to 47, ...) at most 12 rows name the same one
- route_weights: bfloat16 [768, 8], P('wide'), may hold values from 0.049804688 to 1
- w_gate: bfloat16 [32, 4096, 1536], P('wide', None, 'narrow'), may hold values from -0.09375 to 0.09375
- w_up: bfloat16 [32, 4096, 1536], P('wide', None, 'narrow'), may hold values from -0.09375 to 0.09375
- w_down: bfloat16 [32, 1536, 4096], P('wide', 'narrow'), may hold values from -0.15625 to 0.15625
Outputs:
- grad_tokens: bfloat16 [768, 4096], P('wide', 'narrow')
- grad_route: bfloat16 [768, 8], P('wide')
- grad_down: bfloat16 [32, 1536, 4096], P('wide', 'narrow')
Inputs may be any that keep to these rules, and one draw needn't show every extreme that they name: `expert_ids`: each row names 8 different experts. In each aligned block of 24 rows (the tokens of one index of wide) no expert is named by more than 12 rows, a bound that some block reaches.
All inputs are finite; a program needn't handle non-finite values.
Results may differ from a plain program's by a relative error of at most 0.019.
Values may be sent and summed in bfloat16 or wider, within the bound.
No kernel may reach another device: no remote copies, remote signals or barrier semaphores. Data moves between devices by JAX's collectives and lax.ppermute only.
A program may use at most 128 MiB of HBM per device.

v0:
```python
import functools

import jax
import jax.numpy as jnp
from jax import lax
from jax.experimental import pallas as pl
from jax.experimental.pallas import tpu as pltpu
from jax.sharding import PartitionSpec as P

LANES = 128
CHUNKS = 2
bf16, f32 = jnp.bfloat16, jnp.float32


def dot(a, b, dims):
    return lax.dot_general(a, b, ((dims[0], dims[1]), ((), ())), preferred_element_type=f32)


def add(*terms):
    total = terms[0].astype(f32)
    for term in terms[1:]:
        total = total + term.astype(f32)
    return total.astype(terms[0].dtype)


def tile(size, most):
    fits = [t for t in range(LANES, min(size, most) + 1, LANES) if size % t == 0]
    return fits[-1] if fits else size


def call(kernel, flops, moved, **kwargs):
    return pl.pallas_call(
        kernel,
        compiler_params=pltpu.CompilerParams(vmem_limit_bytes=52 * 1024 * 1024),
        cost_estimate=pl.CostEstimate(flops=flops, bytes_accessed=moved, transcendentals=0),
        **kwargs,
    )


def whole(*shape):
    return pl.BlockSpec(shape, lambda i: (0,) * len(shape))


CORE, X, Y, Z = 1, 2, 4, 8


def flip(value, mask):
    count = lax.axis_size("wide")
    return lax.ppermute(value, "wide", [(i, i ^ mask) for i in range(count)])


def after(value, *deps):
    return lax.optimization_barrier((value, *deps))[0]


def depth():
    return lax.axis_size("wide") // Z


def gather_z(shard):
    return jnp.concatenate([shard] + [flip(shard, Z * k) for k in range(1, depth())], axis=0)


def gather_sides(first):
    return flip(first, X), flip(first, Y)


def gather_far(by_x, by_y):
    half = by_x.shape[0] // 2
    return [flip(by_y[:half], X), flip(by_x[half:], Y)]


def gather_core(pieces):
    return pieces + [flip(piece, CORE) for piece in pieces]


def offsets():
    return [Z * k + m + c for c in (0, CORE) for m in (0, X, Y, X | Y) for k in range(depth())]


def quarters(mine):
    size = mine.shape[0] // 4
    return [mine[k * size : (k + 1) * size] for k in range(4)]


def scatter_far(mine):
    first, by_x, by_y, far = quarters(mine)
    half = far.shape[0] // 2
    to_y, to_x = flip(far[:half], X), flip(far[half:], Y)
    by_y = jnp.concatenate([add(by_y[:half], to_y), by_y[half:]], axis=0)
    by_x = jnp.concatenate([by_x[:half], add(by_x[half:], to_x)], axis=0)
    return first, by_x, by_y


def scatter_sides(first, by_x, by_y):
    return add(first, flip(by_x, X), flip(by_y, Y))


def scatter_z(first):
    step = first.shape[0] // depth()
    blocks = [first[k * step : (k + 1) * step] for k in range(depth())]
    return add(blocks[0], *[flip(blocks[k], Z * k) for k in range(1, depth())])


def meta_kernel(sizes, cols, *refs):
    pieces, (out_ref, sems) = refs[: len(sizes)], refs[len(sizes) :]
    starts = [sum(sizes[:k]) for k in range(len(sizes))]
    copies = [
        pltpu.make_async_copy(
            pieces[k].at[:, pl.ds(cols, LANES)], out_ref.at[pl.ds(starts[k], sizes[k]), :], sems.at[k]
        )
        for k in range(len(sizes))
    ]
    for copy in copies:
        copy.start()
    for copy in copies:
        copy.wait()


def gather_meta(pieces, cols):
    sizes = [piece.shape[0] for piece in pieces]
    return call(
        functools.partial(meta_kernel, sizes, cols),
        0,
        4 * sum(sizes) * LANES,
        grid=(1,),
        in_specs=[pl.BlockSpec(memory_space=pl.ANY)] * len(pieces),
        out_specs=whole(sum(sizes), LANES),
        out_shape=jax.ShapeDtypeStruct((sum(sizes), LANES), bf16),
        scratch_shapes=[pltpu.SemaphoreType.DMA((len(sizes),))],
    )(*pieces)


def pick_kernel(sizes, block, slot_ref, *refs):
    pieces, (out_ref, held, place, sems) = refs[: len(sizes)], refs[len(sizes) :]
    step = pl.program_id(0)
    starts = [sum(sizes[:k]) for k in range(len(sizes))]

    def copy(at, k):
        return pltpu.make_async_copy(
            pieces[k].at[:, pl.ds(pl.multiple_of(at * block, LANES), block)],
            held.at[at, pl.ds(starts[k], sizes[k]), :],
            sems.at[at, k],
        )

    @pl.when(step == 0)
    def _():
        @pl.loop(0, pl.num_programs(0))
        def _(at):
            for k in range(len(sizes)):
                copy(at, k).start()

        rows = lax.broadcasted_iota(jnp.int32, place.shape, 0)
        place[...] = jnp.where(rows == slot_ref[...], 1.0, 0.0).astype(bf16)

    for k in range(len(sizes)):
        copy(step, k).wait()
    out_ref[...] = dot(place[...], held[step], ((1,), (0,))).astype(bf16)


def pick_rows(slot, pieces, rows, cols):
    sizes = [piece.shape[0] for piece in pieces]
    total = sum(sizes)
    block = tile(cols, 512)
    steps = cols // block
    return call(
        functools.partial(pick_kernel, sizes, block),
        2 * rows * total * cols,
        2 * (rows + total) * cols,
        grid=(steps,),
        in_specs=[whole(1, total)] + [pl.BlockSpec(memory_space=pl.ANY)] * len(pieces),
        out_specs=pl.BlockSpec((rows, block), lambda i: (0, i)),
        out_shape=jax.ShapeDtypeStruct((rows, cols), bf16),
        scratch_shapes=[
            pltpu.VMEM((steps, total, block), bf16),
            pltpu.VMEM((rows, total), bf16),
            pltpu.SemaphoreType.DMA((steps, len(sizes))),
        ],
    )(slot.reshape(1, total), *pieces)


def forward_kernel(x_ref, gate_ref, up_ref, hidden_ref, turned_ref, active_ref, pull_ref):
    gate_pre = dot(x_ref[...], gate_ref[...], ((1,), (0,)))
    up_pre = dot(x_ref[...], up_ref[...], ((1,), (0,)))
    sig = jax.nn.sigmoid(gate_pre)
    active = gate_pre * sig
    hidden = active * up_pre
    hidden_ref[...] = hidden.astype(bf16)
    turned_ref[...] = hidden.T.astype(bf16)
    active_ref[...] = active.astype(bf16)
    pull_ref[...] = (up_pre * (sig * (1.0 + gate_pre * (1.0 - sig)))).astype(bf16)


def forward(x, w_gate, w_up, part, parts):
    rows, width = x.shape
    units = w_gate.shape[1] // parts
    block = tile(units, 256)
    first = part * (units // block)
    weight = pl.BlockSpec((width, block), lambda i: (0, first + i))
    unit = pl.BlockSpec((rows, block), lambda i: (0, i))
    turned = pl.BlockSpec((block, rows), lambda i: (i, 0))
    shape = jax.ShapeDtypeStruct((rows, units), bf16)
    return call(
        forward_kernel,
        4 * rows * width * units,
        4 * width * units,
        grid=(units // block,),
        in_specs=[whole(rows, width), weight, weight],
        out_specs=[unit, turned, unit, unit],
        out_shape=[shape, jax.ShapeDtypeStruct((units, rows), bf16), shape, shape],
    )(x, w_gate, w_up)


def back_kernel(steps, g_ref, gain_ref, down_ref, *refs):
    parts, (d_gate_ref, d_up_ref, route_ref) = refs[:-3], refs[-3:]
    step = pl.program_id(0)
    back = dot(g_ref[...], down_ref[...], ((1,), (1,)))
    d_hidden = gain_ref[...] * back

    @pl.when(step == 0)
    def _():
        route_ref[...] = jnp.zeros_like(route_ref)

    for k in range(len(parts) // 3):
        hidden_ref, active_ref, pull_ref = parts[3 * k : 3 * k + 3]

        @pl.when((step >= k * steps) & (step < (k + 1) * steps))
        def _(hidden_ref=hidden_ref, active_ref=active_ref, pull_ref=pull_ref):
            d_gate_ref[...] = (d_hidden * pull_ref[...].astype(f32)).astype(bf16)
            d_up_ref[...] = (d_hidden * active_ref[...].astype(f32)).astype(bf16)
            route_ref[...] += jnp.sum(hidden_ref[...].astype(f32) * back, axis=1, keepdims=True)


def back_project(g, gain, w_down, parts):
    rows, width = g.shape
    units = w_down.shape[0]
    block = tile(parts[0][0].shape[1], 256)
    steps = units // block // len(parts)
    unit = pl.BlockSpec((rows, block), lambda i: (0, i))

    def unit_of(part):
        return pl.BlockSpec((rows, block), lambda i: (0, jnp.clip(i - part * steps, 0, steps - 1)))

    shape = jax.ShapeDtypeStruct((rows, units), bf16)
    return call(
        functools.partial(back_kernel, steps),
        2 * rows * width * units,
        2 * width * units,
        grid=(units // block,),
        in_specs=[
            whole(rows, width),
            whole(rows, 1),
            pl.BlockSpec((block, width), lambda i: (i, 0)),
        ]
        + [unit_of(k) for k in range(len(parts)) for _ in range(3)],
        out_specs=[unit, unit, whole(rows, 1)],
        out_shape=[shape, shape, jax.ShapeDtypeStruct((rows, 1), f32)],
    )(g, gain, w_down, *[array for part in parts for array in part])


ANY = pl.BlockSpec(memory_space=pl.ANY)


def pick_phase(sizes, picks, blocks, slot_ref, pieces, x_out, scratch, weights):
    held, place, x, piece_sems, x_sems = scratch
    step = pl.program_id(0)
    width = held.shape[2]
    starts = [sum(sizes[:k]) for k in range(len(sizes))]

    def columns(at):
        return pl.ds(pl.multiple_of(at * width, LANES), width)

    def loads(at):
        return [
            pltpu.make_async_copy(
                pieces[k].at[:, columns(at)],
                held.at[at, pl.ds(starts[k], sizes[k]), :],
                piece_sems.at[at, k],
            )
            for k in range(len(sizes))
        ]

    def store(at):
        return pltpu.make_async_copy(x.at[:, columns(at)], x_out.at[:, columns(at)], x_sems.at[at])

    @pl.when(step == 0)
    def _():
        for at in range(min(2, picks)):
            for copy in loads(at):
                copy.start()
        rows = lax.broadcasted_iota(jnp.int32, place.shape, 0)
        place[...] = jnp.where(rows == slot_ref[...], 1.0, 0.0).astype(bf16)

    @pl.when(step + 2 < picks)
    def _():
        for copy in loads(step + 2):
            copy.start()

    @pl.when((step >= 1) & (step <= blocks))
    def _():
        for copy in weights(step - 1):
            copy.start()

    @pl.when(step < picks)
    def _():
        for copy in loads(step):
            copy.wait()
        x[:, columns(step)] = dot(place[...], held[step], ((1,), (0,))).astype(bf16)
        store(step).start()

    @pl.when(step == picks + blocks - 1)
    def _():
        for at in range(picks):
            store(at).wait()

    return x


def pick_scratch(rows, sizes, cols):
    block = tile(cols, 1024)
    picks = cols // block
    return picks, [
        pltpu.VMEM((picks, sum(sizes), block), bf16),
        pltpu.VMEM((rows, sum(sizes)), bf16),
        pltpu.VMEM((rows, cols), bf16),
        pltpu.SemaphoreType.DMA((picks, len(sizes))),
        pltpu.SemaphoreType.DMA((picks,)),
    ]


def pick_forward_kernel(sizes, picks, blocks, slot_ref, *refs):
    count = len(sizes)
    pieces, (gate_any, up_any, x_out, hidden_ref, turned_ref, active_ref, pull_ref) = refs[:count], refs[count : count + 7]
    *scratch, gates, ups, sems = refs[count + 7 :]
    step = pl.program_id(0)
    width = gates.shape[2]

    def weights(at):
        source = pl.ds(pl.multiple_of(at * width, LANES), width)
        return [
            pltpu.make_async_copy(gate_any.at[:, source], gates.at[at], sems.at[0, at]),
            pltpu.make_async_copy(up_any.at[:, source], ups.at[at], sems.at[1, at]),
        ]

    x = pick_phase(sizes, picks, blocks, slot_ref, pieces, x_out, scratch, weights)

    @pl.when(step >= picks)
    def _():
        at = step - picks
        for copy in weights(at):
            copy.wait()
        forward_kernel(x, gates.at[at], ups.at[at], hidden_ref, turned_ref, active_ref, pull_ref)


def pick_forward(slot, pieces, rows, w_gate, w_up, parts):
    sizes = [piece.shape[0] for piece in pieces]
    cols, units = w_gate.shape[0], w_gate.shape[1] // parts
    picks, scratch = pick_scratch(rows, sizes, cols)
    block = tile(units, 256)
    blocks = units // block
    unit = pl.BlockSpec((rows, block), lambda i: (0, jnp.maximum(i - picks, 0)))
    turned = pl.BlockSpec((block, rows), lambda i: (jnp.maximum(i - picks, 0), 0))
    shape = jax.ShapeDtypeStruct((rows, units), bf16)
    x, *ahead = call(
        functools.partial(pick_forward_kernel, sizes, picks, blocks),
        4 * rows * cols * units + 2 * rows * sum(sizes) * cols,
        4 * cols * units + 2 * (rows + sum(sizes)) * cols,
        grid=(picks + blocks,),
        in_specs=[whole(1, sum(sizes))] + [ANY] * (len(sizes) + 2),
        out_specs=[ANY, unit, turned, unit, unit],
        out_shape=[
            jax.ShapeDtypeStruct((rows, cols), bf16),
            shape,
            jax.ShapeDtypeStruct((units, rows), bf16),
            shape,
            shape,
        ],
        scratch_shapes=scratch
        + [pltpu.VMEM((blocks, cols, block), bf16)] * 2
        + [pltpu.SemaphoreType.DMA((2, blocks))],
    )(slot.reshape(1, sum(sizes)), *pieces, w_gate, w_up)
    return x, ahead


def pick_back_kernel(sizes, picks, blocks, steps, slot_ref, gain_ref, *refs):
    count = len(sizes)
    pieces, down_any, refs = refs[:count], refs[count], refs[count + 1 :]
    *refs, held, place, rows_ref, piece_sems, x_sems, downs, sems = refs
    *parts, g_out, d_gate_ref, d_up_ref, route_ref = refs
    step = pl.program_id(0)
    width = downs.shape[1]

    def weights(at):
        source = down_any.at[pl.ds(pl.multiple_of(at * width, LANES), width), :]
        return [pltpu.make_async_copy(source, downs.at[at], sems.at[at])]

    scratch = (held, place, rows_ref, piece_sems, x_sems)
    g = pick_phase(sizes, picks, blocks, slot_ref, pieces, g_out, scratch, weights)

    @pl.when(step == 0)
    def _():
        route_ref[...] = jnp.zeros_like(route_ref)

    for k in range(len(parts) // 3):
        hidden_ref, active_ref, pull_ref = parts[3 * k : 3 * k + 3]

        @pl.when((step >= picks + k * steps) & (step < picks + (k + 1) * steps))
        def _(hidden_ref=hidden_ref, active_ref=active_ref, pull_ref=pull_ref):
            at = step - picks
            for copy in weights(at):
                copy.wait()
            back = dot(g[...], downs[at], ((1,), (1,)))
            d_hidden = gain_ref[...] * back
            d_gate_ref[...] = (d_hidden * pull_ref[...].astype(f32)).astype(bf16)
            d_up_ref[...] = (d_hidden * active_ref[...].astype(f32)).astype(bf16)
            route_ref[...] += jnp.sum(hidden_ref[...].astype(f32) * back, axis=1, keepdims=True)


def pick_back(slot, pieces, gain, w_down, parts):
    sizes = [piece.shape[0] for piece in pieces]
    rows = gain.shape[0]
    units, cols = w_down.shape
    picks, scratch = pick_scratch(rows, sizes, cols)
    block = tile(parts[0][0].shape[1], 256)
    blocks = units // block
    steps = blocks // len(parts)
    unit = pl.BlockSpec((rows, block), lambda i: (0, jnp.maximum(i - picks, 0)))

    def unit_of(part):
        return pl.BlockSpec((rows, block), lambda i: (0, jnp.clip(i - picks - part * steps, 0, steps - 1)))

    shape = jax.ShapeDtypeStruct((rows, units), bf16)
    return call(
        functools.partial(pick_back_kernel, sizes, picks, blocks, steps),
        2 * rows * cols * units + 2 * rows * sum(sizes) * cols,
        2 * cols * units + 2 * (rows + sum(sizes)) * cols,
        grid=(picks + blocks,),
        in_specs=[whole(1, sum(sizes)), whole(rows, 1)]
        + [ANY] * (len(sizes) + 1)
        + [unit_of(k) for k in range(len(parts)) for _ in range(3)],
        out_specs=[ANY, unit, unit, whole(rows, 1)],
        out_shape=[
            jax.ShapeDtypeStruct((rows, cols), bf16),
            shape,
            shape,
            jax.ShapeDtypeStruct((rows, 1), f32),
        ],
        scratch_shapes=scratch
        + [pltpu.VMEM((blocks, block, cols), bf16), pltpu.SemaphoreType.DMA((blocks,))],
    )(slot.reshape(1, sum(sizes)), gain, *pieces, w_down, *[array for part in parts for array in part])


def token_kernel(steps, spread, d_gate_ref, d_up_ref, slot_ref, route_ref, gate_ref, up_ref, *outs):
    step = pl.program_id(0)

    def store(part):
        if not spread:
            outs[0][...] = part
            return
        half = slot_ref.shape[0] // 2
        width = part.shape[1]
        for k in range(2):
            slot = slot_ref[k * half : (k + 1) * half, :]
            lanes = lax.broadcasted_iota(jnp.int32, (half, part.shape[0]), 1)
            place = jnp.where(lanes == slot, 1.0, 0.0).astype(bf16)
            outs[k][:, :width] = dot(place, part, ((1,), (0,))).astype(bf16)

    @pl.when(step < steps)
    def _():
        part = dot(d_gate_ref[...], gate_ref[...], ((1,), (1,)))
        store((part + dot(d_up_ref[...], up_ref[...], ((1,), (1,)))).astype(bf16))

    if spread:

        @pl.when(step >= steps)
        def _():
            store(route_ref[...])


def token_grad(d_gate, d_up, slot, route, w_gate, w_up, chunk, chunks, spread):
    rows, units = d_gate.shape
    width = w_gate.shape[0] // chunks
    total = slot.shape[0]
    block = tile(width, 512)
    steps = width // block
    first = chunk * steps
    extra = route.shape[1] if spread and chunk == chunks - 1 else 0
    weight = pl.BlockSpec((block, units), lambda i: (first + jnp.minimum(i, steps - 1), 0))
    out_rows = [total // 2] * 2 if spread else [rows]
    return call(
        functools.partial(token_kernel, steps, spread),
        4 * rows * width * units + 2 * rows * width * total * spread,
        4 * width * units + 2 * total * width,
        grid=(steps + (extra > 0),),
        in_specs=[whole(rows, units), whole(rows, units), whole(total, 1), whole(*route.shape), weight, weight],
        out_specs=[pl.BlockSpec((n, block), lambda i: (0, i)) for n in out_rows],
        out_shape=[jax.ShapeDtypeStruct((n, width + extra), bf16) for n in out_rows],
    )(d_gate, d_up, slot.reshape(total, 1), route, w_gate, w_up)


def down_kernel(count, g_ref, gain_ref, *refs):
    turned, out_ref = refs[:count], refs[-1]
    scaled = (gain_ref[...] * g_ref[...].astype(f32)).astype(bf16)
    at = 0
    for ref in turned:
        out_ref[at : at + ref.shape[0], :] = dot(ref[...], scaled, ((1,), (0,))).astype(bf16)
        at += ref.shape[0]


def down_grad(turned, g, gain, chunk, chunks, into):
    rows, width = g.shape
    units = sum(part.shape[0] for part in turned)
    block = tile(width // chunks, 512)
    steps = width // chunks // block
    first = chunk * steps
    kept = [] if into is None else [into]
    return call(
        functools.partial(down_kernel, len(turned)),
        2 * rows * width * units // chunks,
        2 * width * units // chunks,
        grid=(steps,),
        in_specs=[pl.BlockSpec((rows, block), lambda i: (0, first + i)), whole(rows, 1)]
        + [whole(*part.shape) for part in turned]
        + [pl.BlockSpec(memory_space=pl.ANY)] * len(kept),
        out_specs=pl.BlockSpec((units, block), lambda i: (0, first + i)),
        out_shape=jax.ShapeDtypeStruct((units, width), bf16),
        input_output_aliases={2 + len(turned): 0} if kept else {},
    )(g, gain, *turned, *kept)


def body(tokens, grad_out, expert_ids, route_weights, w_gate, w_up, w_down):
    wide_count = lax.axis_size("wide")
    narrow_count = lax.axis_size("narrow")
    local_experts = w_gate.shape[0]
    experts_all = local_experts * wide_count
    tok_count, top_count = expert_ids.shape
    capacity = min(tok_count, 2 * tok_count * top_count // experts_all)
    rows = wide_count * capacity
    total = wide_count * tok_count
    cols = tokens.shape[1]
    me = lax.axis_index("wide")
    pad = -2 * top_count % LANES
    meta = jnp.concatenate(
        [expert_ids.astype(bf16), route_weights, jnp.zeros((tok_count, pad), bf16)], axis=1
    )
    first_t = gather_z(jnp.concatenate([tokens, meta], axis=1))
    x_t, y_t = gather_sides(first_t)
    first_g = gather_z(after(grad_out, first_t))
    far_t = gather_far(x_t, y_t)
    x_g, y_g = gather_sides(after(first_g, *far_t))
    pieces_t = gather_core([first_t, x_t, y_t] + far_t)
    all_meta = gather_meta(pieces_t, cols)
    all_ids = all_meta[:, :top_count].astype(jnp.int32)
    all_weights = all_meta[:, top_count : 2 * top_count].astype(f32)
    first = me * local_experts
    fused = narrow_count == 1 and local_experts == 1
    chunks = CHUNKS if fused else 1
    units = w_gate.shape[2]
    parts = 2 if units % (2 * LANES) == 0 else 1
    picked = []
    for j in range(local_experts):
        match = all_ids == first + j
        chosen = jnp.any(match, axis=1)
        gain = jnp.sum(jnp.where(match, all_weights, 0.0), axis=1)
        rank = jnp.cumsum(chosen.astype(jnp.int32)) - 1
        slot = jnp.where(chosen, rank, -1)
        place = slot[None, :] == jnp.arange(rows, dtype=jnp.int32)[:, None]
        row_gain = jnp.sum(jnp.where(place, gain[None, :], 0.0), axis=1, keepdims=True)
        if fused:
            x, first_part = pick_forward(slot, pieces_t, rows, w_gate[j], w_up[j], parts)
        else:
            x = pick_rows(slot, pieces_t, rows, cols)
            x = lax.all_gather(x, "narrow", axis=1, tiled=True)
            first_part = forward(x, w_gate[j], w_up[j], 0, parts)
        ahead = [first_part]
        picked.append((slot, place, row_gain, x, ahead))
    x_g, y_g, *_ = lax.optimization_barrier((x_g, y_g, *[ahead[0][0] for *_, ahead in picked]))
    far_g = gather_far(x_g, y_g)
    for j in range(local_experts):
        slot, place, row_gain, x, ahead = picked[j]
        if parts == 2:
            ahead.append(forward(after(x, x_g, y_g), w_gate[j], w_up[j], 1, parts))
    far_g = lax.optimization_barrier((*far_g, *[ahead[-1][0] for *_, ahead in picked]))[: len(far_g)]
    pieces_g = gather_core([first_g, x_g, y_g, *far_g])
    expert_cols = experts_all + -experts_all % LANES
    dense = [0, 0]
    route_all = 0
    ends = []
    for j in range(local_experts):
        slot, place, row_gain, x, ahead = picked[j]
        straight = [(hidden, active, pull) for hidden, _, active, pull in ahead]
        if fused:
            g, d_gate, d_up, route = pick_back(slot, pieces_g, row_gain, w_down[j], straight)
        else:
            g = pick_rows(slot, pieces_g, rows, cols)
            g = lax.all_gather(g, "narrow", axis=1, tiled=True)
            d_gate, d_up, route = back_project(g, row_gain, w_down[j], straight)
        route = lax.psum(route.astype(bf16).astype(f32), "narrow")
        at = jnp.arange(expert_cols, dtype=jnp.int32) == first + j
        route = jnp.where(at[None, :], route, 0.0).astype(bf16)
        ends.append(([part[1] for part in ahead], g, row_gain))
        if fused:
            own, other = token_grad(d_gate, d_up, slot, route, w_gate[j], w_up[j], 0, chunks, True)
            dense = [own, other]
            continue
        (part,) = token_grad(d_gate, d_up, slot, route, w_gate[j], w_up[j], 0, 1, False)
        part = lax.psum_scatter(part, "narrow", scatter_dimension=1, tiled=True)
        part = jnp.concatenate([part, route], axis=1)
        part = dot(place.astype(bf16), part, ((0,), (0,)))
        dense = [dense[0] + part[: total // 2], dense[1] + part[total // 2 :]]
    mine = [add(dense[0].astype(bf16), flip(dense[1].astype(bf16), CORE))]
    if fused and chunks == 2:
        own, other = token_grad(after(d_gate, dense[0]), d_up, slot, route, w_gate[0], w_up[0], 1, chunks, True)
        mine[0] = add(after(dense[0], own), flip(dense[1], CORE))
        mine.append(add(own, flip(other, CORE)))
    sides = [scatter_far(rows_) for rows_ in mine]
    firsts = [scatter_sides(*side) for side in sides]
    shares = [scatter_z(first_) for first_ in firsts]
    gates = [mine[0], sides[0][1], firsts[0], firsts[-1]] if fused else [mine[0]]
    grad_downs = []
    for turned, g, row_gain in ends:
        out = None
        for k, gate in enumerate(gates):
            out = down_grad(turned, after(g, gate), row_gain, k, len(gates), out)
        grad_downs.append(out)
    joined = jnp.concatenate(shares, axis=1)
    width = tokens.shape[1]
    by_expert = joined[:, width : width + experts_all].astype(f32)
    pick = expert_ids[:, :, None] == jnp.arange(experts_all, dtype=jnp.int32)[None, None, :]
    grad_route = jnp.sum(jnp.where(pick, by_expert[:, None, :], 0.0), axis=2)
    return (joined[:, :width], grad_route.astype(bf16), jnp.stack(grad_downs))


def solution(mesh):
    in_specs = (
        P("wide", "narrow"),
        P("wide", "narrow"),
        P("wide", None),
        P("wide", None),
        P("wide", None, "narrow"),
        P("wide", None, "narrow"),
        P("wide", "narrow", None),
    )
    out_specs = (P("wide", "narrow"), P("wide", None), P("wide", "narrow", None))
    return jax.shard_map(body, mesh=mesh, in_specs=in_specs, out_specs=out_specs, check_vma=False)
```

profile of v0, /device:TPU:0, one launch (start us, length us, event | category | flops | bytes accessed | tf_op | source)
XLA Modules:
  0.0 187.0 jit_solution(4922129234077868072)
XLA Ops:
  3.2 5.1 %collective-permute-start.2 = (bf16[24,4224]{1,0:T(8,128)(2,1)S(1)}, bf16[24,4224]{1,0:T(8,128)(2,1)S(1)}, u32[]{:S(2)}, u32[]{:S(2)}) collective-permute-start(bf16[24,4224]{1,0:T(8,128)(2,1)S(1)} %concatenate.24), channel_id=1, source_target_pairs={{0,24},{1,25},{2,26},{3,27},{4,28},{5,29},{6,30},{7,31},{8,16},{9,... | collective-permute-start | bytes 608264 | tf_op jit(solution)/shard_map/ppermute | solution.py:49
  9.0 5.4 %collective-permute-done.2 = bf16[24,4224]{1,0:T(8,128)(2,1)S(1)} collective-permute-done((bf16[24,4224]{1,0:T(8,128)(2,1)S(1)}, bf16[24,4224]{1,0:T(8,128)(2,1)S(1)}, u32[]{:S(2)}, u32[]{:S(2)}) %collective-permute-start.2) | collective-permute-done | bytes 202784 | tf_op jit(solution)/shard_map/ppermute | solution.py:49
  14.3 11.2 %collective-permute-done.1 = bf16[24,4224]{1,0:T(8,128)(2,1)S(1)} collective-permute-done((bf16[24,4224]{1,0:T(8,128)(2,1)S(1)}, bf16[24,4224]{1,0:T(8,128)(2,1)S(1)}, u32[]{:S(2)}, u32[]{:S(2)}) %collective-permute-start.1) | collective-permute-done | bytes 202784 | tf_op jit(solution)/shard_map/ppermute | solution.py:49
  25.6 2.6 %collective-permute-start.14 = (bf16[24,4096]{1,0:T(8,128)(2,1)S(1)}, bf16[24,4096]{1,0:T(8,128)(2,1)S(1)}, u32[]{:S(2)}, u32[]{:S(2)}) collective-permute-start(bf16[24,4096]{1,0:T(8,128)(2,1)S(1)} %copy-done.11), channel_id=1, source_target_pairs={{0,24},{1,25},{2,26},{3,27},{4,28},{5,29},{6,30},{7,31},{8,16},{9,... | collective-permute-start | bytes 589832 | tf_op jit(solution)/shard_map/ppermute | solution.py:49
  28.3 1.8 collective-permute-start.12
  30.1 1.5 collective-permute-start.4
  31.6 1.5 collective-permute-start.3
  33.8 6.2 %collective-permute-done.12 = bf16[24,4096]{1,0:T(8,128)(2,1)S(1)} collective-permute-done((bf16[24,4096]{1,0:T(8,128)(2,1)S(1)}, bf16[24,4096]{1,0:T(8,128)(2,1)S(1)}, u32[]{:S(2)}, u32[]{:S(2)}) %collective-permute-start.12) | collective-permute-done | bytes 196640 | tf_op jit(solution)/shard_map/ppermute | solution.py:49
  40.7 7.7 %collective-permute-done.4.refs_2_ = bf16[96,4224]{1,0:T(8,128)(2,1)S(1)} collective-permute-done((bf16[96,4224]{1,0:T(8,128)(2,1)S(1)}, bf16[96,4224]{1,0:T(8,128)(2,1)S(1)}, u32[]{:S(2)}, u32[]{:S(2)}) %collective-permute-start.4) | collective-permute-done | bytes 811040 | tf_op jit(solution)/shard_map/ppermute | solution.py:49
  48.4 1.6 collective-permute-start.5
  52.8 5.5 %collective-permute-done.5.refs_3_ = bf16[48,4224]{1,0:T(8,128)(2,1)S(1)} collective-permute-done((bf16[48,4224]{1,0:T(8,128)(2,1)S(1)}, bf16[48,4224]{1,0:T(8,128)(2,1)S(1)}, u32[]{:S(2)}, u32[]{:S(2)}) %collective-permute-start.5) | collective-permute-done | bytes 405536 | tf_op jit(solution)/shard_map/ppermute | solution.py:49
  59.9 1.3 collective-permute-start.16
  63.9 13.2 %shard_map.95 = (bf16[384,4096]{1,0:T(8,128)(2,1)}, bf16[384,768]{1,0:T(8,128)(2,1)}, bf16[768,384]{1,0:T(8,128)(2,1)}, bf16[384,768]{1,0:T(8,128)(2,1)}, bf16[384,768]{1,0:T(8,128)(2,1)}) custom-call(s32[1,768]{1,0:T(1,128)S(1)} %get-tuple-element.69.slot_ref, bf16[96,4224]{1,0:T(8,128)(2,1)} %copy-done.4, bf16[96,4224]{1,0:T(8,128)(2,1)} %copy-done.6, ...), custom_call_target="tpu_custom_call" | custom-call | flops 7247757312 | bytes 22020096 | tf_op jit(solution)/shard_map/pallas_call | solution.py:364
  77.2 2.6 %collective-permute-done.16.refs_2_ = bf16[96,4096]{1,0:T(8,128)(2,1)} collective-permute-done((bf16[96,4096]{1,0:T(8,128)(2,1)}, bf16[96,4096]{1,0:T(8,128)(2,1)}, u32[]{:S(2)}, u32[]{:S(2)}) %collective-permute-start.16) | collective-permute-done | bytes 786464 | tf_op jit(solution)/shard_map/ppermute | solution.py:49
  84.2 1.5 collective-permute-start.18
  85.7 10.1 %shard_map.96 = (bf16[384,768]{1,0:T(8,128)(2,1)S(1)}, bf16[768,384]{1,0:T(8,128)(2,1)S(1)}, bf16[384,768]{1,0:T(8,128)(2,1)S(1)}, bf16[384,768]{1,0:T(8,128)(2,1)}) custom-call(bf16[384,4096]{1,0:T(8,128)(2,1)} %get-tuple-element.39.x_ref, bf16[4096,1536]{1,0:T(8,128)(2,1)} %bitcast.21, bf16[4096,1536]{1,0:T(8,128)(2,1)} %bitcast.25), custom_call_target="tpu_custom_call" | custom-call | flops 4831838208 | bytes 12582912 | tf_op jit(solution)/shard_map/pallas_call | solution.py:203
  99.0 15.5 %shard_map.97 = (bf16[384,4096]{1,0:T(8,128)(2,1)}, bf16[384,1536]{1,0:T(8,128)(2,1)}, bf16[384,1536]{1,0:T(8,128)(2,1)}, f32[384,1]{1,0:T(8,128)S(1)}) custom-call(s32[1,768]{1,0:T(1,128)S(1)} %get-tuple-element.69.slot_ref, f32[384,1]{1,0:T(8,128)S(1)} %broadcast_in_dim.81.gain_ref, bf16[96,4096]{1,0:T(8,128)(2,1)} %constant_dynamic-update-slice_fusion.refs_0_, ...), custom_call_target="tpu_custom_call" | custom-call | flops 7247757312 | bytes 22020096 | tf_op jit(solution)/shard_map/pallas_call | solution.py:433
  116.1 11.2 %shard_map.98 = (bf16[384,2048]{1,0:T(8,128)(2,1)}, bf16[384,2048]{1,0:T(8,128)(2,1)}) custom-call(bf16[384,1536]{1,0:T(8,128)(2,1)S(1)} %copy-done.1, bf16[384,1536]{1,0:T(8,128)(2,1)} %get-tuple-element.48.d_up_ref, s32[768,1]{1,0:T(8,128)S(1)} %bitcast_select_fusion.slot_ref, bf16[384,128]{1,0:T(8,128)(2,1)S(1)} %select_convert_fusion.route_ref, ...), custom_call_target="tpu_custom_call" | custom-call | flops 6039797760 | bytes 15728640 | tf_op jit(solution)/shard_map/pallas_call | solution.py:490
  127.4 11.4 %shard_map.99 = (bf16[384,2176]{1,0:T(8,128)(2,1)}, bf16[384,2176]{1,0:T(8,128)(2,1)}) custom-call(bf16[384,1536]{1,0:T(8,128)(2,1)S(1)} %copy-done.1, bf16[384,1536]{1,0:T(8,128)(2,1)} %get-tuple-element.48.d_up_ref, s32[768,1]{1,0:T(8,128)S(1)} %bitcast_select_fusion.slot_ref, bf16[384,128]{1,0:T(8,128)(2,1)S(1)} %select_convert_fusion.route_ref, ...), custom_call_target="tpu_custom_call" | custom-call | flops 6039797760 | bytes 15728640 | tf_op jit(solution)/shard_map/pallas_call | solution.py:490
  139.3 2.5 %add_convert_fusion.1 = bf16[384,2048]{1,0:T(8,128)(2,1)S(1)} fusion(bf16[384,2048]{1,0:T(8,128)(2,1)} %collective-permute-done.24, bf16[384,2048]{1,0:T(8,128)(2,1)} %get-tuple-element.53), kind=kLoop, calls=%fused_computation.1 | loop fusion | flops 3145728 | bytes 4718592 | tf_op jit(solution)/shard_map/convert_element_type | solution.py:23
  143.7 4.4 %shard_map.100.refs_2_ = bf16[1536,4096]{1,0:T(8,128)(2,1)} custom-call(bf16[384,4096]{1,0:T(8,128)(2,1)} %get-tuple-element.62.g_ref, f32[384,1]{1,0:T(8,128)S(1)} %broadcast_in_dim.81.gain_ref, bf16[768,384]{1,0:T(8,128)(2,1)S(1)} %copy-done, bf16[768,384]{1,0:T(8,128)(2,1)S(1)} %get-tuple-element.59.refs_1_), custom_call_target="tpu_custom_call" | custom-call | flops 1207959552 | bytes 3145728 | tf_op jit(solution)/shard_map/pallas_call | solution.py:517
  149.4 1.5 collective-permute-start.33
  151.8 1.3 collective-permute-start.28
  153.1 4.3 %shard_map.101.refs_2_ = bf16[1536,4096]{1,0:T(8,128)(2,1)} custom-call(bf16[384,4096]{1,0:T(8,128)(2,1)} %get-tuple-element.62.g_ref, f32[384,1]{1,0:T(8,128)S(1)} %broadcast_in_dim.81.gain_ref, bf16[768,384]{1,0:T(8,128)(2,1)S(1)} %copy-done, bf16[768,384]{1,0:T(8,128)(2,1)S(1)} %get-tuple-element.59.refs_1_, ...), custom_call_target="tpu_custom_call", output_to_operand_aliasing={{}: (4, {})} | custom-call | flops 1207959552 | bytes 3145728 | tf_op jit(solution)/shard_map/pallas_call | solution.py:517
  157.7 1.6 collective-permute-start.36
  160.0 6.0 %collective-permute-done.28 = bf16[96,2048]{1,0:T(8,128)(2,1)S(1)} collective-permute-done((bf16[96,2048]{1,0:T(8,128)(2,1)S(1)}, bf16[96,2048]{1,0:T(8,128)(2,1)S(1)}, u32[]{:S(2)}, u32[]{:S(2)}) %collective-permute-start.28) | collective-permute-done | bytes 393248 | tf_op jit(solution)/shard_map/ppermute | solution.py:49
  166.5 2.3 %collective-permute-start.31 = (bf16[24,2048]{1,0:T(8,128)(2,1)S(1)}, bf16[24,2048]{1,0:T(8,128)(2,1)S(1)}, u32[]{:S(2)}, u32[]{:S(2)}) collective-permute-start(bf16[24,2048]{1,0:T(8,128)(2,1)S(1)} %get-tuple-element.87), channel_id=1, source_target_pairs={{0,24},{1,25},{2,26},{3,27},{4,28},{5,29},{6,30},{7,31},{8,16},{9,... | collective-permute-start | bytes 294920 | tf_op jit(solution)/shard_map/ppermute | solution.py:49
  169.7 4.3 %shard_map.102.refs_2_ = bf16[1536,4096]{1,0:T(8,128)(2,1)} custom-call(bf16[384,4096]{1,0:T(8,128)(2,1)} %get-tuple-element.62.g_ref, f32[384,1]{1,0:T(8,128)S(1)} %broadcast_in_dim.81.gain_ref, bf16[768,384]{1,0:T(8,128)(2,1)S(1)} %copy-done, bf16[768,384]{1,0:T(8,128)(2,1)S(1)} %get-tuple-element.59.refs_1_, ...), custom_call_target="tpu_custom_call", output_to_operand_aliasing={{}: (4, {})} | custom-call | flops 1207959552 | bytes 3145728 | tf_op jit(solution)/shard_map/pallas_call | solution.py:517
  174.0 1.6 collective-permute-done.30
  175.9 2.4 %collective-permute-start.39 = (bf16[24,2176]{1,0:T(8,128)(2,1)S(1)}, bf16[24,2176]{1,0:T(8,128)(2,1)S(1)}, u32[]{:S(2)}, u32[]{:S(2)}) collective-permute-start(bf16[24,2176]{1,0:T(8,128)(2,1)S(1)} %get-tuple-element.84), channel_id=1, source_target_pairs={{0,24},{1,25},{2,26},{3,27},{4,28},{5,29},{6,30},{7,31},{8,16},{9,... | collective-permute-start | bytes 313352 | tf_op jit(solution)/shard_map/ppermute | solution.py:49
  179.4 4.3 %shard_map.103 = bf16[1536,4096]{1,0:T(8,128)(2,1)} custom-call(bf16[384,4096]{1,0:T(8,128)(2,1)} %get-tuple-element.62.g_ref, f32[384,1]{1,0:T(8,128)S(1)} %broadcast_in_dim.81.gain_ref, bf16[768,384]{1,0:T(8,128)(2,1)S(1)} %copy-done, bf16[768,384]{1,0:T(8,128)(2,1)S(1)} %get-tuple-element.59.refs_1_, ...), custom_call_target="tpu_custom_call", output_to_operand_aliasing={{}: (4, {})} | custom-call | flops 1207959552 | bytes 3145728 | tf_op jit(solution)/shard_map/pallas_call | solution.py:517
  183.7 1.7 collective-permute-done.38
  (136 shorter events, 30.9 us)
Async XLA Ops:
  3.2 11.1 %collective-permute-start.2 = (bf16[24,4224]{1,0:T(8,128)(2,1)S(1)}, bf16[24,4224]{1,0:T(8,128)(2,1)S(1)}, u32[]{:S(2)}, u32[]{:S(2)}) collective-permute-start(bf16[24,4224]{1,0:T(8,128)(2,1)S(1)} %concatenate.24), channel_id=1, source_target_pairs={{0,24},{1,25},{2,26},{3,27},{4,28},{5,29},{6,30},{7,31},{8,16},{9,... | collective-permute-start | bytes 608264 | tf_op jit(solution)/shard_map/ppermute | solution.py:49
  8.3 17.2 %collective-permute-start.1 = (bf16[24,4224]{1,0:T(8,128)(2,1)S(1)}, bf16[24,4224]{1,0:T(8,128)(2,1)S(1)}, u32[]{:S(2)}, u32[]{:S(2)}) collective-permute-start(bf16[24,4224]{1,0:T(8,128)(2,1)S(1)} %concatenate.24), channel_id=1, source_target_pairs={{0,16},{1,17},{2,18},{3,19},{4,20},{5,21},{6,22},{7,23},{8,24},{9,... | collective-permute-start | bytes 608264 | tf_op jit(solution)/shard_map/ppermute | solution.py:49
  8.3 17.2 %collective-permute-start = (bf16[24,4224]{1,0:T(8,128)(2,1)S(1)}, bf16[24,4224]{1,0:T(8,128)(2,1)S(1)}, u32[]{:S(2)}, u32[]{:S(2)}) collective-permute-start(bf16[24,4224]{1,0:T(8,128)(2,1)S(1)} %concatenate.24), channel_id=1, source_target_pairs={{0,8},{1,9},{2,10},{3,11},{4,12},{5,13},{6,14},{7,15},{8,0},{9,1},... | collective-permute-start | bytes 608264 | tf_op jit(solution)/shard_map/ppermute | solution.py:49
  25.6 26.0 %collective-permute-start.14 = (bf16[24,4096]{1,0:T(8,128)(2,1)S(1)}, bf16[24,4096]{1,0:T(8,128)(2,1)S(1)}, u32[]{:S(2)}, u32[]{:S(2)}) collective-permute-start(bf16[24,4096]{1,0:T(8,128)(2,1)S(1)} %copy-done.11), channel_id=1, source_target_pairs={{0,24},{1,25},{2,26},{3,27},{4,28},{5,29},{6,30},{7,31},{8,16},{9,... | collective-permute-start | bytes 589832 | tf_op jit(solution)/shard_map/ppermute | solution.py:49
  28.3 23.4 %collective-permute-start.13 = (bf16[24,4096]{1,0:T(8,128)(2,1)S(1)}, bf16[24,4096]{1,0:T(8,128)(2,1)S(1)}, u32[]{:S(2)}, u32[]{:S(2)}) collective-permute-start(bf16[24,4096]{1,0:T(8,128)(2,1)S(1)} %copy-done.11), channel_id=1, source_target_pairs={{0,16},{1,17},{2,18},{3,19},{4,20},{5,21},{6,22},{7,23},{8,24},{9,... | collective-permute-start | bytes 589832 | tf_op jit(solution)/shard_map/ppermute | solution.py:49
  28.3 11.7 %collective-permute-start.12 = (bf16[24,4096]{1,0:T(8,128)(2,1)S(1)}, bf16[24,4096]{1,0:T(8,128)(2,1)S(1)}, u32[]{:S(2)}, u32[]{:S(2)}) collective-permute-start(bf16[24,4096]{1,0:T(8,128)(2,1)S(1)} %copy-done.11), channel_id=1, source_target_pairs={{0,8},{1,9},{2,10},{3,11},{4,12},{5,13},{6,14},{7,15},{8,0},{9,1},... | collective-permute-start | bytes 589832 | tf_op jit(solution)/shard_map/ppermute | solution.py:49
  30.1 18.3 %collective-permute-start.4 = (bf16[96,4224]{1,0:T(8,128)(2,1)S(1)}, bf16[96,4224]{1,0:T(8,128)(2,1)S(1)}, u32[]{:S(2)}, u32[]{:S(2)}) collective-permute-start(bf16[96,4224]{1,0:T(8,128)(2,1)S(1)} %pad_maximum_fusion.refs_0_), channel_id=1, source_target_pairs={{0,4},{1,5},{2,6},{3,7},{4,0},{5,1},{6,2},{7,3},{8,12},{9,13},{10,... | collective-permute-start | bytes 2433032 | tf_op jit(solution)/shard_map/ppermute | solution.py:49
  31.6 19.1 %collective-permute-start.3 = (bf16[96,4224]{1,0:T(8,128)(2,1)S(1)}, bf16[96,4224]{1,0:T(8,128)(2,1)S(1)}, u32[]{:S(2)}, u32[]{:S(2)}) collective-permute-start(bf16[96,4224]{1,0:T(8,128)(2,1)S(1)} %pad_maximum_fusion.refs_0_), channel_id=1, source_target_pairs={{0,2},{1,3},{2,0},{3,1},{4,6},{5,7},{6,4},{7,5},{8,10},{9,11},{10,... | collective-permute-start | bytes 2433032 | tf_op jit(solution)/shard_map/ppermute | solution.py:49
  40.0 19.5 %collective-permute-start.7 = (bf16[96,4224]{1,0:T(8,128)(2,1)S(1)}, bf16[96,4224]{1,0:T(8,128)(2,1)S(1)}, u32[]{:S(2)}, u32[]{:S(2)}) collective-permute-start(bf16[96,4224]{1,0:T(8,128)(2,1)S(1)} %pad_maximum_fusion.refs_0_), channel_id=1, source_target_pairs={{0,1},{1,0},{2,3},{3,2},{4,5},{5,4},{6,7},{7,6},{8,9},{9,8},{10,11... | collective-permute-start | bytes 2433032 | tf_op jit(solution)/shard_map/ppermute | solution.py:49
  48.4 9.9 %collective-permute-start.5 = (bf16[48,4224]{1,0:T(8,128)(2,1)S(1)}, bf16[48,4224]{1,0:T(8,128)(2,1)S(1)}, u32[]{:S(2)}, u32[]{:S(2)}) collective-permute-start(bf16[48,4224]{1,0:T(8,128)(2,1)S(1)} %slice.147), channel_id=1, source_target_pairs={{0,2},{1,3},{2,0},{3,1},{4,6},{5,7},{6,4},{7,5},{8,10},{9,11},{10,... | collective-permute-start | bytes 1216520 | tf_op jit(solution)/shard_map/ppermute | solution.py:49
  50.7 8.0 %collective-permute-start.6 = (bf16[48,4224]{1,0:T(8,128)(2,1)S(1)}, bf16[48,4224]{1,0:T(8,128)(2,1)S(1)}, u32[]{:S(2)}, u32[]{:S(2)}) collective-permute-start(bf16[48,4224]{1,0:T(8,128)(2,1)S(1)} %slice.148), channel_id=1, source_target_pairs={{0,4},{1,5},{2,6},{3,7},{4,0},{5,1},{6,2},{7,3},{8,12},{9,13},{10,... | collective-permute-start | bytes 1216520 | tf_op jit(solution)/shard_map/ppermute | solution.py:49
  51.6 8.3 %collective-permute-start.9 = (bf16[96,4224]{1,0:T(8,128)(2,1)S(1)}, bf16[96,4224]{1,0:T(8,128)(2,1)S(1)}, u32[]{:S(2)}, u32[]{:S(2)}) collective-permute-start(bf16[96,4224]{1,0:T(8,128)(2,1)S(1)} %collective-permute-done.4.refs_2_), channel_id=1, source_target_pairs={{0,1},{1,0},{2,3},{3,2},{4,5},{5,4},{6,7},{7,6},{8,9},{9,8},{10,11... | collective-permute-start | bytes 2433032 | tf_op jit(solution)/shard_map/ppermute | solution.py:49
  51.6 9.6 %collective-permute-start.8 = (bf16[96,4224]{1,0:T(8,128)(2,1)S(1)}, bf16[96,4224]{1,0:T(8,128)(2,1)S(1)}, u32[]{:S(2)}, u32[]{:S(2)}) collective-permute-start(bf16[96,4224]{1,0:T(8,128)(2,1)S(1)} %collective-permute-done.3.refs_1_), channel_id=1, source_target_pairs={{0,1},{1,0},{2,3},{3,2},{4,5},{5,4},{6,7},{7,6},{8,9},{9,8},{10,11... | collective-permute-start | bytes 2433032 | tf_op jit(solution)/shard_map/ppermute | solution.py:49
  59.5 38.7 %collective-permute-start.19 = (bf16[96,4096]{1,0:T(8,128)(2,1)}, bf16[96,4096]{1,0:T(8,128)(2,1)}, u32[]{:S(2)}, u32[]{:S(2)}) collective-permute-start(bf16[96,4096]{1,0:T(8,128)(2,1)} %constant_dynamic-update-slice_fusion.refs_0_), channel_id=1, source_target_pairs={{0,1},{1,0},{2,3},{3,2},{4,5},{5,4},{6,7},{7,6},{8,9},{9,8},{10,11... | collective-permute-start | bytes 2359304 | tf_op jit(solution)/shard_map/ppermute | solution.py:49
  59.9 19.9 %collective-permute-start.16 = (bf16[96,4096]{1,0:T(8,128)(2,1)}, bf16[96,4096]{1,0:T(8,128)(2,1)}, u32[]{:S(2)}, u32[]{:S(2)}) collective-permute-start(bf16[96,4096]{1,0:T(8,128)(2,1)} %constant_dynamic-update-slice_fusion.refs_0_), channel_id=1, source_target_pairs={{0,4},{1,5},{2,6},{3,7},{4,0},{5,1},{6,2},{7,3},{8,12},{9,13},{10,... | collective-permute-start | bytes 2359304 | tf_op jit(solution)/shard_map/ppermute | solution.py:49
  61.2 19.6 %collective-permute-start.15 = (bf16[96,4096]{1,0:T(8,128)(2,1)}, bf16[96,4096]{1,0:T(8,128)(2,1)}, u32[]{:S(2)}, u32[]{:S(2)}) collective-permute-start(bf16[96,4096]{1,0:T(8,128)(2,1)} %constant_dynamic-update-slice_fusion.refs_0_), channel_id=1, source_target_pairs={{0,2},{1,3},{2,0},{3,1},{4,6},{5,7},{6,4},{7,5},{8,10},{9,11},{10,... | collective-permute-start | bytes 2359304 | tf_op jit(solution)/shard_map/ppermute | solution.py:49
  81.8 17.2 %collective-permute-start.20 = (bf16[96,4096]{1,0:T(8,128)(2,1)}, bf16[96,4096]{1,0:T(8,128)(2,1)}, u32[]{:S(2)}, u32[]{:S(2)}) collective-permute-start(bf16[96,4096]{1,0:T(8,128)(2,1)} %collective-permute-done.15.refs_1_), channel_id=1, source_target_pairs={{0,1},{1,0},{2,3},{3,2},{4,5},{5,4},{6,7},{7,6},{8,9},{9,8},{10,11... | collective-permute-start | bytes 2359304 | tf_op jit(solution)/shard_map/ppermute | solution.py:49
  82.9 16.1 %collective-permute-start.21 = (bf16[96,4096]{1,0:T(8,128)(2,1)}, bf16[96,4096]{1,0:T(8,128)(2,1)}, u32[]{:S(2)}, u32[]{:S(2)}) collective-permute-start(bf16[96,4096]{1,0:T(8,128)(2,1)} %collective-permute-done.16.refs_2_), channel_id=1, source_target_pairs={{0,1},{1,0},{2,3},{3,2},{4,5},{5,4},{6,7},{7,6},{8,9},{9,8},{10,11... | collective-permute-start | bytes 2359304 | tf_op jit(solution)/shard_map/ppermute | solution.py:49
  83.5 13.2 %collective-permute-start.17 = (bf16[48,4096]{1,0:T(8,128)(2,1)S(1)}, bf16[48,4096]{1,0:T(8,128)(2,1)S(1)}, u32[]{:S(2)}, u32[]{:S(2)}) collective-permute-start(bf16[48,4096]{1,0:T(8,128)(2,1)S(1)} %slice.121), channel_id=1, source_target_pairs={{0,2},{1,3},{2,0},{3,1},{4,6},{5,7},{6,4},{7,5},{8,10},{9,11},{10,... | collective-permute-start | bytes 1179656 | tf_op jit(solution)/shard_map/ppermute | solution.py:49
  84.2 12.5 %collective-permute-start.18 = (bf16[48,4096]{1,0:T(8,128)(2,1)S(1)}, bf16[48,4096]{1,0:T(8,128)(2,1)S(1)}, u32[]{:S(2)}, u32[]{:S(2)}) collective-permute-start(bf16[48,4096]{1,0:T(8,128)(2,1)S(1)} %slice.122), channel_id=1, source_target_pairs={{0,4},{1,5},{2,6},{3,7},{4,0},{5,1},{6,2},{7,3},{8,12},{9,13},{10,... | collective-permute-start | bytes 1179656 | tf_op jit(solution)/shard_map/ppermute | solution.py:49
  127.2 12.0 %collective-permute-start.24 = (bf16[384,2048]{1,0:T(8,128)(2,1)}, bf16[384,2048]{1,0:T(8,128)(2,1)}, u32[]{:S(2)}, u32[]{:S(2)}) collective-permute-start(bf16[384,2048]{1,0:T(8,128)(2,1)} %get-tuple-element.54), channel_id=1, source_target_pairs={{0,1},{1,0},{2,3},{3,2},{4,5},{5,4},{6,7},{7,6},{8,9},{9,8},{10,11... | collective-permute-start | bytes 4718600 | tf_op jit(solution)/shard_map/ppermute | solution.py:49
  138.8 9.4 %collective-permute-start.32 = (bf16[384,2176]{1,0:T(8,128)(2,1)}, bf16[384,2176]{1,0:T(8,128)(2,1)S(1)}, u32[]{:S(2)}, u32[]{:S(2)}) collective-permute-start(bf16[384,2176]{1,0:T(8,128)(2,1)} %get-tuple-element.55), channel_id=1, source_target_pairs={{0,1},{1,0},{2,3},{3,2},{4,5},{5,4},{6,7},{7,6},{8,9},{9,8},{10,11... | collective-permute-start | bytes 5013512 | tf_op jit(solution)/shard_map/ppermute | solution.py:49
  141.9 9.1 %collective-permute-start.27 = (bf16[48,2048]{1,0:T(8,128)(2,1)S(1)}, bf16[48,2048]{1,0:T(8,128)(2,1)S(1)}, u32[]{:S(2)}, u32[]{:S(2)}) collective-permute-start(bf16[48,2048]{1,0:T(8,128)(2,1)S(1)} %get-tuple-element.79), channel_id=1, source_target_pairs={{0,2},{1,3},{2,0},{3,1},{4,6},{5,7},{6,4},{7,5},{8,10},{9,11},{10,... | collective-permute-start | bytes 589832 | tf_op jit(solution)/shard_map/ppermute | solution.py:49
  142.5 8.5 %collective-permute-start.25 = (bf16[48,2048]{1,0:T(8,128)(2,1)S(1)}, bf16[48,2048]{1,0:T(8,128)(2,1)S(1)}, u32[]{:S(2)}, u32[]{:S(2)}) collective-permute-start(bf16[48,2048]{1,0:T(8,128)(2,1)S(1)} %get-tuple-element.80), channel_id=1, source_target_pairs={{0,4},{1,5},{2,6},{3,7},{4,0},{5,1},{6,2},{7,3},{8,12},{9,13},{10,... | collective-permute-start | bytes 589832 | tf_op jit(solution)/shard_map/ppermute | solution.py:49
  148.6 8.7 %collective-permute-start.35 = (bf16[48,2176]{1,0:T(8,128)(2,1)S(1)}, bf16[48,2176]{1,0:T(8,128)(2,1)S(1)}, u32[]{:S(2)}, u32[]{:S(2)}) collective-permute-start(bf16[48,2176]{1,0:T(8,128)(2,1)S(1)} %get-tuple-element.73), channel_id=1, source_target_pairs={{0,2},{1,3},{2,0},{3,1},{4,6},{5,7},{6,4},{7,5},{8,10},{9,11},{10,... | collective-permute-start | bytes 626696 | tf_op jit(solution)/shard_map/ppermute | solution.py:49
  149.4 8.1 %collective-permute-start.33 = (bf16[48,2176]{1,0:T(8,128)(2,1)S(1)}, bf16[48,2176]{1,0:T(8,128)(2,1)S(1)}, u32[]{:S(2)}, u32[]{:S(2)}) collective-permute-start(bf16[48,2176]{1,0:T(8,128)(2,1)S(1)} %get-tuple-element.74), channel_id=1, source_target_pairs={{0,4},{1,5},{2,6},{3,7},{4,0},{5,1},{6,2},{7,3},{8,12},{9,13},{10,... | collective-permute-start | bytes 626696 | tf_op jit(solution)/shard_map/ppermute | solution.py:49
  151.1 14.9 %collective-permute-start.26 = (bf16[96,2048]{1,0:T(8,128)(2,1)S(1)}, bf16[96,2048]{1,0:T(8,128)(2,1)S(1)}, u32[]{:S(2)}, u32[]{:S(2)}) collective-permute-start(bf16[96,2048]{1,0:T(8,128)(2,1)S(1)} %pad_maximum_fusion.3), channel_id=1, source_target_pairs={{0,2},{1,3},{2,0},{3,1},{4,6},{5,7},{6,4},{7,5},{8,10},{9,11},{10,... | collective-permute-start | bytes 1179656 | tf_op jit(solution)/shard_map/ppermute | solution.py:49
  151.8 14.2 %collective-permute-start.28 = (bf16[96,2048]{1,0:T(8,128)(2,1)S(1)}, bf16[96,2048]{1,0:T(8,128)(2,1)S(1)}, u32[]{:S(2)}, u32[]{:S(2)}) collective-permute-start(bf16[96,2048]{1,0:T(8,128)(2,1)S(1)} %pad_maximum_fusion.4), channel_id=1, source_target_pairs={{0,4},{1,5},{2,6},{3,7},{4,0},{5,1},{6,2},{7,3},{8,12},{9,13},{10,... | collective-permute-start | bytes 1179656 | tf_op jit(solution)/shard_map/ppermute | solution.py:49
  157.7 17.9 %collective-permute-start.36 = (bf16[96,2176]{1,0:T(8,128)(2,1)S(1)}, bf16[96,2176]{1,0:T(8,128)(2,1)S(1)}, u32[]{:S(2)}, u32[]{:S(2)}) collective-permute-start(bf16[96,2176]{1,0:T(8,128)(2,1)S(1)} %pad_maximum_fusion.2), channel_id=1, source_target_pairs={{0,4},{1,5},{2,6},{3,7},{4,0},{5,1},{6,2},{7,3},{8,12},{9,13},{10,... | collective-permute-start | bytes 1253384 | tf_op jit(solution)/shard_map/ppermute | solution.py:49
  159.3 16.3 %collective-permute-start.34 = (bf16[96,2176]{1,0:T(8,128)(2,1)S(1)}, bf16[96,2176]{1,0:T(8,128)(2,1)S(1)}, u32[]{:S(2)}, u32[]{:S(2)}) collective-permute-start(bf16[96,2176]{1,0:T(8,128)(2,1)S(1)} %pad_maximum_fusion.1), channel_id=1, source_target_pairs={{0,2},{1,3},{2,0},{3,1},{4,6},{5,7},{6,4},{7,5},{8,10},{9,11},{10,... | collective-permute-start | bytes 1253384 | tf_op jit(solution)/shard_map/ppermute | solution.py:49
  166.2 7.8 %collective-permute-start.29 = (bf16[24,2048]{1,0:T(8,128)(2,1)S(1)}, bf16[24,2048]{1,0:T(8,128)(2,1)S(1)}, u32[]{:S(2)}, u32[]{:S(2)}) collective-permute-start(bf16[24,2048]{1,0:T(8,128)(2,1)S(1)} %get-tuple-element.86), channel_id=1, source_target_pairs={{0,8},{1,9},{2,10},{3,11},{4,12},{5,13},{6,14},{7,15},{8,0},{9,1},... | collective-permute-start | bytes 294920 | tf_op jit(solution)/shard_map/ppermute | solution.py:49
  175.9 7.8 %collective-permute-start.37 = (bf16[24,2176]{1,0:T(8,128)(2,1)S(1)}, bf16[24,2176]{1,0:T(8,128)(2,1)S(1)}, u32[]{:S(2)}, u32[]{:S(2)}) collective-permute-start(bf16[24,2176]{1,0:T(8,128)(2,1)S(1)} %get-tuple-element.83), channel_id=1, source_target_pairs={{0,8},{1,9},{2,10},{3,11},{4,12},{5,13},{6,14},{7,15},{8,0},{9,1},... | collective-permute-start | bytes 313352 | tf_op jit(solution)/shard_map/ppermute | solution.py:49
  (21 other events, 152.9 us)
where the time goes:
time: 188 us; the launch traced here: 187 us
  Pallas kernels  79.6 us (42%)
  waiting for transfers between devices  51.1 us (27%)
  starting transfers between devices  37.8 us (20%)
  local copies, waits for them, and re-layouts  10.6 us (6%)
  other arithmetic  6.89 us (4%)
    ppermute x40, waiting for transfers between devices, flip(): return lax.ppermute(value, 'wide', [(i, i ^ mask) for i in range(count)])  51.1 us
    ppermute x40, starting transfers between devices, flip(): return lax.ppermute(value, 'wide', [(i, i ^ mask) for i in range(count)])  37.8 us
    pallas_call x2, Pallas kernels, token_grad(): call(functools.partial(token_kernel, steps, spread), 4 * rows * width * u...  22.6 us
    pallas_call x4, Pallas kernels, down_grad(): call(functools.partial(down_kernel, len(turned)), 2 * rows * width * unit...  17.3 us
    pallas_call x1, Pallas kernels, pick_back(): call(functools.partial(pick_back_kernel, sizes, picks, blocks, steps), 2...  15.5 us
    pallas_call x1, Pallas kernels, pick_forward(): call(functools.partial(pick_forward_kernel, sizes, picks, blocks), 4 * ro...  13.2 us
    pallas_call x1, Pallas kernels, forward(): call(forward_kernel, 4 * rows * width * units, 4 * width * units, grid=(u...  10.1 us
    unnamed x33, local copies, waits for them, and re-layouts  6.22 us
  transfers between devices with their start and end apart: 40, of which 15 were waited for; matrix products, arithmetic and copies ran while one was open for 6% of the time, Pallas kernels for 28%

commit v1 on v0

--- a/solution.py
+++ b/solution.py
@@ -261,7 +261,7 @@
 ANY = pl.BlockSpec(memory_space=pl.ANY)
 
 
-def pick_phase(sizes, picks, blocks, slot_ref, pieces, x_out, scratch, weights):
+def pick_phase(sizes, picks, slot_ref, pieces, x_out, scratch, start_weights):
     held, place, x, piece_sems, x_sems = scratch
     step = pl.program_id(0)
     width = held.shape[2]
@@ -296,10 +296,9 @@
         for copy in loads(step + 2):
             copy.start()
 
-    @pl.when((step >= 1) & (step <= blocks))
-    def _():
-        for copy in weights(step - 1):
-            copy.start()
+    @pl.when(step >= 1)
+    def _():
+        start_weights(step - 1)
 
     @pl.when(step < picks)
     def _():
@@ -308,7 +307,7 @@
         x[:, columns(step)] = dot(place[...], held[step], ((1,), (0,))).astype(bf16)
         store(step).start()
 
-    @pl.when(step == picks + blocks - 1)
+    @pl.when(step == pl.num_programs(0) - 1)
     def _():
         for at in range(picks):
             store(at).wait()
@@ -342,7 +341,13 @@
             pltpu.make_async_copy(up_any.at[:, source], ups.at[at], sems.at[1, at]),
         ]
 
-    x = pick_phase(sizes, picks, blocks, slot_ref, pieces, x_out, scratch, weights)
+    def start_weights(at):
+        @pl.when(at < blocks)
+        def _():
+            for copy in weights(at):
+                copy.start()
+
+    x = pick_phase(sizes, picks, slot_ref, pieces, x_out, scratch, start_weights)
 
     @pl.when(step >= picks)
     def _():
@@ -382,20 +387,38 @@
     return x, ahead
 
 
-def pick_back_kernel(sizes, picks, blocks, steps, slot_ref, gain_ref, *refs):
+def pick_back_kernel(sizes, picks, blocks, steps, tokens, slot_ref, slot_col, gain_ref, *refs):
     count = len(sizes)
-    pieces, down_any, refs = refs[:count], refs[count], refs[count + 1 :]
-    *refs, held, place, rows_ref, piece_sems, x_sems, downs, sems = refs
-    *parts, g_out, d_gate_ref, d_up_ref, route_ref = refs
+    pieces, (down_any, gate_any, up_any), refs = refs[:count], refs[count : count + 3], refs[count + 3 :]
+    *refs, held, place, rows_ref, piece_sems, x_sems, downs, gates, ups, d_gate, d_up, sems, token_sems = refs
+    *parts, g_out, d_gate_ref, d_up_ref, route_ref, own_ref, other_ref = refs
     step = pl.program_id(0)
-    width = downs.shape[1]
+    width, token_width = downs.shape[1], gates.shape[1]
 
     def weights(at):
         source = down_any.at[pl.ds(pl.multiple_of(at * width, LANES), width), :]
         return [pltpu.make_async_copy(source, downs.at[at], sems.at[at])]
 
+    def token_weights(at):
+        source = pl.ds(pl.multiple_of(at * token_width, LANES), token_width)
+        return [
+            pltpu.make_async_copy(gate_any.at[source, :], gates.at[at], token_sems.at[0, at]),
+            pltpu.make_async_copy(up_any.at[source, :], ups.at[at], token_sems.at[1, at]),
+        ]
+
+    def start_weights(at):
+        @pl.when(at < blocks)
+        def _():
+            for copy in weights(at):
+                copy.start()
+
+        @pl.when((at >= blocks) & (at < blocks + tokens))
+        def _():
+            for copy in token_weights(at - blocks):
+                copy.start()
+
     scratch = (held, place, rows_ref, piece_sems, x_sems)
-    g = pick_phase(sizes, picks, blocks, slot_ref, pieces, g_out, scratch, weights)
+    g = pick_phase(sizes, picks, slot_ref, pieces, g_out, scratch, start_weights)
 
     @pl.when(step == 0)
     def _():
@@ -411,59 +434,92 @@
                 copy.wait()
             back = dot(g[...], downs[at], ((1,), (1,)))
             d_hidden = gain_ref[...] * back
+            units = pl.ds(pl.multiple_of(at * width, LANES), width)
             d_gate_ref[...] = (d_hidden * pull_ref[...].astype(f32)).astype(bf16)
             d_up_ref[...] = (d_hidden * active_ref[...].astype(f32)).astype(bf16)
+            d_gate[:, units] = d_gate_ref[...]
+            d_up[:, units] = d_up_ref[...]
             route_ref[...] += jnp.sum(hidden_ref[...].astype(f32) * back, axis=1, keepdims=True)
 
-
-def pick_back(slot, pieces, gain, w_down, parts):
+    @pl.when(step >= picks + blocks)
+    def _():
+        at = step - picks - blocks
+        for copy in token_weights(at):
+            copy.wait()
+        part = dot(d_gate[...], gates[at], ((1,), (1,)))
+        part = (part + dot(d_up[...], ups[at], ((1,), (1,)))).astype(bf16)
+        spread_rows(slot_col, part, (own_ref, other_ref))
+
+
+def pick_back(slot, pieces, gain, w_down, w_gate, w_up, parts, high):
     sizes = [piece.shape[0] for piece in pieces]
+    total = sum(sizes)
     rows = gain.shape[0]
     units, cols = w_down.shape
     picks, scratch = pick_scratch(rows, sizes, cols)
     block = tile(parts[0][0].shape[1], 256)
     blocks = units // block
     steps = blocks // len(parts)
-    unit = pl.BlockSpec((rows, block), lambda i: (0, jnp.maximum(i - picks, 0)))
+    token_block = tile(cols, 512)
+    tokens = high // token_block
+    unit = pl.BlockSpec((rows, block), lambda i: (0, jnp.clip(i - picks, 0, blocks - 1)))
+    dense = pl.BlockSpec((total // 2, token_block), lambda i: (0, jnp.maximum(i - picks - blocks, 0)))
 
     def unit_of(part):
         return pl.BlockSpec((rows, block), lambda i: (0, jnp.clip(i - picks - part * steps, 0, steps - 1)))
 
     shape = jax.ShapeDtypeStruct((rows, units), bf16)
     return call(
-        functools.partial(pick_back_kernel, sizes, picks, blocks, steps),
-        2 * rows * cols * units + 2 * rows * sum(sizes) * cols,
-        2 * cols * units + 2 * (rows + sum(sizes)) * cols,
-        grid=(picks + blocks,),
-        in_specs=[whole(1, sum(sizes)), whole(rows, 1)]
-        + [ANY] * (len(sizes) + 1)
+        functools.partial(pick_back_kernel, sizes, picks, blocks, steps, tokens),
+        2 * rows * (cols * units + total * cols + 2 * high * units + total * high),
+        2 * cols * units + 4 * high * units + 2 * (rows + total) * cols,
+        grid=(picks + blocks + tokens,),
+        in_specs=[whole(1, total), whole(total, 1), whole(rows, 1)]
+        + [ANY] * (len(sizes) + 3)
         + [unit_of(k) for k in range(len(parts)) for _ in range(3)],
-        out_specs=[ANY, unit, unit, whole(rows, 1)],
+        out_specs=[ANY, unit, unit, whole(rows, 1), dense, dense],
         out_shape=[
             jax.ShapeDtypeStruct((rows, cols), bf16),
             shape,
             shape,
             jax.ShapeDtypeStruct((rows, 1), f32),
-        ],
+        ]
+        + [jax.ShapeDtypeStruct((total // 2, high), bf16)] * 2,
         scratch_shapes=scratch
-        + [pltpu.VMEM((blocks, block, cols), bf16), pltpu.SemaphoreType.DMA((blocks,))],
-    )(slot.reshape(1, sum(sizes)), gain, *pieces, w_down, *[array for part in parts for array in part])
+        + [pltpu.VMEM((blocks, block, cols), bf16)]
+        + [pltpu.VMEM((tokens, token_block, units), bf16)] * 2
+        + [pltpu.VMEM((rows, units), bf16)] * 2
+        + [pltpu.SemaphoreType.DMA((blocks,)), pltpu.SemaphoreType.DMA((2, tokens))],
+    )(
+        slot.reshape(1, total),
+        slot.reshape(total, 1),
+        gain,
+        *pieces,
+        w_down,
+        w_gate,
+        w_up,
+        *[array for part in parts for array in part],
+    )
+
+
+def spread_rows(slot_ref, part, outs):
+    half = slot_ref.shape[0] // 2
+    rows, width = part.shape
+    for k in range(2):
+        slot = slot_ref[k * half : (k + 1) * half, :]
+        lanes = lax.broadcasted_iota(jnp.int32, (half, rows), 1)
+        place = jnp.where(lanes == slot, 1.0, 0.0).astype(bf16)
+        outs[k][:, :width] = dot(place, part, ((1,), (0,))).astype(bf16)
 
 
 def token_kernel(steps, spread, d_gate_ref, d_up_ref, slot_ref, route_ref, gate_ref, up_ref, *outs):
     step = pl.program_id(0)
 
     def store(part):
-        if not spread:
+        if spread:
+            spread_rows(slot_ref, part, outs)
+        else:
             outs[0][...] = part
-            return
-        half = slot_ref.shape[0] // 2
-        width = part.shape[1]
-        for k in range(2):
-            slot = slot_ref[k * half : (k + 1) * half, :]
-            lanes = lax.broadcasted_iota(jnp.int32, (half, part.shape[0]), 1)
-            place = jnp.where(lanes == slot, 1.0, 0.0).astype(bf16)
-            outs[k][:, :width] = dot(place, part, ((1,), (0,))).astype(bf16)
 
     @pl.when(step < steps)
     def _():
@@ -545,10 +601,12 @@
     )
     first_t = gather_z(jnp.concatenate([tokens, meta], axis=1))
     x_t, y_t = gather_sides(first_t)
-    first_g = gather_z(after(grad_out, first_t))
+    first_core = flip(first_t, CORE)
+    first_g = gather_z(after(grad_out, first_core))
     far_t = gather_far(x_t, y_t)
     x_g, y_g = gather_sides(after(first_g, *far_t))
-    pieces_t = gather_core([first_t, x_t, y_t] + far_t)
+    pieces_t = [first_t, x_t, y_t, *far_t, first_core]
+    pieces_t += [flip(piece, CORE) for piece in pieces_t[1:5]]
     all_meta = gather_meta(pieces_t, cols)
     all_ids = all_meta[:, :top_count].astype(jnp.int32)
     all_weights = all_meta[:, top_count : 2 * top_count].astype(f32)
@@ -556,7 +614,7 @@
     fused = narrow_count == 1 and local_experts == 1
     chunks = CHUNKS if fused else 1
     units = w_gate.shape[2]
-    parts = 2 if units % (2 * LANES) == 0 else 1
+    parts = 1 if fused or units % (2 * LANES) else 2
     picked = []
     for j in range(local_experts):
         match = all_ids == first + j
@@ -590,7 +648,9 @@
         slot, place, row_gain, x, ahead = picked[j]
         straight = [(hidden, active, pull) for hidden, _, active, pull in ahead]
         if fused:
-            g, d_gate, d_up, route = pick_back(slot, pieces_g, row_gain, w_down[j], straight)
+            g, d_gate, d_up, route, *dense = pick_back(
+                slot, pieces_g, row_gain, w_down[j], w_gate[j], w_up[j], straight, w_gate.shape[1] // chunks
+            )
         else:
             g = pick_rows(slot, pieces_g, rows, cols)
             g = lax.all_gather(g, "narrow", axis=1, tiled=True)
@@ -600,8 +660,6 @@
         route = jnp.where(at[None, :], route, 0.0).astype(bf16)
         ends.append(([part[1] for part in ahead], g, row_gain))
         if fused:
-            own, other = token_grad(d_gate, d_up, slot, route, w_gate[j], w_up[j], 0, chunks, True)
-            dense = [own, other]
             continue
         (part,) = token_grad(d_gate, d_up, slot, route, w_gate[j], w_up[j], 0, 1, False)
         part = lax.psum_scatter(part, "narrow", scatter_dimension=1, tiled=True)

time: 188 us -> 187 us (level)
  Pallas kernels: 79.6 us -> 72.6 us
  waiting for transfers between devices: 51.1 us -> 55.6 us
  local copies, waits for them, and re-layouts: 10.6 us -> 13.1 us
    pallas_call x2 -> x1, Pallas kernels: 22.6 us -> 11.6 us  [token_grad(): call(functools.partial(token_kernel, steps, spread), 4 * rows * width * u...]
    pallas_call x1, Pallas kernels: 13.2 us -> 19.1 us  [pick_forward(): call(functools.partial(pick_forward_kernel, sizes, picks, blocks), 4 * ro...]
    ppermute x40, waiting for transfers between devices: 51.1 us -> 55.6 us  [flip(): return lax.ppermute(value, 'wide', [(i, i ^ mask) for i in range(count)])]
    pallas_call x2 -> x1, Pallas kernels: 25.6 us -> 23.8 us  [pick_back(): call(functools.partial(pick_back_kernel, sizes, picks, blocks, steps, tok...]
    unnamed x33 -> x31, local copies, waits for them, and re-layouts: 6.22 us -> 7.78 us
  transfers between devices with their start and end apart: 40 -> 40, of which waited for: 15 -> 13; matrix products, arithmetic and copies ran while one was open for 6% -> 5% of each run, Pallas kernels for 28% -> 26%
where the time goes in v1:
time: 187 us
  Pallas kernels  72.6 us (39%)
  waiting for transfers between devices  55.6 us (30%)
  starting transfers between devices  37.8 us (20%)
  local copies, waits for them, and re-layouts  13.1 us (7%)
  other arithmetic  6.32 us (3%)
    ppermute x40, waiting for transfers between devices, flip(): return lax.ppermute(value, 'wide', [(i, i ^ mask) for i in range(count)])  55.6 us
    ppermute x40, starting transfers between devices, flip(): return lax.ppermute(value, 'wide', [(i, i ^ mask) for i in range(count)])  37.8 us
    pallas_call x1, Pallas kernels, pick_back(): call(functools.partial(pick_back_kernel, sizes, picks, blocks, steps, tok...  23.8 us
    pallas_call x1, Pallas kernels, pick_forward(): call(functools.partial(pick_forward_kernel, sizes, picks, blocks), 4 * ro...  19.1 us
    pallas_call x4, Pallas kernels, down_grad(): call(functools.partial(down_kernel, len(turned)), 2 * rows * width * unit...  17.3 us
    pallas_call x1, Pallas kernels, token_grad(): call(functools.partial(token_kernel, steps, spread), 4 * rows * width * u...  11.6 us
    unnamed x31, local copies, waits for them, and re-layouts  7.78 us
  transfers between devices with their start and end apart: 40, of which 13 were waited for; matrix products, arithmetic and copies ran while one was open for 5% of the time, Pallas kernels for 26%

profile of v1, /device:TPU:0, one launch (start us, length us, event | category | flops | bytes accessed | tf_op | source)
XLA Modules:
  0.0 186.5 jit_solution(16030182412455378504)
XLA Ops:
  3.2 5.1 %collective-permute-start.2 = (bf16[24,4224]{1,0:T(8,128)(2,1)S(1)}, bf16[24,4224]{1,0:T(8,128)(2,1)S(1)}, u32[]{:S(2)}, u32[]{:S(2)}) collective-permute-start(bf16[24,4224]{1,0:T(8,128)(2,1)S(1)} %concatenate.24), channel_id=1, source_target_pairs={{0,24},{1,25},{2,26},{3,27},{4,28},{5,29},{6,30},{7,31},{8,16},{9,... | collective-permute-start | bytes 608264 | tf_op jit(solution)/shard_map/ppermute | solution.py:49
  8.9 5.4 %collective-permute-done.2 = bf16[24,4224]{1,0:T(8,128)(2,1)S(1)} collective-permute-done((bf16[24,4224]{1,0:T(8,128)(2,1)S(1)}, bf16[24,4224]{1,0:T(8,128)(2,1)S(1)}, u32[]{:S(2)}, u32[]{:S(2)}) %collective-permute-start.2) | collective-permute-done | bytes 202784 | tf_op jit(solution)/shard_map/ppermute | solution.py:49
  14.3 11.2 %collective-permute-done.1 = bf16[24,4224]{1,0:T(8,128)(2,1)S(1)} collective-permute-done((bf16[24,4224]{1,0:T(8,128)(2,1)S(1)}, bf16[24,4224]{1,0:T(8,128)(2,1)S(1)}, u32[]{:S(2)}, u32[]{:S(2)}) %collective-permute-start.1) | collective-permute-done | bytes 202784 | tf_op jit(solution)/shard_map/ppermute | solution.py:49
  25.7 1.6 collective-permute-start.4
  27.2 1.5 collective-permute-start.3
  28.7 2.5 %collective-permute-start.14 = (bf16[24,4096]{1,0:T(8,128)(2,1)}, bf16[24,4096]{1,0:T(8,128)(2,1)S(1)}, u32[]{:S(2)}, u32[]{:S(2)}) collective-permute-start(bf16[24,4096]{1,0:T(8,128)(2,1)} %param.8), channel_id=1, source_target_pairs={{0,24},{1,25},{2,26},{3,27},{4,28},{5,29},{6,30},{7,31},{8,16},{9,... | collective-permute-start | bytes 589832 | tf_op jit(solution)/shard_map/ppermute | solution.py:49
  31.2 1.9 %collective-permute-start.12 = (bf16[24,4096]{1,0:T(8,128)(2,1)}, bf16[24,4096]{1,0:T(8,128)(2,1)S(1)}, u32[]{:S(2)}, u32[]{:S(2)}) collective-permute-start(bf16[24,4096]{1,0:T(8,128)(2,1)} %param.8), channel_id=1, source_target_pairs={{0,8},{1,9},{2,10},{3,11},{4,12},{5,13},{6,14},{7,15},{8,0},{9,1},... | collective-permute-start | bytes 589832 | tf_op jit(solution)/shard_map/ppermute | solution.py:49
  33.1 1.7 constant_dynamic-update-slice_fusion.3
  34.8 11.4 %collective-permute-done.4.refs_2_ = bf16[96,4224]{1,0:T(8,128)(2,1)S(1)} collective-permute-done((bf16[96,4224]{1,0:T(8,128)(2,1)S(1)}, bf16[96,4224]{1,0:T(8,128)(2,1)S(1)}, u32[]{:S(2)}, u32[]{:S(2)}) %collective-permute-start.4) | collective-permute-done | bytes 811040 | tf_op jit(solution)/shard_map/ppermute | solution.py:49
  46.2 1.6 collective-permute-start.5
  48.8 1.6 collective-permute-start.6
  52.3 5.0 %collective-permute-done.5.refs_3_ = bf16[48,4224]{1,0:T(8,128)(2,1)S(1)} collective-permute-done((bf16[48,4224]{1,0:T(8,128)(2,1)S(1)}, bf16[48,4224]{1,0:T(8,128)(2,1)S(1)}, u32[]{:S(2)}, u32[]{:S(2)}) %collective-permute-start.5) | collective-permute-done | bytes 405536 | tf_op jit(solution)/shard_map/ppermute | solution.py:49
  57.3 2.3 %collective-permute-done.6.refs_4_ = bf16[48,4224]{1,0:T(8,128)(2,1)S(1)} collective-permute-done((bf16[48,4224]{1,0:T(8,128)(2,1)S(1)}, bf16[48,4224]{1,0:T(8,128)(2,1)S(1)}, u32[]{:S(2)}, u32[]{:S(2)}) %collective-permute-start.6) | collective-permute-done | bytes 405536 | tf_op jit(solution)/shard_map/ppermute | solution.py:49
  60.3 1.5 collective-permute-start.16
  65.0 19.1 %shard_map.95 = (bf16[384,4096]{1,0:T(8,128)(2,1)}, bf16[384,1536]{1,0:T(8,128)(2,1)}, bf16[1536,384]{1,0:T(8,128)(2,1)}, bf16[384,1536]{1,0:T(8,128)(2,1)}, bf16[384,1536]{1,0:T(8,128)(2,1)}) custom-call(s32[1,768]{1,0:T(1,128)S(1)} %get-tuple-element.57.slot_ref, bf16[96,4224]{1,0:T(8,128)(2,1)} %copy-done.2, ...), custom_call_target="tpu_custom_call" | custom-call | flops 12079595520 | bytes 34603008 | tf_op jit(solution)/shard_map/pallas_call | solution.py:369
  86.2 1.6 collective-permute-start.17
  88.8 8.4 %collective-permute-done.17.refs_3_ = bf16[48,4096]{1,0:T(8,128)(2,1)S(1)} collective-permute-done((bf16[48,4096]{1,0:T(8,128)(2,1)S(1)}, bf16[48,4096]{1,0:T(8,128)(2,1)S(1)}, u32[]{:S(2)}, u32[]{:S(2)}) %collective-permute-start.17) | collective-permute-done | bytes 393248 | tf_op jit(solution)/shard_map/ppermute | solution.py:49
  101.7 23.8 %shard_map.96 = (bf16[384,4096]{1,0:T(8,128)(2,1)}, bf16[384,1536]{1,0:T(8,128)(2,1)}, bf16[384,1536]{1,0:T(8,128)(2,1)}, f32[384,1]{1,0:T(8,128)S(1)}, bf16[384...) custom-call(s32[1,768]{1,0:T(1,128)S(1)} %get-tuple-element.57.slot_ref, s32[768,1]{1,0:T(8,128)S(1)} %bitcast_select_fusion.slot_col.slot_ref, ...), custom_call_target="tpu_custom_call" | custom-call | flops 13287555072 | bytes 34603008 | tf_op jit(solution)/shard_map/pallas_call | solution.py:472
  126.0 1.3 copy-done.1
  127.3 11.6 %shard_map.97 = (bf16[384,2176]{1,0:T(8,128)(2,1)}, bf16[384,2176]{1,0:T(8,128)(2,1)}) custom-call(bf16[384,1536]{1,0:T(8,128)(2,1)S(1)} %copy-done.1, bf16[384,1536]{1,0:T(8,128)(2,1)} %get-tuple-element.39.d_up_ref, s32[768,1]{1,0:T(8,128)S(1)} %bitcast_select_fusion.slot_col.slot_ref, bf16[384,128]{1,0:T(8,128)(2,1)S(1)} %select_convert_fusion.route_ref, ...), custom_call_target="tpu_custom_call" | custom-call | flops 6039797760 | bytes 15728640 | tf_op jit(solution)/shard_map/pallas_call | solution.py:546
  139.3 2.0 %add_convert_fusion.1 = bf16[384,2048]{1,0:T(8,128)(2,1)S(1)} fusion(bf16[384,2048]{1,0:T(8,128)(2,1)} %collective-permute-done.24, bf16[384,2048]{1,0:T(8,128)(2,1)S(1)} %copy-done.5), kind=kLoop, calls=%fused_computation.1 | loop fusion | flops 3145728 | bytes 4718592 | tf_op jit(solution)/shard_map/convert_element_type | solution.py:23
  143.0 4.4 %shard_map.98.refs_1_ = bf16[1536,4096]{1,0:T(8,128)(2,1)} custom-call(bf16[384,4096]{1,0:T(8,128)(2,1)} %get-tuple-element.50.g_ref, f32[384,1]{1,0:T(8,128)S(1)} %broadcast_in_dim.81.gain_ref, bf16[1536,384]{1,0:T(8,128)(2,1)S(1)} %copy-done), custom_call_target="tpu_custom_call" | custom-call | flops 1207959552 | bytes 3145728 | tf_op jit(solution)/shard_map/pallas_call | solution.py:573
  148.9 1.5 collective-permute-start.33
  152.3 4.3 %shard_map.99.refs_1_ = bf16[1536,4096]{1,0:T(8,128)(2,1)} custom-call(bf16[384,4096]{1,0:T(8,128)(2,1)} %get-tuple-element.50.g_ref, f32[384,1]{1,0:T(8,128)S(1)} %broadcast_in_dim.81.gain_ref, bf16[1536,384]{1,0:T(8,128)(2,1)S(1)} %copy-done, bf16[1536,4096]{1,0:T(8,128)(2,1)} %shard_map.98.refs_1_), custom_call_target="tpu_custom_call", output_to_operand_aliasing={{}: (3, {})} | custom-call | flops 1207959552 | bytes 3145728 | tf_op jit(solution)/shard_map/pallas_call | solution.py:573
  157.2 1.6 collective-permute-start.36
  159.4 6.0 %collective-permute-done.28 = bf16[96,2048]{1,0:T(8,128)(2,1)S(1)} collective-permute-done((bf16[96,2048]{1,0:T(8,128)(2,1)S(1)}, bf16[96,2048]{1,0:T(8,128)(2,1)S(1)}, u32[]{:S(2)}, u32[]{:S(2)}) %collective-permute-start.28) | collective-permute-done | bytes 393248 | tf_op jit(solution)/shard_map/ppermute | solution.py:49
  165.7 2.5 %collective-permute-start.31 = (bf16[24,2048]{1,0:T(8,128)(2,1)S(1)}, bf16[24,2048]{1,0:T(8,128)(2,1)S(1)}, u32[]{:S(2)}, u32[]{:S(2)}) collective-permute-start(bf16[24,2048]{1,0:T(8,128)(2,1)S(1)} %get-tuple-element.75), channel_id=1, source_target_pairs={{0,24},{1,25},{2,26},{3,27},{4,28},{5,29},{6,30},{7,31},{8,16},{9,... | collective-permute-start | bytes 294920 | tf_op jit(solution)/shard_map/ppermute | solution.py:49
  169.2 4.3 %shard_map.100.refs_1_ = bf16[1536,4096]{1,0:T(8,128)(2,1)} custom-call(bf16[384,4096]{1,0:T(8,128)(2,1)} %get-tuple-element.50.g_ref, f32[384,1]{1,0:T(8,128)S(1)} %broadcast_in_dim.81.gain_ref, bf16[1536,384]{1,0:T(8,128)(2,1)S(1)} %copy-done, bf16[1536,4096]{1,0:T(8,128)(2,1)} %shard_map.99.refs_1_), custom_call_target="tpu_custom_call", output_to_operand_aliasing={{}: (3, {})} | custom-call | flops 1207959552 | bytes 3145728 | tf_op jit(solution)/shard_map/pallas_call | solution.py:573
  173.5 1.6 collective-permute-done.30
  175.4 2.5 %collective-permute-start.39 = (bf16[24,2176]{1,0:T(8,128)(2,1)S(1)}, bf16[24,2176]{1,0:T(8,128)(2,1)S(1)}, u32[]{:S(2)}, u32[]{:S(2)}) collective-permute-start(bf16[24,2176]{1,0:T(8,128)(2,1)S(1)} %get-tuple-element.72), channel_id=1, source_target_pairs={{0,24},{1,25},{2,26},{3,27},{4,28},{5,29},{6,30},{7,31},{8,16},{9,... | collective-permute-start | bytes 313352 | tf_op jit(solution)/shard_map/ppermute | solution.py:49
  178.9 4.3 %shard_map.101 = bf16[1536,4096]{1,0:T(8,128)(2,1)} custom-call(bf16[384,4096]{1,0:T(8,128)(2,1)} %get-tuple-element.50.g_ref, f32[384,1]{1,0:T(8,128)S(1)} %broadcast_in_dim.81.gain_ref, bf16[1536,384]{1,0:T(8,128)(2,1)S(1)} %copy-done, bf16[1536,4096]{1,0:T(8,128)(2,1)} %shard_map.100.refs_1_), custom_call_target="tpu_custom_call", output_to_operand_aliasing={{}: (3, {})} | custom-call | flops 1207959552 | bytes 3145728 | tf_op jit(solution)/shard_map/pallas_call | solution.py:573
  183.2 1.7 collective-permute-done.38
  (132 shorter events, 28.9 us)
Async XLA Ops:
  3.2 11.1 %collective-permute-start.2 = (bf16[24,4224]{1,0:T(8,128)(2,1)S(1)}, bf16[24,4224]{1,0:T(8,128)(2,1)S(1)}, u32[]{:S(2)}, u32[]{:S(2)}) collective-permute-start(bf16[24,4224]{1,0:T(8,128)(2,1)S(1)} %concatenate.24), channel_id=1, source_target_pairs={{0,24},{1,25},{2,26},{3,27},{4,28},{5,29},{6,30},{7,31},{8,16},{9,... | collective-permute-start | bytes 608264 | tf_op jit(solution)/shard_map/ppermute | solution.py:49
  8.3 17.2 %collective-permute-start.1 = (bf16[24,4224]{1,0:T(8,128)(2,1)S(1)}, bf16[24,4224]{1,0:T(8,128)(2,1)S(1)}, u32[]{:S(2)}, u32[]{:S(2)}) collective-permute-start(bf16[24,4224]{1,0:T(8,128)(2,1)S(1)} %concatenate.24), channel_id=1, source_target_pairs={{0,16},{1,17},{2,18},{3,19},{4,20},{5,21},{6,22},{7,23},{8,24},{9,... | collective-permute-start | bytes 608264 | tf_op jit(solution)/shard_map/ppermute | solution.py:49
  8.3 17.2 %collective-permute-start = (bf16[24,4224]{1,0:T(8,128)(2,1)S(1)}, bf16[24,4224]{1,0:T(8,128)(2,1)S(1)}, u32[]{:S(2)}, u32[]{:S(2)}) collective-permute-start(bf16[24,4224]{1,0:T(8,128)(2,1)S(1)} %concatenate.24), channel_id=1, source_target_pairs={{0,8},{1,9},{2,10},{3,11},{4,12},{5,13},{6,14},{7,15},{8,0},{9,1},... | collective-permute-start | bytes 608264 | tf_op jit(solution)/shard_map/ppermute | solution.py:49
  25.7 20.5 %collective-permute-start.4 = (bf16[96,4224]{1,0:T(8,128)(2,1)S(1)}, bf16[96,4224]{1,0:T(8,128)(2,1)S(1)}, u32[]{:S(2)}, u32[]{:S(2)}) collective-permute-start(bf16[96,4224]{1,0:T(8,128)(2,1)S(1)} %pad_maximum_fusion.refs_0_), channel_id=1, source_target_pairs={{0,4},{1,5},{2,6},{3,7},{4,0},{5,1},{6,2},{7,3},{8,12},{9,13},{10,... | collective-permute-start | bytes 2433032 | tf_op jit(solution)/shard_map/ppermute | solution.py:49
  27.2 20.5 %collective-permute-start.3 = (bf16[96,4224]{1,0:T(8,128)(2,1)S(1)}, bf16[96,4224]{1,0:T(8,128)(2,1)}, u32[]{:S(2)}, u32[]{:S(2)}) collective-permute-start(bf16[96,4224]{1,0:T(8,128)(2,1)S(1)} %pad_maximum_fusion.refs_0_), channel_id=1, source_target_pairs={{0,2},{1,3},{2,0},{3,1},{4,6},{5,7},{6,4},{7,5},{8,10},{9,11},{10,... | collective-permute-start | bytes 2433032 | tf_op jit(solution)/shard_map/ppermute | solution.py:49
  28.7 30.9 %collective-permute-start.14 = (bf16[24,4096]{1,0:T(8,128)(2,1)}, bf16[24,4096]{1,0:T(8,128)(2,1)S(1)}, u32[]{:S(2)}, u32[]{:S(2)}) collective-permute-start(bf16[24,4096]{1,0:T(8,128)(2,1)} %param.8), channel_id=1, source_target_pairs={{0,24},{1,25},{2,26},{3,27},{4,28},{5,29},{6,30},{7,31},{8,16},{9,... | collective-permute-start | bytes 589832 | tf_op jit(solution)/shard_map/ppermute | solution.py:49
  31.2 19.8 %collective-permute-start.13 = (bf16[24,4096]{1,0:T(8,128)(2,1)}, bf16[24,4096]{1,0:T(8,128)(2,1)S(1)}, u32[]{:S(2)}, u32[]{:S(2)}) collective-permute-start(bf16[24,4096]{1,0:T(8,128)(2,1)} %param.8), channel_id=1, source_target_pairs={{0,16},{1,17},{2,18},{3,19},{4,20},{5,21},{6,22},{7,23},{8,24},{9,... | collective-permute-start | bytes 589832 | tf_op jit(solution)/shard_map/ppermute | solution.py:49
  31.2 19.1 %collective-permute-start.12 = (bf16[24,4096]{1,0:T(8,128)(2,1)}, bf16[24,4096]{1,0:T(8,128)(2,1)S(1)}, u32[]{:S(2)}, u32[]{:S(2)}) collective-permute-start(bf16[24,4096]{1,0:T(8,128)(2,1)} %param.8), channel_id=1, source_target_pairs={{0,8},{1,9},{2,10},{3,11},{4,12},{5,13},{6,14},{7,15},{8,0},{9,1},... | collective-permute-start | bytes 589832 | tf_op jit(solution)/shard_map/ppermute | solution.py:49
  46.2 11.1 %collective-permute-start.5 = (bf16[48,4224]{1,0:T(8,128)(2,1)S(1)}, bf16[48,4224]{1,0:T(8,128)(2,1)S(1)}, u32[]{:S(2)}, u32[]{:S(2)}) collective-permute-start(bf16[48,4224]{1,0:T(8,128)(2,1)S(1)} %slice.147), channel_id=1, source_target_pairs={{0,2},{1,3},{2,0},{3,1},{4,6},{5,7},{6,4},{7,5},{8,10},{9,11},{10,... | collective-permute-start | bytes 1216520 | tf_op jit(solution)/shard_map/ppermute | solution.py:49
  48.8 10.8 %collective-permute-start.6 = (bf16[48,4224]{1,0:T(8,128)(2,1)S(1)}, bf16[48,4224]{1,0:T(8,128)(2,1)S(1)}, u32[]{:S(2)}, u32[]{:S(2)}) collective-permute-start(bf16[48,4224]{1,0:T(8,128)(2,1)S(1)} %slice.148), channel_id=1, source_target_pairs={{0,4},{1,5},{2,6},{3,7},{4,0},{5,1},{6,2},{7,3},{8,12},{9,13},{10,... | collective-permute-start | bytes 1216520 | tf_op jit(solution)/shard_map/ppermute | solution.py:49
  50.4 11.5 %collective-permute-start.9 = (bf16[96,4224]{1,0:T(8,128)(2,1)S(1)}, bf16[96,4224]{1,0:T(8,128)(2,1)S(1)}, u32[]{:S(2)}, u32[]{:S(2)}) collective-permute-start(bf16[96,4224]{1,0:T(8,128)(2,1)S(1)} %collective-permute-done.4.refs_2_), channel_id=1, source_target_pairs={{0,1},{1,0},{2,3},{3,2},{4,5},{5,4},{6,7},{7,6},{8,9},{9,8},{10,11... | collective-permute-start | bytes 2433032 | tf_op jit(solution)/shard_map/ppermute | solution.py:49
  51.1 11.3 %collective-permute-start.8 = (bf16[96,4224]{1,0:T(8,128)(2,1)}, bf16[96,4224]{1,0:T(8,128)(2,1)S(1)}, u32[]{:S(2)}, u32[]{:S(2)}) collective-permute-start(bf16[96,4224]{1,0:T(8,128)(2,1)} %collective-permute-done.3.refs_1_), channel_id=1, source_target_pairs={{0,1},{1,0},{2,3},{3,2},{4,5},{5,4},{6,7},{7,6},{8,9},{9,8},{10,11... | collective-permute-start | bytes 2433032 | tf_op jit(solution)/shard_map/ppermute | solution.py:49
  60.3 23.8 %collective-permute-start.16 = (bf16[96,4096]{1,0:T(8,128)(2,1)}, bf16[96,4096]{1,0:T(8,128)(2,1)}, u32[]{:S(2)}, u32[]{:S(2)}) collective-permute-start(bf16[96,4096]{1,0:T(8,128)(2,1)} %constant_dynamic-update-slice_fusion.refs_0_), channel_id=1, source_target_pairs={{0,4},{1,5},{2,6},{3,7},{4,0},{5,1},{6,2},{7,3},{8,12},{9,13},{10,... | collective-permute-start | bytes 2359304 | tf_op jit(solution)/shard_map/ppermute | solution.py:49
  61.8 22.3 %collective-permute-start.15 = (bf16[96,4096]{1,0:T(8,128)(2,1)}, bf16[96,4096]{1,0:T(8,128)(2,1)}, u32[]{:S(2)}, u32[]{:S(2)}) collective-permute-start(bf16[96,4096]{1,0:T(8,128)(2,1)} %constant_dynamic-update-slice_fusion.refs_0_), channel_id=1, source_target_pairs={{0,2},{1,3},{2,0},{3,1},{4,6},{5,7},{6,4},{7,5},{8,10},{9,11},{10,... | collective-permute-start | bytes 2359304 | tf_op jit(solution)/shard_map/ppermute | solution.py:49
  86.2 11.1 %collective-permute-start.17 = (bf16[48,4096]{1,0:T(8,128)(2,1)S(1)}, bf16[48,4096]{1,0:T(8,128)(2,1)S(1)}, u32[]{:S(2)}, u32[]{:S(2)}) collective-permute-start(bf16[48,4096]{1,0:T(8,128)(2,1)S(1)} %slice.121), channel_id=1, source_target_pairs={{0,2},{1,3},{2,0},{3,1},{4,6},{5,7},{6,4},{7,5},{8,10},{9,11},{10,... | collective-permute-start | bytes 1179656 | tf_op jit(solution)/shard_map/ppermute | solution.py:49
  87.7 10.7 %collective-permute-start.18 = (bf16[48,4096]{1,0:T(8,128)(2,1)S(1)}, bf16[48,4096]{1,0:T(8,128)(2,1)S(1)}, u32[]{:S(2)}, u32[]{:S(2)}) collective-permute-start(bf16[48,4096]{1,0:T(8,128)(2,1)S(1)} %slice.122), channel_id=1, source_target_pairs={{0,4},{1,5},{2,6},{3,7},{4,0},{5,1},{6,2},{7,3},{8,12},{9,13},{10,... | collective-permute-start | bytes 1179656 | tf_op jit(solution)/shard_map/ppermute | solution.py:49
  88.2 11.6 %collective-permute-start.19 = (bf16[96,4096]{1,0:T(8,128)(2,1)}, bf16[96,4096]{1,0:T(8,128)(2,1)S(1)}, u32[]{:S(2)}, u32[]{:S(2)}) collective-permute-start(bf16[96,4096]{1,0:T(8,128)(2,1)} %constant_dynamic-update-slice_fusion.refs_0_), channel_id=1, source_target_pairs={{0,1},{1,0},{2,3},{3,2},{4,5},{5,4},{6,7},{7,6},{8,9},{9,8},{10,11... | collective-permute-start | bytes 2359304 | tf_op jit(solution)/shard_map/ppermute | solution.py:49
  88.2 12.6 %collective-permute-start.20 = (bf16[96,4096]{1,0:T(8,128)(2,1)}, bf16[96,4096]{1,0:T(8,128)(2,1)S(1)}, u32[]{:S(2)}, u32[]{:S(2)}) collective-permute-start(bf16[96,4096]{1,0:T(8,128)(2,1)} %collective-permute-done.15.refs_1_), channel_id=1, source_target_pairs={{0,1},{1,0},{2,3},{3,2},{4,5},{5,4},{6,7},{7,6},{8,9},{9,8},{10,11... | collective-permute-start | bytes 2359304 | tf_op jit(solution)/shard_map/ppermute | solution.py:49
  88.7 12.1 %collective-permute-start.21 = (bf16[96,4096]{1,0:T(8,128)(2,1)}, bf16[96,4096]{1,0:T(8,128)(2,1)}, u32[]{:S(2)}, u32[]{:S(2)}) collective-permute-start(bf16[96,4096]{1,0:T(8,128)(2,1)} %collective-permute-done.16.refs_2_), channel_id=1, source_target_pairs={{0,1},{1,0},{2,3},{3,2},{4,5},{5,4},{6,7},{7,6},{8,9},{9,8},{10,11... | collective-permute-start | bytes 2359304 | tf_op jit(solution)/shard_map/ppermute | solution.py:49
  125.5 13.8 %collective-permute-start.24 = (bf16[384,2048]{1,0:T(8,128)(2,1)}, bf16[384,2048]{1,0:T(8,128)(2,1)}, u32[]{:S(2)}, u32[]{:S(2)}) collective-permute-start(bf16[384,2048]{1,0:T(8,128)(2,1)} %get-tuple-element.43), channel_id=1, source_target_pairs={{0,1},{1,0},{2,3},{3,2},{4,5},{5,4},{6,7},{7,6},{8,9},{9,8},{10,11... | collective-permute-start | bytes 4718600 | tf_op jit(solution)/shard_map/ppermute | solution.py:49
  138.8 8.6 %collective-permute-start.32 = (bf16[384,2176]{1,0:T(8,128)(2,1)}, bf16[384,2176]{1,0:T(8,128)(2,1)S(1)}, u32[]{:S(2)}, u32[]{:S(2)}) collective-permute-start(bf16[384,2176]{1,0:T(8,128)(2,1)} %get-tuple-element.44), channel_id=1, source_target_pairs={{0,1},{1,0},{2,3},{3,2},{4,5},{5,4},{6,7},{7,6},{8,9},{9,8},{10,11... | collective-permute-start | bytes 5013512 | tf_op jit(solution)/shard_map/ppermute | solution.py:49
  141.4 9.1 %collective-permute-start.27 = (bf16[48,2048]{1,0:T(8,128)(2,1)S(1)}, bf16[48,2048]{1,0:T(8,128)(2,1)S(1)}, u32[]{:S(2)}, u32[]{:S(2)}) collective-permute-start(bf16[48,2048]{1,0:T(8,128)(2,1)S(1)} %get-tuple-element.67), channel_id=1, source_target_pairs={{0,2},{1,3},{2,0},{3,1},{4,6},{5,7},{6,4},{7,5},{8,10},{9,11},{10,... | collective-permute-start | bytes 589832 | tf_op jit(solution)/shard_map/ppermute | solution.py:49
  142.0 8.4 %collective-permute-start.25 = (bf16[48,2048]{1,0:T(8,128)(2,1)S(1)}, bf16[48,2048]{1,0:T(8,128)(2,1)S(1)}, u32[]{:S(2)}, u32[]{:S(2)}) collective-permute-start(bf16[48,2048]{1,0:T(8,128)(2,1)S(1)} %get-tuple-element.68), channel_id=1, source_target_pairs={{0,4},{1,5},{2,6},{3,7},{4,0},{5,1},{6,2},{7,3},{8,12},{9,13},{10,... | collective-permute-start | bytes 589832 | tf_op jit(solution)/shard_map/ppermute | solution.py:49
  147.9 8.7 %collective-permute-start.35 = (bf16[48,2176]{1,0:T(8,128)(2,1)S(1)}, bf16[48,2176]{1,0:T(8,128)(2,1)S(1)}, u32[]{:S(2)}, u32[]{:S(2)}) collective-permute-start(bf16[48,2176]{1,0:T(8,128)(2,1)S(1)} %get-tuple-element.61), channel_id=1, source_target_pairs={{0,2},{1,3},{2,0},{3,1},{4,6},{5,7},{6,4},{7,5},{8,10},{9,11},{10,... | collective-permute-start | bytes 626696 | tf_op jit(solution)/shard_map/ppermute | solution.py:49
  148.9 8.1 %collective-permute-start.33 = (bf16[48,2176]{1,0:T(8,128)(2,1)S(1)}, bf16[48,2176]{1,0:T(8,128)(2,1)S(1)}, u32[]{:S(2)}, u32[]{:S(2)}) collective-permute-start(bf16[48,2176]{1,0:T(8,128)(2,1)S(1)} %get-tuple-element.62), channel_id=1, source_target_pairs={{0,4},{1,5},{2,6},{3,7},{4,0},{5,1},{6,2},{7,3},{8,12},{9,13},{10,... | collective-permute-start | bytes 626696 | tf_op jit(solution)/shard_map/ppermute | solution.py:49
  150.6 14.9 %collective-permute-start.26 = (bf16[96,2048]{1,0:T(8,128)(2,1)S(1)}, bf16[96,2048]{1,0:T(8,128)(2,1)S(1)}, u32[]{:S(2)}, u32[]{:S(2)}) collective-permute-start(bf16[96,2048]{1,0:T(8,128)(2,1)S(1)} %pad_maximum_fusion.3), channel_id=1, source_target_pairs={{0,2},{1,3},{2,0},{3,1},{4,6},{5,7},{6,4},{7,5},{8,10},{9,11},{10,... | collective-permute-start | bytes 1179656 | tf_op jit(solution)/shard_map/ppermute | solution.py:49
  151.2 14.2 %collective-permute-start.28 = (bf16[96,2048]{1,0:T(8,128)(2,1)S(1)}, bf16[96,2048]{1,0:T(8,128)(2,1)S(1)}, u32[]{:S(2)}, u32[]{:S(2)}) collective-permute-start(bf16[96,2048]{1,0:T(8,128)(2,1)S(1)} %pad_maximum_fusion.4), channel_id=1, source_target_pairs={{0,4},{1,5},{2,6},{3,7},{4,0},{5,1},{6,2},{7,3},{8,12},{9,13},{10,... | collective-permute-start | bytes 1179656 | tf_op jit(solution)/shard_map/ppermute | solution.py:49
  157.2 17.9 %collective-permute-start.36 = (bf16[96,2176]{1,0:T(8,128)(2,1)S(1)}, bf16[96,2176]{1,0:T(8,128)(2,1)S(1)}, u32[]{:S(2)}, u32[]{:S(2)}) collective-permute-start(bf16[96,2176]{1,0:T(8,128)(2,1)S(1)} %pad_maximum_fusion.2), channel_id=1, source_target_pairs={{0,4},{1,5},{2,6},{3,7},{4,0},{5,1},{6,2},{7,3},{8,12},{9,13},{10,... | collective-permute-start | bytes 1253384 | tf_op jit(solution)/shard_map/ppermute | solution.py:49
  158.8 16.3 %collective-permute-start.34 = (bf16[96,2176]{1,0:T(8,128)(2,1)S(1)}, bf16[96,2176]{1,0:T(8,128)(2,1)S(1)}, u32[]{:S(2)}, u32[]{:S(2)}) collective-permute-start(bf16[96,2176]{1,0:T(8,128)(2,1)S(1)} %pad_maximum_fusion.1), channel_id=1, source_target_pairs={{0,2},{1,3},{2,0},{3,1},{4,6},{5,7},{6,4},{7,5},{8,10},{9,11},{10,... | collective-permute-start | bytes 1253384 | tf_op jit(solution)/shard_map/ppermute | solution.py:49
  165.6 7.8 %collective-permute-start.29 = (bf16[24,2048]{1,0:T(8,128)(2,1)S(1)}, bf16[24,2048]{1,0:T(8,128)(2,1)S(1)}, u32[]{:S(2)}, u32[]{:S(2)}) collective-permute-start(bf16[24,2048]{1,0:T(8,128)(2,1)S(1)} %get-tuple-element.74), channel_id=1, source_target_pairs={{0,8},{1,9},{2,10},{3,11},{4,12},{5,13},{6,14},{7,15},{8,0},{9,1},... | collective-permute-start | bytes 294920 | tf_op jit(solution)/shard_map/ppermute | solution.py:49
  165.7 7.8 %collective-permute-start.31 = (bf16[24,2048]{1,0:T(8,128)(2,1)S(1)}, bf16[24,2048]{1,0:T(8,128)(2,1)S(1)}, u32[]{:S(2)}, u32[]{:S(2)}) collective-permute-start(bf16[24,2048]{1,0:T(8,128)(2,1)S(1)} %get-tuple-element.75), channel_id=1, source_target_pairs={{0,24},{1,25},{2,26},{3,27},{4,28},{5,29},{6,30},{7,31},{8,16},{9,... | collective-permute-start | bytes 294920 | tf_op jit(solution)/shard_map/ppermute | solution.py:49
  175.3 7.8 %collective-permute-start.37 = (bf16[24,2176]{1,0:T(8,128)(2,1)S(1)}, bf16[24,2176]{1,0:T(8,128)(2,1)S(1)}, u32[]{:S(2)}, u32[]{:S(2)}) collective-permute-start(bf16[24,2176]{1,0:T(8,128)(2,1)S(1)} %get-tuple-element.71), channel_id=1, source_target_pairs={{0,8},{1,9},{2,10},{3,11},{4,12},{5,13},{6,14},{7,15},{8,0},{9,1},... | collective-permute-start | bytes 313352 | tf_op jit(solution)/shard_map/ppermute | solution.py:49
  (20 other events, 142.7 us)

commit v2 on v1

--- a/solution.py
+++ b/solution.py
@@ -191,11 +191,11 @@
     pull_ref[...] = (up_pre * (sig * (1.0 + gate_pre * (1.0 - sig)))).astype(bf16)
 
 
-def forward(x, w_gate, w_up, part, parts):
+def forward(x, w_gate, w_up, low, high):
     rows, width = x.shape
-    units = w_gate.shape[1] // parts
+    units = high - low
     block = tile(units, 256)
-    first = part * (units // block)
+    first = low // block
     weight = pl.BlockSpec((width, block), lambda i: (0, first + i))
     unit = pl.BlockSpec((rows, block), lambda i: (0, i))
     turned = pl.BlockSpec((block, rows), lambda i: (i, 0))
@@ -357,9 +357,9 @@
         forward_kernel(x, gates.at[at], ups.at[at], hidden_ref, turned_ref, active_ref, pull_ref)
 
 
-def pick_forward(slot, pieces, rows, w_gate, w_up, parts):
+def pick_forward(slot, pieces, rows, w_gate, w_up, units):
     sizes = [piece.shape[0] for piece in pieces]
-    cols, units = w_gate.shape[0], w_gate.shape[1] // parts
+    cols = w_gate.shape[0]
     picks, scratch = pick_scratch(rows, sizes, cols)
     block = tile(units, 256)
     blocks = units // block
@@ -387,7 +387,7 @@
     return x, ahead
 
 
-def pick_back_kernel(sizes, picks, blocks, steps, tokens, slot_ref, slot_col, gain_ref, *refs):
+def pick_back_kernel(sizes, picks, blocks, ranges, tokens, slot_ref, slot_col, gain_ref, *refs):
     count = len(sizes)
     pieces, (down_any, gate_any, up_any), refs = refs[:count], refs[count : count + 3], refs[count + 3 :]
     *refs, held, place, rows_ref, piece_sems, x_sems, downs, gates, ups, d_gate, d_up, sems, token_sems = refs
@@ -424,10 +424,10 @@
     def _():
         route_ref[...] = jnp.zeros_like(route_ref)
 
-    for k in range(len(parts) // 3):
+    for k, (low, high) in enumerate(ranges):
         hidden_ref, active_ref, pull_ref = parts[3 * k : 3 * k + 3]
 
-        @pl.when((step >= picks + k * steps) & (step < picks + (k + 1) * steps))
+        @pl.when((step >= picks + low) & (step < picks + high))
         def _(hidden_ref=hidden_ref, active_ref=active_ref, pull_ref=pull_ref):
             at = step - picks
             for copy in weights(at):
@@ -457,26 +457,27 @@
     rows = gain.shape[0]
     units, cols = w_down.shape
     picks, scratch = pick_scratch(rows, sizes, cols)
-    block = tile(parts[0][0].shape[1], 256)
+    block = min(tile(part[0].shape[1], 256) for part in parts)
     blocks = units // block
-    steps = blocks // len(parts)
+    ends = [sum(part[0].shape[1] for part in parts[: k + 1]) // block for k in range(len(parts))]
+    ranges = list(zip([0] + ends[:-1], ends))
     token_block = tile(cols, 512)
     tokens = high // token_block
     unit = pl.BlockSpec((rows, block), lambda i: (0, jnp.clip(i - picks, 0, blocks - 1)))
     dense = pl.BlockSpec((total // 2, token_block), lambda i: (0, jnp.maximum(i - picks - blocks, 0)))
 
     def unit_of(part):
-        return pl.BlockSpec((rows, block), lambda i: (0, jnp.clip(i - picks - part * steps, 0, steps - 1)))
+        return pl.BlockSpec((rows, block), lambda i: (0, jnp.clip(i - picks - part[0], 0, part[1] - part[0] - 1)))
 
     shape = jax.ShapeDtypeStruct((rows, units), bf16)
     return call(
-        functools.partial(pick_back_kernel, sizes, picks, blocks, steps, tokens),
+        functools.partial(pick_back_kernel, sizes, picks, blocks, ranges, tokens),
         2 * rows * (cols * units + total * cols + 2 * high * units + total * high),
         2 * cols * units + 4 * high * units + 2 * (rows + total) * cols,
         grid=(picks + blocks + tokens,),
         in_specs=[whole(1, total), whole(total, 1), whole(rows, 1)]
         + [ANY] * (len(sizes) + 3)
-        + [unit_of(k) for k in range(len(parts)) for _ in range(3)],
+        + [unit_of(part) for part in ranges for _ in range(3)],
         out_specs=[ANY, unit, unit, whole(rows, 1), dense, dense],
         out_shape=[
             jax.ShapeDtypeStruct((rows, cols), bf16),
@@ -601,12 +602,10 @@
     )
     first_t = gather_z(jnp.concatenate([tokens, meta], axis=1))
     x_t, y_t = gather_sides(first_t)
-    first_core = flip(first_t, CORE)
-    first_g = gather_z(after(grad_out, first_core))
+    first_g = gather_z(after(grad_out, first_t))
     far_t = gather_far(x_t, y_t)
     x_g, y_g = gather_sides(after(first_g, *far_t))
-    pieces_t = [first_t, x_t, y_t, *far_t, first_core]
-    pieces_t += [flip(piece, CORE) for piece in pieces_t[1:5]]
+    pieces_t = gather_core([first_t, x_t, y_t] + far_t)
     all_meta = gather_meta(pieces_t, cols)
     all_ids = all_meta[:, :top_count].astype(jnp.int32)
     all_weights = all_meta[:, top_count : 2 * top_count].astype(f32)
@@ -614,7 +613,7 @@
     fused = narrow_count == 1 and local_experts == 1
     chunks = CHUNKS if fused else 1
     units = w_gate.shape[2]
-    parts = 1 if fused or units % (2 * LANES) else 2
+    ahead_units = units * 2 // 3 if fused and units % (6 * LANES) == 0 else units
     picked = []
     for j in range(local_experts):
         match = all_ids == first + j
@@ -625,19 +624,19 @@
         place = slot[None, :] == jnp.arange(rows, dtype=jnp.int32)[:, None]
         row_gain = jnp.sum(jnp.where(place, gain[None, :], 0.0), axis=1, keepdims=True)
         if fused:
-            x, first_part = pick_forward(slot, pieces_t, rows, w_gate[j], w_up[j], parts)
+            x, first_part = pick_forward(slot, pieces_t, rows, w_gate[j], w_up[j], ahead_units)
         else:
             x = pick_rows(slot, pieces_t, rows, cols)
             x = lax.all_gather(x, "narrow", axis=1, tiled=True)
-            first_part = forward(x, w_gate[j], w_up[j], 0, parts)
+            first_part = forward(x, w_gate[j], w_up[j], 0, ahead_units)
         ahead = [first_part]
         picked.append((slot, place, row_gain, x, ahead))
     x_g, y_g, *_ = lax.optimization_barrier((x_g, y_g, *[ahead[0][0] for *_, ahead in picked]))
     far_g = gather_far(x_g, y_g)
     for j in range(local_experts):
         slot, place, row_gain, x, ahead = picked[j]
-        if parts == 2:
-            ahead.append(forward(after(x, x_g, y_g), w_gate[j], w_up[j], 1, parts))
+        if ahead_units < units:
+            ahead.append(forward(after(x, x_g, y_g), w_gate[j], w_up[j], ahead_units, units))
     far_g = lax.optimization_barrier((*far_g, *[ahead[-1][0] for *_, ahead in picked]))[: len(far_g)]
     pieces_g = gather_core([first_g, x_g, y_g, *far_g])
     expert_cols = experts_all + -experts_all % LANES

time: 187 us -> 184 us (0.984)
  waiting for transfers between devices: 55.6 us -> 50.3 us
  Pallas kernels: 72.6 us -> 76.4 us
    pallas_call x1 -> x2, Pallas kernels: 23.8 us -> 31.5 us  [the longest x1 24.4 us: pick_back(): call(functools.partial(pick_back_kernel, sizes, picks, blocks, ranges, to...]
    ppermute x40, waiting for transfers between devices: 55.6 us -> 50.3 us  [flip(): return lax.ppermute(value, 'wide', [(i, i ^ mask) for i in range(count)])]
    pallas_call x1, Pallas kernels: 19.1 us -> 15.2 us  [pick_forward(): call(functools.partial(pick_forward_kernel, sizes, picks, blocks), 4 * ro...]
    unnamed x31 -> x37, local copies, waits for them, and re-layouts: 7.78 us -> 7.03 us
  transfers between devices with their start and end apart: 40 -> 40, of which waited for: 13 -> 15; matrix products, arithmetic and copies ran while one was open for 5% -> 6% of each run, Pallas kernels for 26% -> 28%
where the time goes in v2:
time: 184 us; the launch traced here: 183 us
  Pallas kernels  76.4 us (42%)
  waiting for transfers between devices  50.3 us (27%)
  starting transfers between devices  37.5 us (20%)
  local copies, waits for them, and re-layouts  11.4 us (6%)
  other arithmetic  6.89 us (4%)
    ppermute x40, waiting for transfers between devices, flip(): return lax.ppermute(value, 'wide', [(i, i ^ mask) for i in range(count)])  50.3 us
    ppermute x40, starting transfers between devices, flip(): return lax.ppermute(value, 'wide', [(i, i ^ mask) for i in range(count)])  37.5 us
    pallas_call x1, Pallas kernels, pick_back(): call(functools.partial(pick_back_kernel, sizes, picks, blocks, ranges, to...  24.4 us
    pallas_call x4, Pallas kernels, down_grad(): call(functools.partial(down_kernel, len(turned)), 2 * rows * width * unit...  17.3 us
    pallas_call x1, Pallas kernels, pick_forward(): call(functools.partial(pick_forward_kernel, sizes, picks, blocks), 4 * ro...  15.2 us
    pallas_call x1, Pallas kernels, token_grad(): call(functools.partial(token_kernel, steps, spread), 4 * rows * width * u...  11.4 us
    pallas_call x1, Pallas kernels, forward(): call(forward_kernel, 4 * rows * width * units, 4 * width * units, grid=(u...  7.16 us
    unnamed x37, local copies, waits for them, and re-layouts  7.03 us
  transfers between devices with their start and end apart: 40, of which 15 were waited for; matrix products, arithmetic and copies ran while one was open for 6% of the time, Pallas kernels for 28%

profile of v2, /device:TPU:0, one launch (start us, length us, event | category | flops | bytes accessed | tf_op | source)
XLA Modules:
  0.0 183.5 jit_solution(15225271514665158319)
XLA Ops:
  3.2 5.1 %collective-permute-start.2 = (bf16[24,4224]{1,0:T(8,128)(2,1)S(1)}, bf16[24,4224]{1,0:T(8,128)(2,1)S(1)}, u32[]{:S(2)}, u32[]{:S(2)}) collective-permute-start(bf16[24,4224]{1,0:T(8,128)(2,1)S(1)} %concatenate.24), channel_id=1, source_target_pairs={{0,24},{1,25},{2,26},{3,27},{4,28},{5,29},{6,30},{7,31},{8,16},{9,... | collective-permute-start | bytes 608264 | tf_op jit(solution)/shard_map/ppermute | solution.py:49
  9.0 5.4 %collective-permute-done.2 = bf16[24,4224]{1,0:T(8,128)(2,1)S(1)} collective-permute-done((bf16[24,4224]{1,0:T(8,128)(2,1)S(1)}, bf16[24,4224]{1,0:T(8,128)(2,1)S(1)}, u32[]{:S(2)}, u32[]{:S(2)}) %collective-permute-start.2) | collective-permute-done | bytes 202784 | tf_op jit(solution)/shard_map/ppermute | solution.py:49
  14.3 11.2 %collective-permute-done.1 = bf16[24,4224]{1,0:T(8,128)(2,1)S(1)} collective-permute-done((bf16[24,4224]{1,0:T(8,128)(2,1)S(1)}, bf16[24,4224]{1,0:T(8,128)(2,1)S(1)}, u32[]{:S(2)}, u32[]{:S(2)}) %collective-permute-start.1) | collective-permute-done | bytes 202784 | tf_op jit(solution)/shard_map/ppermute | solution.py:49
  25.6 2.6 %collective-permute-start.14 = (bf16[24,4096]{1,0:T(8,128)(2,1)S(1)}, bf16[24,4096]{1,0:T(8,128)(2,1)S(1)}, u32[]{:S(2)}, u32[]{:S(2)}) collective-permute-start(bf16[24,4096]{1,0:T(8,128)(2,1)S(1)} %copy-done.12), channel_id=1, source_target_pairs={{0,24},{1,25},{2,26},{3,27},{4,28},{5,29},{6,30},{7,31},{8,16},{9,... | collective-permute-start | bytes 589832 | tf_op jit(solution)/shard_map/ppermute | solution.py:49
  28.3 1.8 %collective-permute-start.12 = (bf16[24,4096]{1,0:T(8,128)(2,1)S(1)}, bf16[24,4096]{1,0:T(8,128)(2,1)S(1)}, u32[]{:S(2)}, u32[]{:S(2)}) collective-permute-start(bf16[24,4096]{1,0:T(8,128)(2,1)S(1)} %copy-done.12), channel_id=1, source_target_pairs={{0,8},{1,9},{2,10},{3,11},{4,12},{5,13},{6,14},{7,15},{8,0},{9,1},... | collective-permute-start | bytes 589832 | tf_op jit(solution)/shard_map/ppermute | solution.py:49
  30.1 1.5 collective-permute-start.4
  31.6 1.5 collective-permute-start.3
  33.8 6.2 %collective-permute-done.12 = bf16[24,4096]{1,0:T(8,128)(2,1)S(1)} collective-permute-done((bf16[24,4096]{1,0:T(8,128)(2,1)S(1)}, bf16[24,4096]{1,0:T(8,128)(2,1)S(1)}, u32[]{:S(2)}, u32[]{:S(2)}) %collective-permute-start.12) | collective-permute-done | bytes 196640 | tf_op jit(solution)/shard_map/ppermute | solution.py:49
  40.7 7.7 %collective-permute-done.4.refs_2_ = bf16[96,4224]{1,0:T(8,128)(2,1)S(1)} collective-permute-done((bf16[96,4224]{1,0:T(8,128)(2,1)S(1)}, bf16[96,4224]{1,0:T(8,128)(2,1)S(1)}, u32[]{:S(2)}, u32[]{:S(2)}) %collective-permute-start.4) | collective-permute-done | bytes 811040 | tf_op jit(solution)/shard_map/ppermute | solution.py:49
  48.4 1.6 collective-permute-start.5
  52.8 5.5 %collective-permute-done.5.refs_3_ = bf16[48,4224]{1,0:T(8,128)(2,1)S(1)} collective-permute-done((bf16[48,4224]{1,0:T(8,128)(2,1)S(1)}, bf16[48,4224]{1,0:T(8,128)(2,1)S(1)}, u32[]{:S(2)}, u32[]{:S(2)}) %collective-permute-start.5) | collective-permute-done | bytes 405536 | tf_op jit(solution)/shard_map/ppermute | solution.py:49
  60.0 1.3 collective-permute-start.16
  63.9 15.2 %shard_map.95 = (bf16[384,4096]{1,0:T(8,128)(2,1)}, bf16[384,1024]{1,0:T(8,128)(2,1)}, bf16[1024,384]{1,0:T(8,128)(2,1)}, bf16[384,1024]{1,0:T(8,128)(2,1)}, bf16[384,1024]{1,0:T(8,128)(2,1)}) custom-call(s32[1,768]{1,0:T(1,128)S(1)} %get-tuple-element.69.slot_ref, bf16[96,4224]{1,0:T(8,128)(2,1)} %copy-done.5, bf16[96,4224]{1,0:T(8,128)(2,1)} %copy-done.7, ...), custom_call_target="tpu_custom_call" | custom-call | flops 8858370048 | bytes 26214400 | tf_op jit(solution)/shard_map/pallas_call | solution.py:369
  80.8 1.0 slice.122
  81.8 1.0 slice.121
  83.7 1.5 collective-permute-start.18
  85.8 7.2 %shard_map.96 = (bf16[384,512]{1,0:T(8,128)(2,1)S(1)}, bf16[512,384]{1,0:T(8,128)(2,1)S(1)}, bf16[384,512]{1,0:T(8,128)(2,1)S(1)}, bf16[384,512]{1,0:T(8,128)(2,1)S(1)}) custom-call(bf16[384,4096]{1,0:T(8,128)(2,1)} %get-tuple-element.39.x_ref, bf16[4096,1536]{1,0:T(8,128)(2,1)} %bitcast.21, bf16[4096,1536]{1,0:T(8,128)(2,1)} %bitcast.25), custom_call_target="tpu_custom_call" | custom-call | flops 3221225472 | bytes 8388608 | tf_op jit(solution)/shard_map/pallas_call | solution.py:203
  97.1 24.4 %shard_map.97 = (bf16[384,4096]{1,0:T(8,128)(2,1)}, bf16[384,1536]{1,0:T(8,128)(2,1)}, bf16[384,1536]{1,0:T(8,128)(2,1)}, f32[384,1]{1,0:T(8,128)S(1)}, bf16[384...) custom-call(s32[1,768]{1,0:T(1,128)S(1)} %get-tuple-element.69.slot_ref, s32[768,1]{1,0:T(8,128)S(1)} %bitcast_select_fusion.slot_col.slot_ref, ...), custom_call_target="tpu_custom_call" | custom-call | flops 13287555072 | bytes 34603008 | tf_op jit(solution)/shard_map/pallas_call | solution.py:473
  122.0 1.3 copy-done.1
  123.2 11.4 %shard_map.98 = (bf16[384,2176]{1,0:T(8,128)(2,1)}, bf16[384,2176]{1,0:T(8,128)(2,1)}) custom-call(bf16[384,1536]{1,0:T(8,128)(2,1)S(1)} %copy-done.1, bf16[384,1536]{1,0:T(8,128)(2,1)} %get-tuple-element.50.d_up_ref, s32[768,1]{1,0:T(8,128)S(1)} %bitcast_select_fusion.slot_col.slot_ref, bf16[384,128]{1,0:T(8,128)(2,1)S(1)} %select_convert_fusion.route_ref, ...), custom_call_target="tpu_custom_call" | custom-call | flops 6039797760 | bytes 15728640 | tf_op jit(solution)/shard_map/pallas_call | solution.py:547
  135.1 2.5 %add_convert_fusion.1 = bf16[384,2048]{1,0:T(8,128)(2,1)S(1)} fusion(bf16[384,2048]{1,0:T(8,128)(2,1)} %collective-permute-done.24, bf16[384,2048]{1,0:T(8,128)(2,1)} %get-tuple-element.53), kind=kLoop, calls=%fused_computation.1 | loop fusion | flops 3145728 | bytes 4718592 | tf_op jit(solution)/shard_map/convert_element_type | solution.py:23
  139.6 4.4 %shard_map.99.refs_2_ = bf16[1536,4096]{1,0:T(8,128)(2,1)} custom-call(bf16[384,4096]{1,0:T(8,128)(2,1)} %get-tuple-element.62.g_ref, f32[384,1]{1,0:T(8,128)S(1)} %broadcast_in_dim.81.gain_ref, bf16[1024,384]{1,0:T(8,128)(2,1)S(1)} %copy-done, bf16[512,384]{1,0:T(8,128)(2,1)S(1)} %get-tuple-element.59.refs_1_), custom_call_target="tpu_custom_call" | custom-call | flops 1207959552 | bytes 3145728 | tf_op jit(solution)/shard_map/pallas_call | solution.py:574
  144.5 1.4 collective-permute-start.35
  147.9 1.0 collective-permute-start.28
  148.9 4.3 %shard_map.100.refs_2_ = bf16[1536,4096]{1,0:T(8,128)(2,1)} custom-call(bf16[384,4096]{1,0:T(8,128)(2,1)} %get-tuple-element.62.g_ref, f32[384,1]{1,0:T(8,128)S(1)} %broadcast_in_dim.81.gain_ref, bf16[1024,384]{1,0:T(8,128)(2,1)S(1)} %copy-done, bf16[512,384]{1,0:T(8,128)(2,1)S(1)} %get-tuple-element.59.refs_1_, ...), custom_call_target="tpu_custom_call", output_to_operand_aliasing={{}: (4, {})} | custom-call | flops 1207959552 | bytes 3145728 | tf_op jit(solution)/shard_map/pallas_call | solution.py:574
  156.0 6.4 %collective-permute-done.28 = bf16[96,2048]{1,0:T(8,128)(2,1)S(1)} collective-permute-done((bf16[96,2048]{1,0:T(8,128)(2,1)S(1)}, bf16[96,2048]{1,0:T(8,128)(2,1)S(1)}, u32[]{:S(2)}, u32[]{:S(2)}) %collective-permute-start.28) | collective-permute-done | bytes 393248 | tf_op jit(solution)/shard_map/ppermute | solution.py:49
  163.0 2.2 %collective-permute-start.31 = (bf16[24,2048]{1,0:T(8,128)(2,1)S(1)}, bf16[24,2048]{1,0:T(8,128)(2,1)S(1)}, u32[]{:S(2)}, u32[]{:S(2)}) collective-permute-start(bf16[24,2048]{1,0:T(8,128)(2,1)S(1)} %get-tuple-element.87), channel_id=1, source_target_pairs={{0,24},{1,25},{2,26},{3,27},{4,28},{5,29},{6,30},{7,31},{8,16},{9,... | collective-permute-start | bytes 294920 | tf_op jit(solution)/shard_map/ppermute | solution.py:49
  166.2 4.3 %shard_map.101.refs_2_ = bf16[1536,4096]{1,0:T(8,128)(2,1)} custom-call(bf16[384,4096]{1,0:T(8,128)(2,1)} %get-tuple-element.62.g_ref, f32[384,1]{1,0:T(8,128)S(1)} %broadcast_in_dim.81.gain_ref, bf16[1024,384]{1,0:T(8,128)(2,1)S(1)} %copy-done, bf16[512,384]{1,0:T(8,128)(2,1)S(1)} %get-tuple-element.59.refs_1_, ...), custom_call_target="tpu_custom_call", output_to_operand_aliasing={{}: (4, {})} | custom-call | flops 1207959552 | bytes 3145728 | tf_op jit(solution)/shard_map/pallas_call | solution.py:574
  170.4 1.6 collective-permute-done.30
  172.4 2.6 %collective-permute-start.39 = (bf16[24,2176]{1,0:T(8,128)(2,1)S(1)}, bf16[24,2176]{1,0:T(8,128)(2,1)S(1)}, u32[]{:S(2)}, u32[]{:S(2)}) collective-permute-start(bf16[24,2176]{1,0:T(8,128)(2,1)S(1)} %get-tuple-element.84), channel_id=1, source_target_pairs={{0,24},{1,25},{2,26},{3,27},{4,28},{5,29},{6,30},{7,31},{8,16},{9,... | collective-permute-start | bytes 313352 | tf_op jit(solution)/shard_map/ppermute | solution.py:49
  175.9 4.3 %shard_map.102 = bf16[1536,4096]{1,0:T(8,128)(2,1)} custom-call(bf16[384,4096]{1,0:T(8,128)(2,1)} %get-tuple-element.62.g_ref, f32[384,1]{1,0:T(8,128)S(1)} %broadcast_in_dim.81.gain_ref, bf16[1024,384]{1,0:T(8,128)(2,1)S(1)} %copy-done, bf16[512,384]{1,0:T(8,128)(2,1)S(1)} %get-tuple-element.59.refs_1_, ...), custom_call_target="tpu_custom_call", output_to_operand_aliasing={{}: (4, {})} | custom-call | flops 1207959552 | bytes 3145728 | tf_op jit(solution)/shard_map/pallas_call | solution.py:574
  180.2 1.7 collective-permute-done.38
  (139 shorter events, 31.4 us)
Async XLA Ops:
  3.2 11.1 %collective-permute-start.2 = (bf16[24,4224]{1,0:T(8,128)(2,1)S(1)}, bf16[24,4224]{1,0:T(8,128)(2,1)S(1)}, u32[]{:S(2)}, u32[]{:S(2)}) collective-permute-start(bf16[24,4224]{1,0:T(8,128)(2,1)S(1)} %concatenate.24), channel_id=1, source_target_pairs={{0,24},{1,25},{2,26},{3,27},{4,28},{5,29},{6,30},{7,31},{8,16},{9,... | collective-permute-start | bytes 608264 | tf_op jit(solution)/shard_map/ppermute | solution.py:49
  8.3 17.2 %collective-permute-start.1 = (bf16[24,4224]{1,0:T(8,128)(2,1)S(1)}, bf16[24,4224]{1,0:T(8,128)(2,1)S(1)}, u32[]{:S(2)}, u32[]{:S(2)}) collective-permute-start(bf16[24,4224]{1,0:T(8,128)(2,1)S(1)} %concatenate.24), channel_id=1, source_target_pairs={{0,16},{1,17},{2,18},{3,19},{4,20},{5,21},{6,22},{7,23},{8,24},{9,... | collective-permute-start | bytes 608264 | tf_op jit(solution)/shard_map/ppermute | solution.py:49
  8.3 17.2 %collective-permute-start = (bf16[24,4224]{1,0:T(8,128)(2,1)S(1)}, bf16[24,4224]{1,0:T(8,128)(2,1)S(1)}, u32[]{:S(2)}, u32[]{:S(2)}) collective-permute-start(bf16[24,4224]{1,0:T(8,128)(2,1)S(1)} %concatenate.24), channel_id=1, source_target_pairs={{0,8},{1,9},{2,10},{3,11},{4,12},{5,13},{6,14},{7,15},{8,0},{9,1},... | collective-permute-start | bytes 608264 | tf_op jit(solution)/shard_map/ppermute | solution.py:49
  25.6 26.0 %collective-permute-start.14 = (bf16[24,4096]{1,0:T(8,128)(2,1)S(1)}, bf16[24,4096]{1,0:T(8,128)(2,1)S(1)}, u32[]{:S(2)}, u32[]{:S(2)}) collective-permute-start(bf16[24,4096]{1,0:T(8,128)(2,1)S(1)} %copy-done.12), channel_id=1, source_target_pairs={{0,24},{1,25},{2,26},{3,27},{4,28},{5,29},{6,30},{7,31},{8,16},{9,... | collective-permute-start | bytes 589832 | tf_op jit(solution)/shard_map/ppermute | solution.py:49
  28.2 23.4 %collective-permute-start.13 = (bf16[24,4096]{1,0:T(8,128)(2,1)S(1)}, bf16[24,4096]{1,0:T(8,128)(2,1)S(1)}, u32[]{:S(2)}, u32[]{:S(2)}) collective-permute-start(bf16[24,4096]{1,0:T(8,128)(2,1)S(1)} %copy-done.12), channel_id=1, source_target_pairs={{0,16},{1,17},{2,18},{3,19},{4,20},{5,21},{6,22},{7,23},{8,24},{9,... | collective-permute-start | bytes 589832 | tf_op jit(solution)/shard_map/ppermute | solution.py:49
  28.3 11.7 %collective-permute-start.12 = (bf16[24,4096]{1,0:T(8,128)(2,1)S(1)}, bf16[24,4096]{1,0:T(8,128)(2,1)S(1)}, u32[]{:S(2)}, u32[]{:S(2)}) collective-permute-start(bf16[24,4096]{1,0:T(8,128)(2,1)S(1)} %copy-done.12), channel_id=1, source_target_pairs={{0,8},{1,9},{2,10},{3,11},{4,12},{5,13},{6,14},{7,15},{8,0},{9,1},... | collective-permute-start | bytes 589832 | tf_op jit(solution)/shard_map/ppermute | solution.py:49
  30.1 18.3 %collective-permute-start.4 = (bf16[96,4224]{1,0:T(8,128)(2,1)S(1)}, bf16[96,4224]{1,0:T(8,128)(2,1)S(1)}, u32[]{:S(2)}, u32[]{:S(2)}) collective-permute-start(bf16[96,4224]{1,0:T(8,128)(2,1)S(1)} %pad_maximum_fusion.refs_0_), channel_id=1, source_target_pairs={{0,4},{1,5},{2,6},{3,7},{4,0},{5,1},{6,2},{7,3},{8,12},{9,13},{10,... | collective-permute-start | bytes 2433032 | tf_op jit(solution)/shard_map/ppermute | solution.py:49
  31.6 19.1 %collective-permute-start.3 = (bf16[96,4224]{1,0:T(8,128)(2,1)S(1)}, bf16[96,4224]{1,0:T(8,128)(2,1)S(1)}, u32[]{:S(2)}, u32[]{:S(2)}) collective-permute-start(bf16[96,4224]{1,0:T(8,128)(2,1)S(1)} %pad_maximum_fusion.refs_0_), channel_id=1, source_target_pairs={{0,2},{1,3},{2,0},{3,1},{4,6},{5,7},{6,4},{7,5},{8,10},{9,11},{10,... | collective-permute-start | bytes 2433032 | tf_op jit(solution)/shard_map/ppermute | solution.py:49
  40.0 19.6 %collective-permute-start.7 = (bf16[96,4224]{1,0:T(8,128)(2,1)S(1)}, bf16[96,4224]{1,0:T(8,128)(2,1)S(1)}, u32[]{:S(2)}, u32[]{:S(2)}) collective-permute-start(bf16[96,4224]{1,0:T(8,128)(2,1)S(1)} %pad_maximum_fusion.refs_0_), channel_id=1, source_target_pairs={{0,1},{1,0},{2,3},{3,2},{4,5},{5,4},{6,7},{7,6},{8,9},{9,8},{10,11... | collective-permute-start | bytes 2433032 | tf_op jit(solution)/shard_map/ppermute | solution.py:49
  48.4 9.9 %collective-permute-start.5 = (bf16[48,4224]{1,0:T(8,128)(2,1)S(1)}, bf16[48,4224]{1,0:T(8,128)(2,1)S(1)}, u32[]{:S(2)}, u32[]{:S(2)}) collective-permute-start(bf16[48,4224]{1,0:T(8,128)(2,1)S(1)} %slice.147), channel_id=1, source_target_pairs={{0,2},{1,3},{2,0},{3,1},{4,6},{5,7},{6,4},{7,5},{8,10},{9,11},{10,... | collective-permute-start | bytes 1216520 | tf_op jit(solution)/shard_map/ppermute | solution.py:49
  50.7 8.0 %collective-permute-start.6 = (bf16[48,4224]{1,0:T(8,128)(2,1)S(1)}, bf16[48,4224]{1,0:T(8,128)(2,1)S(1)}, u32[]{:S(2)}, u32[]{:S(2)}) collective-permute-start(bf16[48,4224]{1,0:T(8,128)(2,1)S(1)} %slice.148), channel_id=1, source_target_pairs={{0,4},{1,5},{2,6},{3,7},{4,0},{5,1},{6,2},{7,3},{8,12},{9,13},{10,... | collective-permute-start | bytes 1216520 | tf_op jit(solution)/shard_map/ppermute | solution.py:49
  51.6 8.4 %collective-permute-start.9 = (bf16[96,4224]{1,0:T(8,128)(2,1)S(1)}, bf16[96,4224]{1,0:T(8,128)(2,1)S(1)}, u32[]{:S(2)}, u32[]{:S(2)}) collective-permute-start(bf16[96,4224]{1,0:T(8,128)(2,1)S(1)} %collective-permute-done.4.refs_2_), channel_id=1, source_target_pairs={{0,1},{1,0},{2,3},{3,2},{4,5},{5,4},{6,7},{7,6},{8,9},{9,8},{10,11... | collective-permute-start | bytes 2433032 | tf_op jit(solution)/shard_map/ppermute | solution.py:49
  51.6 9.6 %collective-permute-start.8 = (bf16[96,4224]{1,0:T(8,128)(2,1)S(1)}, bf16[96,4224]{1,0:T(8,128)(2,1)S(1)}, u32[]{:S(2)}, u32[]{:S(2)}) collective-permute-start(bf16[96,4224]{1,0:T(8,128)(2,1)S(1)} %collective-permute-done.3.refs_1_), channel_id=1, source_target_pairs={{0,1},{1,0},{2,3},{3,2},{4,5},{5,4},{6,7},{7,6},{8,9},{9,8},{10,11... | collective-permute-start | bytes 2433032 | tf_op jit(solution)/shard_map/ppermute | solution.py:49
  59.5 35.7 %collective-permute-start.19 = (bf16[96,4096]{1,0:T(8,128)(2,1)}, bf16[96,4096]{1,0:T(8,128)(2,1)}, u32[]{:S(2)}, u32[]{:S(2)}) collective-permute-start(bf16[96,4096]{1,0:T(8,128)(2,1)} %constant_dynamic-update-slice_fusion.refs_0_), channel_id=1, source_target_pairs={{0,1},{1,0},{2,3},{3,2},{4,5},{5,4},{6,7},{7,6},{8,9},{9,8},{10,11... | collective-permute-start | bytes 2359304 | tf_op jit(solution)/shard_map/ppermute | solution.py:49
  60.0 19.9 %collective-permute-start.16 = (bf16[96,4096]{1,0:T(8,128)(2,1)}, bf16[96,4096]{1,0:T(8,128)(2,1)}, u32[]{:S(2)}, u32[]{:S(2)}) collective-permute-start(bf16[96,4096]{1,0:T(8,128)(2,1)} %constant_dynamic-update-slice_fusion.refs_0_), channel_id=1, source_target_pairs={{0,4},{1,5},{2,6},{3,7},{4,0},{5,1},{6,2},{7,3},{8,12},{9,13},{10,... | collective-permute-start | bytes 2359304 | tf_op jit(solution)/shard_map/ppermute | solution.py:49
  61.2 19.6 %collective-permute-start.15 = (bf16[96,4096]{1,0:T(8,128)(2,1)}, bf16[96,4096]{1,0:T(8,128)(2,1)}, u32[]{:S(2)}, u32[]{:S(2)}) collective-permute-start(bf16[96,4096]{1,0:T(8,128)(2,1)} %constant_dynamic-update-slice_fusion.refs_0_), channel_id=1, source_target_pairs={{0,2},{1,3},{2,0},{3,1},{4,6},{5,7},{6,4},{7,5},{8,10},{9,11},{10,... | collective-permute-start | bytes 2359304 | tf_op jit(solution)/shard_map/ppermute | solution.py:49
  82.9 10.9 %collective-permute-start.17 = (bf16[48,4096]{1,0:T(8,128)(2,1)S(1)}, bf16[48,4096]{1,0:T(8,128)(2,1)S(1)}, u32[]{:S(2)}, u32[]{:S(2)}) collective-permute-start(bf16[48,4096]{1,0:T(8,128)(2,1)S(1)} %slice.121), channel_id=1, source_target_pairs={{0,2},{1,3},{2,0},{3,1},{4,6},{5,7},{6,4},{7,5},{8,10},{9,11},{10,... | collective-permute-start | bytes 1179656 | tf_op jit(solution)/shard_map/ppermute | solution.py:49
  83.7 10.1 %collective-permute-start.18 = (bf16[48,4096]{1,0:T(8,128)(2,1)S(1)}, bf16[48,4096]{1,0:T(8,128)(2,1)S(1)}, u32[]{:S(2)}, u32[]{:S(2)}) collective-permute-start(bf16[48,4096]{1,0:T(8,128)(2,1)S(1)} %slice.122), channel_id=1, source_target_pairs={{0,4},{1,5},{2,6},{3,7},{4,0},{5,1},{6,2},{7,3},{8,12},{9,13},{10,... | collective-permute-start | bytes 1179656 | tf_op jit(solution)/shard_map/ppermute | solution.py:49
  85.3 11.0 %collective-permute-start.20 = (bf16[96,4096]{1,0:T(8,128)(2,1)}, bf16[96,4096]{1,0:T(8,128)(2,1)S(1)}, u32[]{:S(2)}, u32[]{:S(2)}) collective-permute-start(bf16[96,4096]{1,0:T(8,128)(2,1)} %collective-permute-done.15.refs_1_), channel_id=1, source_target_pairs={{0,1},{1,0},{2,3},{3,2},{4,5},{5,4},{6,7},{7,6},{8,9},{9,8},{10,11... | collective-permute-start | bytes 2359304 | tf_op jit(solution)/shard_map/ppermute | solution.py:49
  85.3 11.0 %collective-permute-start.21 = (bf16[96,4096]{1,0:T(8,128)(2,1)}, bf16[96,4096]{1,0:T(8,128)(2,1)}, u32[]{:S(2)}, u32[]{:S(2)}) collective-permute-start(bf16[96,4096]{1,0:T(8,128)(2,1)} %collective-permute-done.16.refs_2_), channel_id=1, source_target_pairs={{0,1},{1,0},{2,3},{3,2},{4,5},{5,4},{6,7},{7,6},{8,9},{9,8},{10,11... | collective-permute-start | bytes 2359304 | tf_op jit(solution)/shard_map/ppermute | solution.py:49
  121.5 13.6 %collective-permute-start.24 = (bf16[384,2048]{1,0:T(8,128)(2,1)}, bf16[384,2048]{1,0:T(8,128)(2,1)}, u32[]{:S(2)}, u32[]{:S(2)}) collective-permute-start(bf16[384,2048]{1,0:T(8,128)(2,1)} %get-tuple-element.54), channel_id=1, source_target_pairs={{0,1},{1,0},{2,3},{3,2},{4,5},{5,4},{6,7},{7,6},{8,9},{9,8},{10,11... | collective-permute-start | bytes 4718600 | tf_op jit(solution)/shard_map/ppermute | solution.py:49
  134.6 9.4 %collective-permute-start.32 = (bf16[384,2176]{1,0:T(8,128)(2,1)}, bf16[384,2176]{1,0:T(8,128)(2,1)S(1)}, u32[]{:S(2)}, u32[]{:S(2)}) collective-permute-start(bf16[384,2176]{1,0:T(8,128)(2,1)} %get-tuple-element.55), channel_id=1, source_target_pairs={{0,1},{1,0},{2,3},{3,2},{4,5},{5,4},{6,7},{7,6},{8,9},{9,8},{10,11... | collective-permute-start | bytes 5013512 | tf_op jit(solution)/shard_map/ppermute | solution.py:49
  137.7 9.1 %collective-permute-start.27 = (bf16[48,2048]{1,0:T(8,128)(2,1)S(1)}, bf16[48,2048]{1,0:T(8,128)(2,1)S(1)}, u32[]{:S(2)}, u32[]{:S(2)}) collective-permute-start(bf16[48,2048]{1,0:T(8,128)(2,1)S(1)} %get-tuple-element.79), channel_id=1, source_target_pairs={{0,2},{1,3},{2,0},{3,1},{4,6},{5,7},{6,4},{7,5},{8,10},{9,11},{10,... | collective-permute-start | bytes 589832 | tf_op jit(solution)/shard_map/ppermute | solution.py:49
  138.6 8.2 %collective-permute-start.25 = (bf16[48,2048]{1,0:T(8,128)(2,1)S(1)}, bf16[48,2048]{1,0:T(8,128)(2,1)S(1)}, u32[]{:S(2)}, u32[]{:S(2)}) collective-permute-start(bf16[48,2048]{1,0:T(8,128)(2,1)S(1)} %get-tuple-element.80), channel_id=1, source_target_pairs={{0,4},{1,5},{2,6},{3,7},{4,0},{5,1},{6,2},{7,3},{8,12},{9,13},{10,... | collective-permute-start | bytes 589832 | tf_op jit(solution)/shard_map/ppermute | solution.py:49
  144.5 8.7 %collective-permute-start.35 = (bf16[48,2176]{1,0:T(8,128)(2,1)S(1)}, bf16[48,2176]{1,0:T(8,128)(2,1)S(1)}, u32[]{:S(2)}, u32[]{:S(2)}) collective-permute-start(bf16[48,2176]{1,0:T(8,128)(2,1)S(1)} %get-tuple-element.73), channel_id=1, source_target_pairs={{0,2},{1,3},{2,0},{3,1},{4,6},{5,7},{6,4},{7,5},{8,10},{9,11},{10,... | collective-permute-start | bytes 626696 | tf_op jit(solution)/shard_map/ppermute | solution.py:49
  145.9 8.1 %collective-permute-start.33 = (bf16[48,2176]{1,0:T(8,128)(2,1)S(1)}, bf16[48,2176]{1,0:T(8,128)(2,1)S(1)}, u32[]{:S(2)}, u32[]{:S(2)}) collective-permute-start(bf16[48,2176]{1,0:T(8,128)(2,1)S(1)} %get-tuple-element.74), channel_id=1, source_target_pairs={{0,4},{1,5},{2,6},{3,7},{4,0},{5,1},{6,2},{7,3},{8,12},{9,13},{10,... | collective-permute-start | bytes 626696 | tf_op jit(solution)/shard_map/ppermute | solution.py:49
  147.0 15.4 %collective-permute-start.26 = (bf16[96,2048]{1,0:T(8,128)(2,1)S(1)}, bf16[96,2048]{1,0:T(8,128)(2,1)S(1)}, u32[]{:S(2)}, u32[]{:S(2)}) collective-permute-start(bf16[96,2048]{1,0:T(8,128)(2,1)S(1)} %pad_maximum_fusion.3), channel_id=1, source_target_pairs={{0,2},{1,3},{2,0},{3,1},{4,6},{5,7},{6,4},{7,5},{8,10},{9,11},{10,... | collective-permute-start | bytes 1179656 | tf_op jit(solution)/shard_map/ppermute | solution.py:49
  147.9 14.5 %collective-permute-start.28 = (bf16[96,2048]{1,0:T(8,128)(2,1)S(1)}, bf16[96,2048]{1,0:T(8,128)(2,1)S(1)}, u32[]{:S(2)}, u32[]{:S(2)}) collective-permute-start(bf16[96,2048]{1,0:T(8,128)(2,1)S(1)} %pad_maximum_fusion.4), channel_id=1, source_target_pairs={{0,4},{1,5},{2,6},{3,7},{4,0},{5,1},{6,2},{7,3},{8,12},{9,13},{10,... | collective-permute-start | bytes 1179656 | tf_op jit(solution)/shard_map/ppermute | solution.py:49
  154.1 17.9 %collective-permute-start.36 = (bf16[96,2176]{1,0:T(8,128)(2,1)S(1)}, bf16[96,2176]{1,0:T(8,128)(2,1)S(1)}, u32[]{:S(2)}, u32[]{:S(2)}) collective-permute-start(bf16[96,2176]{1,0:T(8,128)(2,1)S(1)} %pad_maximum_fusion.2), channel_id=1, source_target_pairs={{0,4},{1,5},{2,6},{3,7},{4,0},{5,1},{6,2},{7,3},{8,12},{9,13},{10,... | collective-permute-start | bytes 1253384 | tf_op jit(solution)/shard_map/ppermute | solution.py:49
  155.2 16.9 %collective-permute-start.34 = (bf16[96,2176]{1,0:T(8,128)(2,1)S(1)}, bf16[96,2176]{1,0:T(8,128)(2,1)S(1)}, u32[]{:S(2)}, u32[]{:S(2)}) collective-permute-start(bf16[96,2176]{1,0:T(8,128)(2,1)S(1)} %pad_maximum_fusion.1), channel_id=1, source_target_pairs={{0,2},{1,3},{2,0},{3,1},{4,6},{5,7},{6,4},{7,5},{8,10},{9,11},{10,... | collective-permute-start | bytes 1253384 | tf_op jit(solution)/shard_map/ppermute | solution.py:49
  162.6 7.8 %collective-permute-start.29 = (bf16[24,2048]{1,0:T(8,128)(2,1)S(1)}, bf16[24,2048]{1,0:T(8,128)(2,1)S(1)}, u32[]{:S(2)}, u32[]{:S(2)}) collective-permute-start(bf16[24,2048]{1,0:T(8,128)(2,1)S(1)} %get-tuple-element.86), channel_id=1, source_target_pairs={{0,8},{1,9},{2,10},{3,11},{4,12},{5,13},{6,14},{7,15},{8,0},{9,1},... | collective-permute-start | bytes 294920 | tf_op jit(solution)/shard_map/ppermute | solution.py:49
  172.3 7.9 %collective-permute-start.37 = (bf16[24,2176]{1,0:T(8,128)(2,1)S(1)}, bf16[24,2176]{1,0:T(8,128)(2,1)S(1)}, u32[]{:S(2)}, u32[]{:S(2)}) collective-permute-start(bf16[24,2176]{1,0:T(8,128)(2,1)S(1)} %get-tuple-element.83), channel_id=1, source_target_pairs={{0,8},{1,9},{2,10},{3,11},{4,12},{5,13},{6,14},{7,15},{8,0},{9,1},... | collective-permute-start | bytes 313352 | tf_op jit(solution)/shard_map/ppermute | solution.py:49
  (23 other events, 154.7 us)

commit v3 on v2

--- a/solution.py
+++ b/solution.py
@@ -387,13 +387,15 @@
     return x, ahead
 
 
-def pick_back_kernel(sizes, picks, blocks, ranges, tokens, slot_ref, slot_col, gain_ref, *refs):
+def pick_back_kernel(sizes, picks, blocks, ranges, tokens, slot_ref, slot_col, gain_ref, expert_ref, *refs):
     count = len(sizes)
     pieces, (down_any, gate_any, up_any), refs = refs[:count], refs[count : count + 3], refs[count + 3 :]
     *refs, held, place, rows_ref, piece_sems, x_sems, downs, gates, ups, d_gate, d_up, sems, token_sems = refs
-    *parts, g_out, d_gate_ref, d_up_ref, route_ref, own_ref, other_ref = refs
+    *parts, g_out, route_ref, own_0, other_0, own_1, other_1 = refs
     step = pl.program_id(0)
     width, token_width = downs.shape[1], gates.shape[1]
+    slots = gates.shape[0]
+    base = picks + blocks
 
     def weights(at):
         source = down_any.at[pl.ds(pl.multiple_of(at * width, LANES), width), :]
@@ -401,9 +403,10 @@
 
     def token_weights(at):
         source = pl.ds(pl.multiple_of(at * token_width, LANES), token_width)
+        to = lax.rem(at, slots)
         return [
-            pltpu.make_async_copy(gate_any.at[source, :], gates.at[at], token_sems.at[0, at]),
-            pltpu.make_async_copy(up_any.at[source, :], ups.at[at], token_sems.at[1, at]),
+            pltpu.make_async_copy(gate_any.at[source, :], gates.at[to], token_sems.at[0, to]),
+            pltpu.make_async_copy(up_any.at[source, :], ups.at[to], token_sems.at[1, to]),
         ]
 
     def start_weights(at):
@@ -435,23 +438,36 @@
             back = dot(g[...], downs[at], ((1,), (1,)))
             d_hidden = gain_ref[...] * back
             units = pl.ds(pl.multiple_of(at * width, LANES), width)
-            d_gate_ref[...] = (d_hidden * pull_ref[...].astype(f32)).astype(bf16)
-            d_up_ref[...] = (d_hidden * active_ref[...].astype(f32)).astype(bf16)
-            d_gate[:, units] = d_gate_ref[...]
-            d_up[:, units] = d_up_ref[...]
+            d_gate[:, units] = (d_hidden * pull_ref[...].astype(f32)).astype(bf16)
+            d_up[:, units] = (d_hidden * active_ref[...].astype(f32)).astype(bf16)
             route_ref[...] += jnp.sum(hidden_ref[...].astype(f32) * back, axis=1, keepdims=True)
 
-    @pl.when(step >= picks + blocks)
-    def _():
-        at = step - picks - blocks
+    @pl.when((step >= base) & (step < base + tokens))
+    def _():
+        at = step - base
         for copy in token_weights(at):
             copy.wait()
-        part = dot(d_gate[...], gates[at], ((1,), (1,)))
-        part = (part + dot(d_up[...], ups[at], ((1,), (1,)))).astype(bf16)
-        spread_rows(slot_col, part, (own_ref, other_ref))
-
-
-def pick_back(slot, pieces, gain, w_down, w_gate, w_up, parts, high):
+        to = lax.rem(at, slots)
+        part = dot(d_gate[...], gates[to], ((1,), (1,)))
+        part = (part + dot(d_up[...], ups[to], ((1,), (1,)))).astype(bf16)
+
+        @pl.when(at < tokens // 2)
+        def _():
+            spread_rows(slot_col, part, (own_0, other_0))
+
+        @pl.when(at >= tokens // 2)
+        def _():
+            spread_rows(slot_col, part, (own_1, other_1))
+
+    @pl.when(step == base + tokens)
+    def _():
+        route = route_ref[...].astype(bf16).astype(f32)
+        lanes = lax.broadcasted_iota(jnp.int32, (route.shape[0], LANES), 1)
+        columns = jnp.where(lanes == expert_ref[...], route, 0.0).astype(bf16)
+        spread_rows(slot_col, columns, (own_1, other_1))
+
+
+def pick_back(slot, pieces, gain, expert, w_down, w_gate, w_up, parts):
     sizes = [piece.shape[0] for piece in pieces]
     total = sum(sizes)
     rows = gain.shape[0]
@@ -462,39 +478,37 @@
     ends = [sum(part[0].shape[1] for part in parts[: k + 1]) // block for k in range(len(parts))]
     ranges = list(zip([0] + ends[:-1], ends))
     token_block = tile(cols, 512)
-    tokens = high // token_block
-    unit = pl.BlockSpec((rows, block), lambda i: (0, jnp.clip(i - picks, 0, blocks - 1)))
-    dense = pl.BlockSpec((total // 2, token_block), lambda i: (0, jnp.maximum(i - picks - blocks, 0)))
+    tokens = cols // token_block
+    half = tokens // 2
+    base = picks + blocks
+    dense_0 = pl.BlockSpec((total // 2, token_block), lambda i: (0, jnp.clip(i - base, 0, half - 1)))
+    dense_1 = pl.BlockSpec((total // 2, token_block), lambda i: (0, jnp.maximum(i - base - half, 0)))
 
     def unit_of(part):
         return pl.BlockSpec((rows, block), lambda i: (0, jnp.clip(i - picks - part[0], 0, part[1] - part[0] - 1)))
 
-    shape = jax.ShapeDtypeStruct((rows, units), bf16)
     return call(
         functools.partial(pick_back_kernel, sizes, picks, blocks, ranges, tokens),
-        2 * rows * (cols * units + total * cols + 2 * high * units + total * high),
-        2 * cols * units + 4 * high * units + 2 * (rows + total) * cols,
-        grid=(picks + blocks + tokens,),
-        in_specs=[whole(1, total), whole(total, 1), whole(rows, 1)]
+        2 * rows * (3 * cols * units + 2 * total * cols),
+        6 * cols * units + 2 * (rows + 2 * total) * cols,
+        grid=(base + tokens + 1,),
+        in_specs=[whole(1, total), whole(total, 1), whole(rows, 1), whole(1, 1)]
         + [ANY] * (len(sizes) + 3)
         + [unit_of(part) for part in ranges for _ in range(3)],
-        out_specs=[ANY, unit, unit, whole(rows, 1), dense, dense],
-        out_shape=[
-            jax.ShapeDtypeStruct((rows, cols), bf16),
-            shape,
-            shape,
-            jax.ShapeDtypeStruct((rows, 1), f32),
-        ]
-        + [jax.ShapeDtypeStruct((total // 2, high), bf16)] * 2,
+        out_specs=[ANY, whole(rows, 1), dense_0, dense_0, dense_1, dense_1],
+        out_shape=[jax.ShapeDtypeStruct((rows, cols), bf16), jax.ShapeDtypeStruct((rows, 1), f32)]
+        + [jax.ShapeDtypeStruct((total // 2, half * token_block), bf16)] * 2
+        + [jax.ShapeDtypeStruct((total // 2, cols - half * token_block + LANES), bf16)] * 2,
         scratch_shapes=scratch
         + [pltpu.VMEM((blocks, block, cols), bf16)]
-        + [pltpu.VMEM((tokens, token_block, units), bf16)] * 2
+        + [pltpu.VMEM((picks, token_block, units), bf16)] * 2
         + [pltpu.VMEM((rows, units), bf16)] * 2
-        + [pltpu.SemaphoreType.DMA((blocks,)), pltpu.SemaphoreType.DMA((2, tokens))],
+        + [pltpu.SemaphoreType.DMA((blocks,)), pltpu.SemaphoreType.DMA((2, picks))],
     )(
         slot.reshape(1, total),
         slot.reshape(total, 1),
         gain,
+        expert.reshape(1, 1),
         *pieces,
         w_down,
         w_gate,
@@ -610,7 +624,7 @@
     all_ids = all_meta[:, :top_count].astype(jnp.int32)
     all_weights = all_meta[:, top_count : 2 * top_count].astype(f32)
     first = me * local_experts
-    fused = narrow_count == 1 and local_experts == 1
+    fused = narrow_count == 1 and local_experts == 1 and experts_all <= LANES
     chunks = CHUNKS if fused else 1
     units = w_gate.shape[2]
     ahead_units = units * 2 // 3 if fused and units % (6 * LANES) == 0 else units
@@ -647,39 +661,39 @@
         slot, place, row_gain, x, ahead = picked[j]
         straight = [(hidden, active, pull) for hidden, _, active, pull in ahead]
         if fused:
-            g, d_gate, d_up, route, *dense = pick_back(
-                slot, pieces_g, row_gain, w_down[j], w_gate[j], w_up[j], straight, w_gate.shape[1] // chunks
+            g, _, *dense = pick_back(
+                slot, pieces_g, row_gain, first + j, w_down[j], w_gate[j], w_up[j], straight
             )
-        else:
-            g = pick_rows(slot, pieces_g, rows, cols)
-            g = lax.all_gather(g, "narrow", axis=1, tiled=True)
-            d_gate, d_up, route = back_project(g, row_gain, w_down[j], straight)
+            ends.append(([part[1] for part in ahead], g, row_gain))
+            continue
+        g = pick_rows(slot, pieces_g, rows, cols)
+        g = lax.all_gather(g, "narrow", axis=1, tiled=True)
+        d_gate, d_up, route = back_project(g, row_gain, w_down[j], straight)
         route = lax.psum(route.astype(bf16).astype(f32), "narrow")
         at = jnp.arange(expert_cols, dtype=jnp.int32) == first + j
         route = jnp.where(at[None, :], route, 0.0).astype(bf16)
         ends.append(([part[1] for part in ahead], g, row_gain))
-        if fused:
-            continue
         (part,) = token_grad(d_gate, d_up, slot, route, w_gate[j], w_up[j], 0, 1, False)
         part = lax.psum_scatter(part, "narrow", scatter_dimension=1, tiled=True)
         part = jnp.concatenate([part, route], axis=1)
         part = dot(place.astype(bf16), part, ((0,), (0,)))
         dense = [dense[0] + part[: total // 2], dense[1] + part[total // 2 :]]
-    mine = [add(dense[0].astype(bf16), flip(dense[1].astype(bf16), CORE))]
-    if fused and chunks == 2:
-        own, other = token_grad(after(d_gate, dense[0]), d_up, slot, route, w_gate[0], w_up[0], 1, chunks, True)
-        mine[0] = add(after(dense[0], own), flip(dense[1], CORE))
-        mine.append(add(own, flip(other, CORE)))
-    sides = [scatter_far(rows_) for rows_ in mine]
-    firsts = [scatter_sides(*side) for side in sides]
-    shares = [scatter_z(first_) for first_ in firsts]
-    gates = [mine[0], sides[0][1], firsts[0], firsts[-1]] if fused else [mine[0]]
     grad_downs = []
-    for turned, g, row_gain in ends:
-        out = None
-        for k, gate in enumerate(gates):
-            out = down_grad(turned, after(g, gate), row_gain, k, len(gates), out)
+    if fused:
+        (turned, g, row_gain), = ends
+        out = down_grad(turned, g, row_gain, 0, 4, None)
+        dense[0], out = lax.optimization_barrier((dense[0], out))
+        mine = [add(dense[k], flip(dense[k + 1], CORE)) for k in (0, 2)]
+        sides = [scatter_far(rows_) for rows_ in mine]
+        firsts = [scatter_sides(*side) for side in sides]
+        shares = [scatter_z(first_) for first_ in firsts]
+        for k, gate in enumerate([sides[1][1], *firsts]):
+            out = down_grad(turned, after(g, gate), row_gain, k + 1, 4, out)
         grad_downs.append(out)
+    else:
+        mine = add(dense[0].astype(bf16), flip(dense[1].astype(bf16), CORE))
+        shares = [scatter_z(scatter_sides(*scatter_far(mine)))]
+        grad_downs += [down_grad(*end, 0, 1, None) for end in ends]
     joined = jnp.concatenate(shares, axis=1)
     width = tokens.shape[1]
     by_expert = joined[:, width : width + experts_all].astype(f32)

time: 184 us -> 183 us (level)
    pallas_call x1 -> x0, Pallas kernels: 11.4 us -> none  [token_grad(): call(functools.partial(token_kernel, steps, spread), 4 * rows * width * u...]
    pallas_call x1, Pallas kernels: 24.4 us -> 34.8 us  [pick_back(): call(functools.partial(pick_back_kernel, sizes, picks, blocks, ranges, to...]
    unnamed x37 -> x35, local copies, waits for them, and re-layouts: 7.03 us -> 7.27 us
  transfers between devices with their start and end apart: 40 -> 40, of which waited for: 15 -> 19; matrix products, arithmetic and copies ran while one was open for 6% -> 6% of each run, Pallas kernels for 28% -> 22%
where the time goes in v3:
time: 183 us
  Pallas kernels  75.4 us (41%)
  waiting for transfers between devices  50.5 us (28%)
  starting transfers between devices  37.9 us (21%)
  local copies, waits for them, and re-layouts  11.6 us (6%)
  other arithmetic  6.23 us (3%)
    ppermute x40, waiting for transfers between devices, flip(): return lax.ppermute(value, 'wide', [(i, i ^ mask) for i in range(count)])  50.5 us
    ppermute x40, starting transfers between devices, flip(): return lax.ppermute(value, 'wide', [(i, i ^ mask) for i in range(count)])  37.9 us
    pallas_call x1, Pallas kernels, pick_back(): call(functools.partial(pick_back_kernel, sizes, picks, blocks, ranges, to...  34.8 us
    pallas_call x4, Pallas kernels, down_grad(): call(functools.partial(down_kernel, len(turned)), 2 * rows * width * unit...  17.3 us
    pallas_call x1, Pallas kernels, pick_forward(): call(functools.partial(pick_forward_kernel, sizes, picks, blocks), 4 * ro...  15.2 us
    unnamed x35, local copies, waits for them, and re-layouts  7.27 us
    pallas_call x1, Pallas kernels, forward(): call(forward_kernel, 4 * rows * width * units, 4 * width * units, grid=(u...  7.16 us
  transfers between devices with their start and end apart: 40, of which 19 were waited for; matrix products, arithmetic and copies ran while one was open for 6% of the time, Pallas kernels for 22%

profile of v3, /device:TPU:0, one launch (start us, length us, event | category | flops | bytes accessed | tf_op | source)
XLA Modules:
  0.0 182.7 jit_solution(10953726239071883109)
XLA Ops:
  3.2 5.1 %collective-permute-start.2 = (bf16[24,4224]{1,0:T(8,128)(2,1)S(1)}, bf16[24,4224]{1,0:T(8,128)(2,1)S(1)}, u32[]{:S(2)}, u32[]{:S(2)}) collective-permute-start(bf16[24,4224]{1,0:T(8,128)(2,1)S(1)} %concatenate.24), channel_id=1, source_target_pairs={{0,24},{1,25},{2,26},{3,27},{4,28},{5,29},{6,30},{7,31},{8,16},{9,... | collective-permute-start | bytes 608264 | tf_op jit(solution)/shard_map/ppermute | solution.py:49
  8.9 5.4 %collective-permute-done.2 = bf16[24,4224]{1,0:T(8,128)(2,1)S(1)} collective-permute-done((bf16[24,4224]{1,0:T(8,128)(2,1)S(1)}, bf16[24,4224]{1,0:T(8,128)(2,1)S(1)}, u32[]{:S(2)}, u32[]{:S(2)}) %collective-permute-start.2) | collective-permute-done | bytes 202784 | tf_op jit(solution)/shard_map/ppermute | solution.py:49
  14.3 11.2 %collective-permute-done.1 = bf16[24,4224]{1,0:T(8,128)(2,1)S(1)} collective-permute-done((bf16[24,4224]{1,0:T(8,128)(2,1)S(1)}, bf16[24,4224]{1,0:T(8,128)(2,1)S(1)}, u32[]{:S(2)}, u32[]{:S(2)}) %collective-permute-start.1) | collective-permute-done | bytes 202784 | tf_op jit(solution)/shard_map/ppermute | solution.py:49
  25.6 2.5 %collective-permute-start.14 = (bf16[24,4096]{1,0:T(8,128)(2,1)}, bf16[24,4096]{1,0:T(8,128)(2,1)S(1)}, u32[]{:S(2)}, u32[]{:S(2)}) collective-permute-start(bf16[24,4096]{1,0:T(8,128)(2,1)} %param.8), channel_id=1, source_target_pairs={{0,24},{1,25},{2,26},{3,27},{4,28},{5,29},{6,30},{7,31},{8,16},{9,... | collective-permute-start | bytes 589832 | tf_op jit(solution)/shard_map/ppermute | solution.py:49
  28.1 1.9 %collective-permute-start.12 = (bf16[24,4096]{1,0:T(8,128)(2,1)}, bf16[24,4096]{1,0:T(8,128)(2,1)S(1)}, u32[]{:S(2)}, u32[]{:S(2)}) collective-permute-start(bf16[24,4096]{1,0:T(8,128)(2,1)} %param.8), channel_id=1, source_target_pairs={{0,8},{1,9},{2,10},{3,11},{4,12},{5,13},{6,14},{7,15},{8,0},{9,1},... | collective-permute-start | bytes 589832 | tf_op jit(solution)/shard_map/ppermute | solution.py:49
  30.0 1.5 collective-permute-start.4
  31.6 1.5 collective-permute-start.3
  33.1 1.6 constant_dynamic-update-slice_fusion.3
  34.7 5.6 %collective-permute-done.12 = bf16[24,4096]{1,0:T(8,128)(2,1)S(1)} collective-permute-done((bf16[24,4096]{1,0:T(8,128)(2,1)}, bf16[24,4096]{1,0:T(8,128)(2,1)S(1)}, u32[]{:S(2)}, u32[]{:S(2)}) %collective-permute-start.12) | collective-permute-done | bytes 196640 | tf_op jit(solution)/shard_map/ppermute | solution.py:49
  40.9 7.4 %collective-permute-done.4.refs_2_ = bf16[96,4224]{1,0:T(8,128)(2,1)S(1)} collective-permute-done((bf16[96,4224]{1,0:T(8,128)(2,1)S(1)}, bf16[96,4224]{1,0:T(8,128)(2,1)S(1)}, u32[]{:S(2)}, u32[]{:S(2)}) %collective-permute-start.4) | collective-permute-done | bytes 811040 | tf_op jit(solution)/shard_map/ppermute | solution.py:49
  48.4 1.6 collective-permute-start.5
  52.8 5.5 %collective-permute-done.5.refs_3_ = bf16[48,4224]{1,0:T(8,128)(2,1)S(1)} collective-permute-done((bf16[48,4224]{1,0:T(8,128)(2,1)S(1)}, bf16[48,4224]{1,0:T(8,128)(2,1)S(1)}, u32[]{:S(2)}, u32[]{:S(2)}) %collective-permute-start.5) | collective-permute-done | bytes 405536 | tf_op jit(solution)/shard_map/ppermute | solution.py:49
  59.9 1.3 collective-permute-start.16
  63.8 15.2 %shard_map.95 = (bf16[384,4096]{1,0:T(8,128)(2,1)}, bf16[384,1024]{1,0:T(8,128)(2,1)}, bf16[1024,384]{1,0:T(8,128)(2,1)}, bf16[384,1024]{1,0:T(8,128)(2,1)}, bf16[384,1024]{1,0:T(8,128)(2,1)}) custom-call(s32[1,768]{1,0:T(1,128)S(1)} %get-tuple-element.61.slot_ref, bf16[96,4224]{1,0:T(8,128)(2,1)} %copy-done.4, bf16[96,4224]{1,0:T(8,128)(2,1)} %copy-done.6, ...), custom_call_target="tpu_custom_call" | custom-call | flops 8858370048 | bytes 26214400 | tf_op jit(solution)/shard_map/pallas_call | solution.py:369
  83.6 1.5 collective-permute-start.18
  85.7 7.2 %shard_map.96 = (bf16[384,512]{1,0:T(8,128)(2,1)S(1)}, bf16[512,384]{1,0:T(8,128)(2,1)S(1)}, bf16[384,512]{1,0:T(8,128)(2,1)S(1)}, bf16[384,512]{1,0:T(8,128)(2,1)S(1)}) custom-call(bf16[384,4096]{1,0:T(8,128)(2,1)} %get-tuple-element.35.x_ref, bf16[4096,1536]{1,0:T(8,128)(2,1)} %bitcast.22, bf16[4096,1536]{1,0:T(8,128)(2,1)} %bitcast.25), custom_call_target="tpu_custom_call" | custom-call | flops 3221225472 | bytes 8388608 | tf_op jit(solution)/shard_map/pallas_call | solution.py:203
  97.5 34.8 %shard_map.97 = (bf16[384,4096]{1,0:T(8,128)(2,1)}, f32[384,1]{1,0:T(8,128)}, bf16[384,2048]{1,0:T(8,128)(2,1)}, bf16[384,2048]{1,0:T(8,128)(2,1)}, bf16[384,217...) custom-call(s32[1,768]{1,0:T(1,128)S(1)} %get-tuple-element.61.slot_ref, s32[768,1]{1,0:T(8,128)S(1)} %bitcast_select_fusion.slot_col, ...), custom_call_target="tpu_custom_call" | custom-call | flops 19327352832 | bytes 53477376 | tf_op jit(solution)/shard_map/pallas_call | solution.py:490
  132.9 4.4 %shard_map.98.refs_2_ = bf16[1536,4096]{1,0:T(8,128)(2,1)} custom-call(bf16[384,4096]{1,0:T(8,128)(2,1)} %get-tuple-element.53.g_ref, f32[384,1]{1,0:T(8,128)S(1)} %broadcast_in_dim.49.gain_ref, bf16[1024,384]{1,0:T(8,128)(2,1)S(1)} %copy-done, bf16[512,384]{1,0:T(8,128)(2,1)S(1)} %get-tuple-element.46.refs_1_), custom_call_target="tpu_custom_call" | custom-call | flops 1207959552 | bytes 3145728 | tf_op jit(solution)/shard_map/pallas_call | solution.py:588
  137.3 2.2 %add_convert_fusion.1 = bf16[384,2048]{1,0:T(8,128)(2,1)S(1)} fusion(bf16[384,2048]{1,0:T(8,128)(2,1)} %collective-permute-done.24, bf16[384,2048]{1,0:T(8,128)(2,1)S(1)} %copy-done.8), kind=kLoop, calls=%fused_computation.1 | loop fusion | flops 3145728 | bytes 4718592 | tf_op jit(solution)/shard_map/convert_element_type | solution.py:23
  142.7 1.5 collective-permute-start.33
  144.3 3.2 %collective-permute-done.27 = bf16[48,2048]{1,0:T(8,128)(2,1)S(1)} collective-permute-done((bf16[48,2048]{1,0:T(8,128)(2,1)S(1)}, bf16[48,2048]{1,0:T(8,128)(2,1)S(1)}, u32[]{:S(2)}, u32[]{:S(2)}) %collective-permute-start.27) | collective-permute-done | bytes 196640 | tf_op jit(solution)/shard_map/ppermute | solution.py:49
  148.2 1.3 collective-permute-start.28
  150.3 1.6 collective-permute-done.35
  152.6 1.6 collective-permute-start.34
  154.8 4.3 %shard_map.99.refs_2_ = bf16[1536,4096]{1,0:T(8,128)(2,1)} custom-call(bf16[384,4096]{1,0:T(8,128)(2,1)} %get-tuple-element.53.g_ref, f32[384,1]{1,0:T(8,128)S(1)} %broadcast_in_dim.49.gain_ref, bf16[1024,384]{1,0:T(8,128)(2,1)S(1)} %copy-done, bf16[512,384]{1,0:T(8,128)(2,1)S(1)} %get-tuple-element.46.refs_1_, ...), custom_call_target="tpu_custom_call", output_to_operand_aliasing={{}: (4, {})} | custom-call | flops 1207959552 | bytes 3145728 | tf_op jit(solution)/shard_map/pallas_call | solution.py:588
  159.1 1.8 collective-permute-done.28
  162.3 2.2 %collective-permute-start.31 = (bf16[24,2048]{1,0:T(8,128)(2,1)S(1)}, bf16[24,2048]{1,0:T(8,128)(2,1)S(1)}, u32[]{:S(2)}, u32[]{:S(2)}) collective-permute-start(bf16[24,2048]{1,0:T(8,128)(2,1)S(1)} %get-tuple-element.79), channel_id=1, source_target_pairs={{0,24},{1,25},{2,26},{3,27},{4,28},{5,29},{6,30},{7,31},{8,16},{9,... | collective-permute-start | bytes 294920 | tf_op jit(solution)/shard_map/ppermute | solution.py:49
  165.4 4.3 %shard_map.100.refs_2_ = bf16[1536,4096]{1,0:T(8,128)(2,1)} custom-call(bf16[384,4096]{1,0:T(8,128)(2,1)} %get-tuple-element.53.g_ref, f32[384,1]{1,0:T(8,128)S(1)} %broadcast_in_dim.49.gain_ref, bf16[1024,384]{1,0:T(8,128)(2,1)S(1)} %copy-done, bf16[512,384]{1,0:T(8,128)(2,1)S(1)} %get-tuple-element.46.refs_1_, ...), custom_call_target="tpu_custom_call", output_to_operand_aliasing={{}: (4, {})} | custom-call | flops 1207959552 | bytes 3145728 | tf_op jit(solution)/shard_map/pallas_call | solution.py:588
  169.7 1.6 collective-permute-done.30
  171.6 2.5 %collective-permute-start.39 = (bf16[24,2176]{1,0:T(8,128)(2,1)S(1)}, bf16[24,2176]{1,0:T(8,128)(2,1)S(1)}, u32[]{:S(2)}, u32[]{:S(2)}) collective-permute-start(bf16[24,2176]{1,0:T(8,128)(2,1)S(1)} %get-tuple-element.76), channel_id=1, source_target_pairs={{0,24},{1,25},{2,26},{3,27},{4,28},{5,29},{6,30},{7,31},{8,16},{9,... | collective-permute-start | bytes 313352 | tf_op jit(solution)/shard_map/ppermute | solution.py:49
  175.1 4.3 %shard_map.101 = bf16[1536,4096]{1,0:T(8,128)(2,1)} custom-call(bf16[384,4096]{1,0:T(8,128)(2,1)} %get-tuple-element.53.g_ref, f32[384,1]{1,0:T(8,128)S(1)} %broadcast_in_dim.49.gain_ref, bf16[1024,384]{1,0:T(8,128)(2,1)S(1)} %copy-done, bf16[512,384]{1,0:T(8,128)(2,1)S(1)} %get-tuple-element.46.refs_1_, ...), custom_call_target="tpu_custom_call", output_to_operand_aliasing={{}: (4, {})} | custom-call | flops 1207959552 | bytes 3145728 | tf_op jit(solution)/shard_map/pallas_call | solution.py:588
  179.4 1.7 collective-permute-done.38
  (133 shorter events, 32.5 us)
Async XLA Ops:
  3.2 11.1 %collective-permute-start.2 = (bf16[24,4224]{1,0:T(8,128)(2,1)S(1)}, bf16[24,4224]{1,0:T(8,128)(2,1)S(1)}, u32[]{:S(2)}, u32[]{:S(2)}) collective-permute-start(bf16[24,4224]{1,0:T(8,128)(2,1)S(1)} %concatenate.24), channel_id=1, source_target_pairs={{0,24},{1,25},{2,26},{3,27},{4,28},{5,29},{6,30},{7,31},{8,16},{9,... | collective-permute-start | bytes 608264 | tf_op jit(solution)/shard_map/ppermute | solution.py:49
  8.3 17.2 %collective-permute-start.1 = (bf16[24,4224]{1,0:T(8,128)(2,1)S(1)}, bf16[24,4224]{1,0:T(8,128)(2,1)S(1)}, u32[]{:S(2)}, u32[]{:S(2)}) collective-permute-start(bf16[24,4224]{1,0:T(8,128)(2,1)S(1)} %concatenate.24), channel_id=1, source_target_pairs={{0,16},{1,17},{2,18},{3,19},{4,20},{5,21},{6,22},{7,23},{8,24},{9,... | collective-permute-start | bytes 608264 | tf_op jit(solution)/shard_map/ppermute | solution.py:49
  8.3 17.2 %collective-permute-start = (bf16[24,4224]{1,0:T(8,128)(2,1)S(1)}, bf16[24,4224]{1,0:T(8,128)(2,1)S(1)}, u32[]{:S(2)}, u32[]{:S(2)}) collective-permute-start(bf16[24,4224]{1,0:T(8,128)(2,1)S(1)} %concatenate.24), channel_id=1, source_target_pairs={{0,8},{1,9},{2,10},{3,11},{4,12},{5,13},{6,14},{7,15},{8,0},{9,1},... | collective-permute-start | bytes 608264 | tf_op jit(solution)/shard_map/ppermute | solution.py:49
  25.6 26.0 %collective-permute-start.14 = (bf16[24,4096]{1,0:T(8,128)(2,1)}, bf16[24,4096]{1,0:T(8,128)(2,1)S(1)}, u32[]{:S(2)}, u32[]{:S(2)}) collective-permute-start(bf16[24,4096]{1,0:T(8,128)(2,1)} %param.8), channel_id=1, source_target_pairs={{0,24},{1,25},{2,26},{3,27},{4,28},{5,29},{6,30},{7,31},{8,16},{9,... | collective-permute-start | bytes 589832 | tf_op jit(solution)/shard_map/ppermute | solution.py:49
  28.1 23.4 %collective-permute-start.13 = (bf16[24,4096]{1,0:T(8,128)(2,1)}, bf16[24,4096]{1,0:T(8,128)(2,1)S(1)}, u32[]{:S(2)}, u32[]{:S(2)}) collective-permute-start(bf16[24,4096]{1,0:T(8,128)(2,1)} %param.8), channel_id=1, source_target_pairs={{0,16},{1,17},{2,18},{3,19},{4,20},{5,21},{6,22},{7,23},{8,24},{9,... | collective-permute-start | bytes 589832 | tf_op jit(solution)/shard_map/ppermute | solution.py:49
  28.1 12.1 %collective-permute-start.12 = (bf16[24,4096]{1,0:T(8,128)(2,1)}, bf16[24,4096]{1,0:T(8,128)(2,1)S(1)}, u32[]{:S(2)}, u32[]{:S(2)}) collective-permute-start(bf16[24,4096]{1,0:T(8,128)(2,1)} %param.8), channel_id=1, source_target_pairs={{0,8},{1,9},{2,10},{3,11},{4,12},{5,13},{6,14},{7,15},{8,0},{9,1},... | collective-permute-start | bytes 589832 | tf_op jit(solution)/shard_map/ppermute | solution.py:49
  30.0 18.3 %collective-permute-start.4 = (bf16[96,4224]{1,0:T(8,128)(2,1)S(1)}, bf16[96,4224]{1,0:T(8,128)(2,1)S(1)}, u32[]{:S(2)}, u32[]{:S(2)}) collective-permute-start(bf16[96,4224]{1,0:T(8,128)(2,1)S(1)} %pad_maximum_fusion.refs_0_), channel_id=1, source_target_pairs={{0,4},{1,5},{2,6},{3,7},{4,0},{5,1},{6,2},{7,3},{8,12},{9,13},{10,... | collective-permute-start | bytes 2433032 | tf_op jit(solution)/shard_map/ppermute | solution.py:49
  31.6 19.1 %collective-permute-start.3 = (bf16[96,4224]{1,0:T(8,128)(2,1)S(1)}, bf16[96,4224]{1,0:T(8,128)(2,1)S(1)}, u32[]{:S(2)}, u32[]{:S(2)}) collective-permute-start(bf16[96,4224]{1,0:T(8,128)(2,1)S(1)} %pad_maximum_fusion.refs_0_), channel_id=1, source_target_pairs={{0,2},{1,3},{2,0},{3,1},{4,6},{5,7},{6,4},{7,5},{8,10},{9,11},{10,... | collective-permute-start | bytes 2433032 | tf_op jit(solution)/shard_map/ppermute | solution.py:49
  40.2 19.2 %collective-permute-start.7 = (bf16[96,4224]{1,0:T(8,128)(2,1)S(1)}, bf16[96,4224]{1,0:T(8,128)(2,1)S(1)}, u32[]{:S(2)}, u32[]{:S(2)}) collective-permute-start(bf16[96,4224]{1,0:T(8,128)(2,1)S(1)} %pad_maximum_fusion.refs_0_), channel_id=1, source_target_pairs={{0,1},{1,0},{2,3},{3,2},{4,5},{5,4},{6,7},{7,6},{8,9},{9,8},{10,11... | collective-permute-start | bytes 2433032 | tf_op jit(solution)/shard_map/ppermute | solution.py:49
  48.4 9.9 %collective-permute-start.5 = (bf16[48,4224]{1,0:T(8,128)(2,1)S(1)}, bf16[48,4224]{1,0:T(8,128)(2,1)S(1)}, u32[]{:S(2)}, u32[]{:S(2)}) collective-permute-start(bf16[48,4224]{1,0:T(8,128)(2,1)S(1)} %slice.147), channel_id=1, source_target_pairs={{0,2},{1,3},{2,0},{3,1},{4,6},{5,7},{6,4},{7,5},{8,10},{9,11},{10,... | collective-permute-start | bytes 1216520 | tf_op jit(solution)/shard_map/ppermute | solution.py:49
  50.7 8.0 %collective-permute-start.6 = (bf16[48,4224]{1,0:T(8,128)(2,1)S(1)}, bf16[48,4224]{1,0:T(8,128)(2,1)S(1)}, u32[]{:S(2)}, u32[]{:S(2)}) collective-permute-start(bf16[48,4224]{1,0:T(8,128)(2,1)S(1)} %slice.148), channel_id=1, source_target_pairs={{0,4},{1,5},{2,6},{3,7},{4,0},{5,1},{6,2},{7,3},{8,12},{9,13},{10,... | collective-permute-start | bytes 1216520 | tf_op jit(solution)/shard_map/ppermute | solution.py:49
  51.5 8.3 %collective-permute-start.9 = (bf16[96,4224]{1,0:T(8,128)(2,1)S(1)}, bf16[96,4224]{1,0:T(8,128)(2,1)S(1)}, u32[]{:S(2)}, u32[]{:S(2)}) collective-permute-start(bf16[96,4224]{1,0:T(8,128)(2,1)S(1)} %collective-permute-done.4.refs_2_), channel_id=1, source_target_pairs={{0,1},{1,0},{2,3},{3,2},{4,5},{5,4},{6,7},{7,6},{8,9},{9,8},{10,11... | collective-permute-start | bytes 2433032 | tf_op jit(solution)/shard_map/ppermute | solution.py:49
  51.5 9.6 %collective-permute-start.8 = (bf16[96,4224]{1,0:T(8,128)(2,1)S(1)}, bf16[96,4224]{1,0:T(8,128)(2,1)S(1)}, u32[]{:S(2)}, u32[]{:S(2)}) collective-permute-start(bf16[96,4224]{1,0:T(8,128)(2,1)S(1)} %collective-permute-done.3.refs_1_), channel_id=1, source_target_pairs={{0,1},{1,0},{2,3},{3,2},{4,5},{5,4},{6,7},{7,6},{8,9},{9,8},{10,11... | collective-permute-start | bytes 2433032 | tf_op jit(solution)/shard_map/ppermute | solution.py:49
  59.5 36.4 %collective-permute-start.19 = (bf16[96,4096]{1,0:T(8,128)(2,1)}, bf16[96,4096]{1,0:T(8,128)(2,1)}, u32[]{:S(2)}, u32[]{:S(2)}) collective-permute-start(bf16[96,4096]{1,0:T(8,128)(2,1)} %constant_dynamic-update-slice_fusion.refs_0_), channel_id=1, source_target_pairs={{0,1},{1,0},{2,3},{3,2},{4,5},{5,4},{6,7},{7,6},{8,9},{9,8},{10,11... | collective-permute-start | bytes 2359304 | tf_op jit(solution)/shard_map/ppermute | solution.py:49
  59.9 19.9 %collective-permute-start.16 = (bf16[96,4096]{1,0:T(8,128)(2,1)}, bf16[96,4096]{1,0:T(8,128)(2,1)}, u32[]{:S(2)}, u32[]{:S(2)}) collective-permute-start(bf16[96,4096]{1,0:T(8,128)(2,1)} %constant_dynamic-update-slice_fusion.refs_0_), channel_id=1, source_target_pairs={{0,4},{1,5},{2,6},{3,7},{4,0},{5,1},{6,2},{7,3},{8,12},{9,13},{10,... | collective-permute-start | bytes 2359304 | tf_op jit(solution)/shard_map/ppermute | solution.py:49
  61.1 19.6 %collective-permute-start.15 = (bf16[96,4096]{1,0:T(8,128)(2,1)}, bf16[96,4096]{1,0:T(8,128)(2,1)}, u32[]{:S(2)}, u32[]{:S(2)}) collective-permute-start(bf16[96,4096]{1,0:T(8,128)(2,1)} %constant_dynamic-update-slice_fusion.refs_0_), channel_id=1, source_target_pairs={{0,2},{1,3},{2,0},{3,1},{4,6},{5,7},{6,4},{7,5},{8,10},{9,11},{10,... | collective-permute-start | bytes 2359304 | tf_op jit(solution)/shard_map/ppermute | solution.py:49
  82.8 11.6 %collective-permute-start.17 = (bf16[48,4096]{1,0:T(8,128)(2,1)S(1)}, bf16[48,4096]{1,0:T(8,128)(2,1)S(1)}, u32[]{:S(2)}, u32[]{:S(2)}) collective-permute-start(bf16[48,4096]{1,0:T(8,128)(2,1)S(1)} %slice.121), channel_id=1, source_target_pairs={{0,2},{1,3},{2,0},{3,1},{4,6},{5,7},{6,4},{7,5},{8,10},{9,11},{10,... | collective-permute-start | bytes 1179656 | tf_op jit(solution)/shard_map/ppermute | solution.py:49
  83.6 10.8 %collective-permute-start.18 = (bf16[48,4096]{1,0:T(8,128)(2,1)S(1)}, bf16[48,4096]{1,0:T(8,128)(2,1)S(1)}, u32[]{:S(2)}, u32[]{:S(2)}) collective-permute-start(bf16[48,4096]{1,0:T(8,128)(2,1)S(1)} %slice.122), channel_id=1, source_target_pairs={{0,4},{1,5},{2,6},{3,7},{4,0},{5,1},{6,2},{7,3},{8,12},{9,13},{10,... | collective-permute-start | bytes 1179656 | tf_op jit(solution)/shard_map/ppermute | solution.py:49
  85.2 11.5 %collective-permute-start.20 = (bf16[96,4096]{1,0:T(8,128)(2,1)}, bf16[96,4096]{1,0:T(8,128)(2,1)}, u32[]{:S(2)}, u32[]{:S(2)}) collective-permute-start(bf16[96,4096]{1,0:T(8,128)(2,1)} %collective-permute-done.15.refs_1_), channel_id=1, source_target_pairs={{0,1},{1,0},{2,3},{3,2},{4,5},{5,4},{6,7},{7,6},{8,9},{9,8},{10,11... | collective-permute-start | bytes 2359304 | tf_op jit(solution)/shard_map/ppermute | solution.py:49
  85.2 11.5 %collective-permute-start.21 = (bf16[96,4096]{1,0:T(8,128)(2,1)}, bf16[96,4096]{1,0:T(8,128)(2,1)}, u32[]{:S(2)}, u32[]{:S(2)}) collective-permute-start(bf16[96,4096]{1,0:T(8,128)(2,1)} %collective-permute-done.16.refs_2_), channel_id=1, source_target_pairs={{0,1},{1,0},{2,3},{3,2},{4,5},{5,4},{6,7},{7,6},{8,9},{9,8},{10,11... | collective-permute-start | bytes 2359304 | tf_op jit(solution)/shard_map/ppermute | solution.py:49
  132.5 9.0 %collective-permute-start.32 = (bf16[384,2176]{1,0:T(8,128)(2,1)}, bf16[384,2176]{1,0:T(8,128)(2,1)S(1)}, u32[]{:S(2)}, u32[]{:S(2)}) collective-permute-start(bf16[384,2176]{1,0:T(8,128)(2,1)} %get-tuple-element.50), channel_id=1, source_target_pairs={{0,1},{1,0},{2,3},{3,2},{4,5},{5,4},{6,7},{7,6},{8,9},{9,8},{10,11... | collective-permute-start | bytes 5013512 | tf_op jit(solution)/shard_map/ppermute | solution.py:49
  139.6 7.8 %collective-permute-start.27 = (bf16[48,2048]{1,0:T(8,128)(2,1)S(1)}, bf16[48,2048]{1,0:T(8,128)(2,1)S(1)}, u32[]{:S(2)}, u32[]{:S(2)}) collective-permute-start(bf16[48,2048]{1,0:T(8,128)(2,1)S(1)} %get-tuple-element.71), channel_id=1, source_target_pairs={{0,2},{1,3},{2,0},{3,1},{4,6},{5,7},{6,4},{7,5},{8,10},{9,11},{10,... | collective-permute-start | bytes 589832 | tf_op jit(solution)/shard_map/ppermute | solution.py:49
  140.2 7.8 %collective-permute-start.25 = (bf16[48,2048]{1,0:T(8,128)(2,1)S(1)}, bf16[48,2048]{1,0:T(8,128)(2,1)S(1)}, u32[]{:S(2)}, u32[]{:S(2)}) collective-permute-start(bf16[48,2048]{1,0:T(8,128)(2,1)S(1)} %get-tuple-element.72), channel_id=1, source_target_pairs={{0,4},{1,5},{2,6},{3,7},{4,0},{5,1},{6,2},{7,3},{8,12},{9,13},{10,... | collective-permute-start | bytes 589832 | tf_op jit(solution)/shard_map/ppermute | solution.py:49
  141.9 10.0 %collective-permute-start.35 = (bf16[48,2176]{1,0:T(8,128)(2,1)S(1)}, bf16[48,2176]{1,0:T(8,128)(2,1)S(1)}, u32[]{:S(2)}, u32[]{:S(2)}) collective-permute-start(bf16[48,2176]{1,0:T(8,128)(2,1)S(1)} %get-tuple-element.65), channel_id=1, source_target_pairs={{0,2},{1,3},{2,0},{3,1},{4,6},{5,7},{6,4},{7,5},{8,10},{9,11},{10,... | collective-permute-start | bytes 626696 | tf_op jit(solution)/shard_map/ppermute | solution.py:49
  142.7 9.7 %collective-permute-start.33 = (bf16[48,2176]{1,0:T(8,128)(2,1)S(1)}, bf16[48,2176]{1,0:T(8,128)(2,1)S(1)}, u32[]{:S(2)}, u32[]{:S(2)}) collective-permute-start(bf16[48,2176]{1,0:T(8,128)(2,1)S(1)} %get-tuple-element.66), channel_id=1, source_target_pairs={{0,4},{1,5},{2,6},{3,7},{4,0},{5,1},{6,2},{7,3},{8,12},{9,13},{10,... | collective-permute-start | bytes 626696 | tf_op jit(solution)/shard_map/ppermute | solution.py:49
  148.2 12.8 %collective-permute-start.28 = (bf16[96,2048]{1,0:T(8,128)(2,1)S(1)}, bf16[96,2048]{1,0:T(8,128)(2,1)S(1)}, u32[]{:S(2)}, u32[]{:S(2)}) collective-permute-start(bf16[96,2048]{1,0:T(8,128)(2,1)S(1)} %pad_maximum_fusion.4), channel_id=1, source_target_pairs={{0,4},{1,5},{2,6},{3,7},{4,0},{5,1},{6,2},{7,3},{8,12},{9,13},{10,... | collective-permute-start | bytes 1179656 | tf_op jit(solution)/shard_map/ppermute | solution.py:49
  149.5 12.1 %collective-permute-start.26 = (bf16[96,2048]{1,0:T(8,128)(2,1)S(1)}, bf16[96,2048]{1,0:T(8,128)(2,1)S(1)}, u32[]{:S(2)}, u32[]{:S(2)}) collective-permute-start(bf16[96,2048]{1,0:T(8,128)(2,1)S(1)} %pad_maximum_fusion.3), channel_id=1, source_target_pairs={{0,2},{1,3},{2,0},{3,1},{4,6},{5,7},{6,4},{7,5},{8,10},{9,11},{10,... | collective-permute-start | bytes 1179656 | tf_op jit(solution)/shard_map/ppermute | solution.py:49
  152.6 18.7 %collective-permute-start.34 = (bf16[96,2176]{1,0:T(8,128)(2,1)S(1)}, bf16[96,2176]{1,0:T(8,128)(2,1)S(1)}, u32[]{:S(2)}, u32[]{:S(2)}) collective-permute-start(bf16[96,2176]{1,0:T(8,128)(2,1)S(1)} %pad_maximum_fusion.1), channel_id=1, source_target_pairs={{0,2},{1,3},{2,0},{3,1},{4,6},{5,7},{6,4},{7,5},{8,10},{9,11},{10,... | collective-permute-start | bytes 1253384 | tf_op jit(solution)/shard_map/ppermute | solution.py:49
  154.2 17.1 %collective-permute-start.36 = (bf16[96,2176]{1,0:T(8,128)(2,1)S(1)}, bf16[96,2176]{1,0:T(8,128)(2,1)S(1)}, u32[]{:S(2)}, u32[]{:S(2)}) collective-permute-start(bf16[96,2176]{1,0:T(8,128)(2,1)S(1)} %pad_maximum_fusion.2), channel_id=1, source_target_pairs={{0,4},{1,5},{2,6},{3,7},{4,0},{5,1},{6,2},{7,3},{8,12},{9,13},{10,... | collective-permute-start | bytes 1253384 | tf_op jit(solution)/shard_map/ppermute | solution.py:49
  161.8 7.9 %collective-permute-start.29 = (bf16[24,2048]{1,0:T(8,128)(2,1)S(1)}, bf16[24,2048]{1,0:T(8,128)(2,1)S(1)}, u32[]{:S(2)}, u32[]{:S(2)}) collective-permute-start(bf16[24,2048]{1,0:T(8,128)(2,1)S(1)} %get-tuple-element.78), channel_id=1, source_target_pairs={{0,8},{1,9},{2,10},{3,11},{4,12},{5,13},{6,14},{7,15},{8,0},{9,1},... | collective-permute-start | bytes 294920 | tf_op jit(solution)/shard_map/ppermute | solution.py:49
  171.6 7.9 %collective-permute-start.37 = (bf16[24,2176]{1,0:T(8,128)(2,1)S(1)}, bf16[24,2176]{1,0:T(8,128)(2,1)S(1)}, u32[]{:S(2)}, u32[]{:S(2)}) collective-permute-start(bf16[24,2176]{1,0:T(8,128)(2,1)S(1)} %get-tuple-element.75), channel_id=1, source_target_pairs={{0,8},{1,9},{2,10},{3,11},{4,12},{5,13},{6,14},{7,15},{8,0},{9,1},... | collective-permute-start | bytes 313352 | tf_op jit(solution)/shard_map/ppermute | solution.py:49
  171.6 7.8 %collective-permute-start.39 = (bf16[24,2176]{1,0:T(8,128)(2,1)S(1)}, bf16[24,2176]{1,0:T(8,128)(2,1)S(1)}, u32[]{:S(2)}, u32[]{:S(2)}) collective-permute-start(bf16[24,2176]{1,0:T(8,128)(2,1)S(1)} %get-tuple-element.76), channel_id=1, source_target_pairs={{0,24},{1,25},{2,26},{3,27},{4,28},{5,29},{6,30},{7,31},{8,16},{9,... | collective-permute-start | bytes 313352 | tf_op jit(solution)/shard_map/ppermute | solution.py:49
  (22 other events, 186.2 us)

commit v4 on v3

--- a/solution.py
+++ b/solution.py
@@ -92,14 +92,14 @@
     return first, by_x, by_y
 
 
-def scatter_sides(first, by_x, by_y):
-    return add(first, flip(by_x, X), flip(by_y, Y))
-
-
-def scatter_z(first):
+def send_sides(first, by_x, by_y):
+    return [first, flip(by_x, X), flip(by_y, Y)]
+
+
+def send_z(first):
     step = first.shape[0] // depth()
     blocks = [first[k * step : (k + 1) * step] for k in range(depth())]
-    return add(blocks[0], *[flip(blocks[k], Z * k) for k in range(1, depth())])
+    return [blocks[0]] + [flip(blocks[k], Z * k) for k in range(1, depth())]
 
 
 def meta_kernel(sizes, cols, *refs):
@@ -684,15 +684,20 @@
         out = down_grad(turned, g, row_gain, 0, 4, None)
         dense[0], out = lax.optimization_barrier((dense[0], out))
         mine = [add(dense[k], flip(dense[k + 1], CORE)) for k in (0, 2)]
+        out = down_grad(turned, after(g, mine[1]), row_gain, 1, 4, out)
         sides = [scatter_far(rows_) for rows_ in mine]
-        firsts = [scatter_sides(*side) for side in sides]
-        shares = [scatter_z(first_) for first_ in firsts]
-        for k, gate in enumerate([sides[1][1], *firsts]):
-            out = down_grad(turned, after(g, gate), row_gain, k + 1, 4, out)
+        sent = [send_sides(*side) for side in sides]
+        out = down_grad(turned, after(g, sides[1][1]), row_gain, 2, 4, out)
+        *sent[0], out = lax.optimization_barrier((*sent[0], out))
+        firsts = [add(*rows_) for rows_ in sent]
+        shares = [send_z(first_) for first_ in firsts]
+        shares[0] = [after(block, firsts[1]) for block in shares[0]]
+        out = down_grad(turned, after(g, firsts[1]), row_gain, 3, 4, out)
+        shares = [add(*share) for share in shares]
         grad_downs.append(out)
     else:
         mine = add(dense[0].astype(bf16), flip(dense[1].astype(bf16), CORE))
-        shares = [scatter_z(scatter_sides(*scatter_far(mine)))]
+        shares = [add(*send_z(add(*send_sides(*scatter_far(mine)))))]
         grad_downs += [down_grad(*end, 0, 1, None) for end in ends]
     joined = jnp.concatenate(shares, axis=1)
     width = tokens.shape[1]

time: 183 us -> 179 us (0.978)
  waiting for transfers between devices: 50.5 us -> 45.9 us
    ppermute x40, waiting for transfers between devices: 50.5 us -> 45.9 us  [flip(): return lax.ppermute(value, 'wide', [(i, i ^ mask) for i in range(count)])]
    unnamed x35 -> x37, local copies, waits for them, and re-layouts: 7.27 us -> 7 us
  transfers between devices with their start and end apart: 40 -> 40, of which waited for: 19 -> 15; matrix products, arithmetic and copies ran while one was open for 6% -> 6% of each run, Pallas kernels for 22% -> 23%
where the time goes in v4:
time: 179 us
  Pallas kernels  75.4 us (42%)
  waiting for transfers between devices  45.9 us (26%)
  starting transfers between devices  39 us (22%)
  local copies, waits for them, and re-layouts  11.4 us (6%)
  other arithmetic  6.07 us (3%)
    ppermute x40, waiting for transfers between devices, flip(): return lax.ppermute(value, 'wide', [(i, i ^ mask) for i in range(count)])  45.9 us
    ppermute x40, starting transfers between devices, flip(): return lax.ppermute(value, 'wide', [(i, i ^ mask) for i in range(count)])  39 us
    pallas_call x1, Pallas kernels, pick_back(): call(functools.partial(pick_back_kernel, sizes, picks, blocks, ranges, to...  34.8 us
    pallas_call x4, Pallas kernels, down_grad(): call(functools.partial(down_kernel, len(turned)), 2 * rows * width * unit...  17.3 us
    pallas_call x1, Pallas kernels, pick_forward(): call(functools.partial(pick_forward_kernel, sizes, picks, blocks), 4 * ro...  15.2 us
    pallas_call x1, Pallas kernels, forward(): call(forward_kernel, 4 * rows * width * units, 4 * width * units, grid=(u...  7.16 us
    unnamed x37, local copies, waits for them, and re-layouts  7 us
  transfers between devices with their start and end apart: 40, of which 15 were waited for; matrix products, arithmetic and copies ran while one was open for 6% of the time, Pallas kernels for 23%

profile of v4, /device:TPU:0, one launch (start us, length us, event | category | flops | bytes accessed | tf_op | source)
XLA Modules:
  0.0 178.8 jit_solution(9281814843062295906)
XLA Ops:
  3.2 5.1 %collective-permute-start.2 = (bf16[24,4224]{1,0:T(8,128)(2,1)S(1)}, bf16[24,4224]{1,0:T(8,128)(2,1)S(1)}, u32[]{:S(2)}, u32[]{:S(2)}) collective-permute-start(bf16[24,4224]{1,0:T(8,128)(2,1)S(1)} %concatenate.24), channel_id=1, source_target_pairs={{0,24},{1,25},{2,26},{3,27},{4,28},{5,29},{6,30},{7,31},{8,16},{9,... | collective-permute-start | bytes 608264 | tf_op jit(solution)/shard_map/ppermute | solution.py:49
  8.9 5.4 %collective-permute-done.2 = bf16[24,4224]{1,0:T(8,128)(2,1)S(1)} collective-permute-done((bf16[24,4224]{1,0:T(8,128)(2,1)S(1)}, bf16[24,4224]{1,0:T(8,128)(2,1)S(1)}, u32[]{:S(2)}, u32[]{:S(2)}) %collective-permute-start.2) | collective-permute-done | bytes 202784 | tf_op jit(solution)/shard_map/ppermute | solution.py:49
  14.3 11.2 %collective-permute-done.1 = bf16[24,4224]{1,0:T(8,128)(2,1)S(1)} collective-permute-done((bf16[24,4224]{1,0:T(8,128)(2,1)S(1)}, bf16[24,4224]{1,0:T(8,128)(2,1)S(1)}, u32[]{:S(2)}, u32[]{:S(2)}) %collective-permute-start.1) | collective-permute-done | bytes 202784 | tf_op jit(solution)/shard_map/ppermute | solution.py:49
  25.6 1.6 collective-permute-start.3
  27.1 1.5 collective-permute-start.4
  28.7 1.6 constant_dynamic-update-slice_fusion.3
  30.3 3.0 %collective-permute-start.13 = (bf16[24,4096]{1,0:T(8,128)(2,1)}, bf16[24,4096]{1,0:T(8,128)(2,1)S(1)}, u32[]{:S(2)}, u32[]{:S(2)}) collective-permute-start(bf16[24,4096]{1,0:T(8,128)(2,1)} %param.8), channel_id=1, source_target_pairs={{0,16},{1,17},{2,18},{3,19},{4,20},{5,21},{6,22},{7,23},{8,24},{9,... | collective-permute-start | bytes 589832 | tf_op jit(solution)/shard_map/ppermute | solution.py:49
  33.4 5.2 %collective-permute-done.12 = bf16[24,4096]{1,0:T(8,128)(2,1)S(1)} collective-permute-done((bf16[24,4096]{1,0:T(8,128)(2,1)}, bf16[24,4096]{1,0:T(8,128)(2,1)S(1)}, u32[]{:S(2)}, u32[]{:S(2)}) %collective-permute-start.12) | collective-permute-done | bytes 196640 | tf_op jit(solution)/shard_map/ppermute | solution.py:49
  38.5 1.5 collective-permute-start.14
  40.7 5.3 %collective-permute-done.4.refs_2_ = bf16[96,4224]{1,0:T(8,128)(2,1)S(1)} collective-permute-done((bf16[96,4224]{1,0:T(8,128)(2,1)S(1)}, bf16[96,4224]{1,0:T(8,128)(2,1)S(1)}, u32[]{:S(2)}, u32[]{:S(2)}) %collective-permute-start.4) | collective-permute-done | bytes 811040 | tf_op jit(solution)/shard_map/ppermute | solution.py:49
  46.7 1.6 collective-permute-start.6
  49.5 5.9 %collective-permute-done.5.refs_3_ = bf16[48,4224]{1,0:T(8,128)(2,1)S(1)} collective-permute-done((bf16[48,4224]{1,0:T(8,128)(2,1)S(1)}, bf16[48,4224]{1,0:T(8,128)(2,1)S(1)}, u32[]{:S(2)}, u32[]{:S(2)}) %collective-permute-start.5) | collective-permute-done | bytes 405536 | tf_op jit(solution)/shard_map/ppermute | solution.py:49
  56.9 1.5 collective-permute-start.15
  58.4 1.5 collective-permute-start.16
  61.7 15.2 %shard_map.95 = (bf16[384,4096]{1,0:T(8,128)(2,1)}, bf16[384,1024]{1,0:T(8,128)(2,1)}, bf16[1024,384]{1,0:T(8,128)(2,1)}, bf16[384,1024]{1,0:T(8,128)(2,1)}, bf16[384,1024]{1,0:T(8,128)(2,1)}) custom-call(s32[1,768]{1,0:T(1,128)S(1)} %get-tuple-element.77.slot_ref, bf16[96,4224]{1,0:T(8,128)(2,1)} %copy-done.5, bf16[96,4224]{1,0:T(8,128)(2,1)} %copy-done.6, ...), custom_call_target="tpu_custom_call" | custom-call | flops 8858370048 | bytes 26214400 | tf_op jit(solution)/shard_map/pallas_call | solution.py:369
  80.7 1.6 collective-permute-start.18
  82.9 7.2 %shard_map.96 = (bf16[384,512]{1,0:T(8,128)(2,1)S(1)}, bf16[512,384]{1,0:T(8,128)(2,1)S(1)}, bf16[384,512]{1,0:T(8,128)(2,1)S(1)}, bf16[384,512]{1,0:T(8,128)(2,1)S(1)}) custom-call(bf16[384,4096]{1,0:T(8,128)(2,1)} %get-tuple-element.43.x_ref, bf16[4096,1536]{1,0:T(8,128)(2,1)} %bitcast.22, bf16[4096,1536]{1,0:T(8,128)(2,1)} %bitcast.25), custom_call_target="tpu_custom_call" | custom-call | flops 3221225472 | bytes 8388608 | tf_op jit(solution)/shard_map/pallas_call | solution.py:203
  94.6 34.8 %shard_map.97 = (bf16[384,4096]{1,0:T(8,128)(2,1)}, f32[384,1]{1,0:T(8,128)}, bf16[384,2048]{1,0:T(8,128)(2,1)}, bf16[384,2048]{1,0:T(8,128)(2,1)}, bf16[384,217...) custom-call(s32[1,768]{1,0:T(1,128)S(1)} %get-tuple-element.77.slot_ref, s32[768,1]{1,0:T(8,128)S(1)} %bitcast_select_fusion.slot_col, ...), custom_call_target="tpu_custom_call" | custom-call | flops 19327352832 | bytes 53477376 | tf_op jit(solution)/shard_map/pallas_call | solution.py:490
  130.1 4.4 %shard_map.98.refs_2_ = bf16[1536,4096]{1,0:T(8,128)(2,1)} custom-call(bf16[384,4096]{1,0:T(8,128)(2,1)} %get-tuple-element.69.g_ref, f32[384,1]{1,0:T(8,128)S(1)} %broadcast_in_dim.49.gain_ref, bf16[1024,384]{1,0:T(8,128)(2,1)S(1)} %copy-done, bf16[512,384]{1,0:T(8,128)(2,1)S(1)} %get-tuple-element.54.refs_1_), custom_call_target="tpu_custom_call" | custom-call | flops 1207959552 | bytes 3145728 | tf_op jit(solution)/shard_map/pallas_call | solution.py:588
  134.5 2.1 %add_convert_fusion.1 = bf16[384,2048]{1,0:T(8,128)(2,1)S(1)} fusion(bf16[384,2048]{1,0:T(8,128)(2,1)} %collective-permute-done.24, bf16[384,2048]{1,0:T(8,128)(2,1)S(1)} %copy-done.9), kind=kLoop, calls=%fused_computation.1 | loop fusion | flops 3145728 | bytes 4718592 | tf_op jit(solution)/shard_map/convert_element_type | solution.py:23
  136.7 1.5 collective-permute-start.27
  139.1 1.6 collective-permute-start.30
  141.3 4.3 %shard_map.99.refs_2_ = bf16[1536,4096]{1,0:T(8,128)(2,1)} custom-call(bf16[384,4096]{1,0:T(8,128)(2,1)} %get-tuple-element.69.g_ref, f32[384,1]{1,0:T(8,128)S(1)} %broadcast_in_dim.49.gain_ref, bf16[1024,384]{1,0:T(8,128)(2,1)S(1)} %copy-done, bf16[512,384]{1,0:T(8,128)(2,1)S(1)} %get-tuple-element.54.refs_1_, ...), custom_call_target="tpu_custom_call", output_to_operand_aliasing={{}: (4, {})} | custom-call | flops 1207959552 | bytes 3145728 | tf_op jit(solution)/shard_map/pallas_call | solution.py:588
  147.9 2.0 %collective-permute-done.30 = bf16[48,2176]{1,0:T(8,128)(2,1)S(1)} collective-permute-done((bf16[48,2176]{1,0:T(8,128)(2,1)S(1)}, bf16[48,2176]{1,0:T(8,128)(2,1)S(1)}, u32[]{:S(2)}, u32[]{:S(2)}) %collective-permute-start.30) | collective-permute-done | bytes 208928 | tf_op jit(solution)/shard_map/ppermute | solution.py:49
  150.7 4.3 %shard_map.100.refs_2_ = bf16[1536,4096]{1,0:T(8,128)(2,1)} custom-call(bf16[384,4096]{1,0:T(8,128)(2,1)} %get-tuple-element.69.g_ref, f32[384,1]{1,0:T(8,128)S(1)} %broadcast_in_dim.49.gain_ref, bf16[1024,384]{1,0:T(8,128)(2,1)S(1)} %copy-done, bf16[512,384]{1,0:T(8,128)(2,1)S(1)} %get-tuple-element.54.refs_1_, ...), custom_call_target="tpu_custom_call", output_to_operand_aliasing={{}: (4, {})} | custom-call | flops 1207959552 | bytes 3145728 | tf_op jit(solution)/shard_map/pallas_call | solution.py:588
  155.0 3.2 %collective-permute-done.26 = bf16[96,2048]{1,0:T(8,128)(2,1)S(1)} collective-permute-done((bf16[96,2048]{1,0:T(8,128)(2,1)S(1)}, bf16[96,2048]{1,0:T(8,128)(2,1)S(1)}, u32[]{:S(2)}, u32[]{:S(2)}) %collective-permute-start.26) | collective-permute-done | bytes 393248 | tf_op jit(solution)/shard_map/ppermute | solution.py:49
  159.6 2.2 %collective-permute-start.36 = (bf16[24,2048]{1,0:T(8,128)(2,1)S(1)}, bf16[24,2048]{1,0:T(8,128)(2,1)S(1)}, u32[]{:S(2)}, u32[]{:S(2)}) collective-permute-start(bf16[24,2048]{1,0:T(8,128)(2,1)S(1)} %get-tuple-element.95), channel_id=1, source_target_pairs={{0,24},{1,25},{2,26},{3,27},{4,28},{5,29},{6,30},{7,31},{8,16},{9,... | collective-permute-start | bytes 294920 | tf_op jit(solution)/shard_map/ppermute | solution.py:49
  161.8 2.3 %collective-permute-start.34 = (bf16[24,2048]{1,0:T(8,128)(2,1)S(1)}, bf16[24,2048]{1,0:T(8,128)(2,1)S(1)}, u32[]{:S(2)}, u32[]{:S(2)}) collective-permute-start(bf16[24,2048]{1,0:T(8,128)(2,1)S(1)} %get-tuple-element.97), channel_id=1, source_target_pairs={{0,8},{1,9},{2,10},{3,11},{4,12},{5,13},{6,14},{7,15},{8,0},{9,1},... | collective-permute-start | bytes 294920 | tf_op jit(solution)/shard_map/ppermute | solution.py:49
  164.1 2.6 %collective-permute-done.33 = bf16[96,2176]{1,0:T(8,128)(2,1)S(1)} collective-permute-done((bf16[96,2176]{1,0:T(8,128)(2,1)S(1)}, bf16[96,2176]{1,0:T(8,128)(2,1)S(1)}, u32[]{:S(2)}, u32[]{:S(2)}) %collective-permute-start.33) | collective-permute-done | bytes 417824 | tf_op jit(solution)/shard_map/ppermute | solution.py:49
  166.9 2.2 %collective-permute-start.39 = (bf16[24,2176]{1,0:T(8,128)(2,1)S(1)}, bf16[24,2176]{1,0:T(8,128)(2,1)S(1)}, u32[]{:S(2)}, u32[]{:S(2)}) collective-permute-start(bf16[24,2176]{1,0:T(8,128)(2,1)S(1)} %get-tuple-element.92), channel_id=1, source_target_pairs={{0,24},{1,25},{2,26},{3,27},{4,28},{5,29},{6,30},{7,31},{8,16},{9,... | collective-permute-start | bytes 313352 | tf_op jit(solution)/shard_map/ppermute | solution.py:49
  169.1 2.3 %collective-permute-start.37 = (bf16[24,2176]{1,0:T(8,128)(2,1)S(1)}, bf16[24,2176]{1,0:T(8,128)(2,1)S(1)}, u32[]{:S(2)}, u32[]{:S(2)}) collective-permute-start(bf16[24,2176]{1,0:T(8,128)(2,1)S(1)} %get-tuple-element.91), channel_id=1, source_target_pairs={{0,8},{1,9},{2,10},{3,11},{4,12},{5,13},{6,14},{7,15},{8,0},{9,1},... | collective-permute-start | bytes 313352 | tf_op jit(solution)/shard_map/ppermute | solution.py:49
  171.4 4.3 %shard_map.101 = bf16[1536,4096]{1,0:T(8,128)(2,1)} custom-call(bf16[384,4096]{1,0:T(8,128)(2,1)} %get-tuple-element.69.g_ref, f32[384,1]{1,0:T(8,128)S(1)} %broadcast_in_dim.49.gain_ref, bf16[1024,384]{1,0:T(8,128)(2,1)S(1)} %copy-done, bf16[512,384]{1,0:T(8,128)(2,1)S(1)} %get-tuple-element.54.refs_1_, ...), custom_call_target="tpu_custom_call", output_to_operand_aliasing={{}: (4, {})} | custom-call | flops 1207959552 | bytes 3145728 | tf_op jit(solution)/shard_map/pallas_call | solution.py:588
  (137 shorter events, 28.0 us)
Async XLA Ops:
  3.2 11.1 %collective-permute-start.2 = (bf16[24,4224]{1,0:T(8,128)(2,1)S(1)}, bf16[24,4224]{1,0:T(8,128)(2,1)S(1)}, u32[]{:S(2)}, u32[]{:S(2)}) collective-permute-start(bf16[24,4224]{1,0:T(8,128)(2,1)S(1)} %concatenate.24), channel_id=1, source_target_pairs={{0,24},{1,25},{2,26},{3,27},{4,28},{5,29},{6,30},{7,31},{8,16},{9,... | collective-permute-start | bytes 608264 | tf_op jit(solution)/shard_map/ppermute | solution.py:49
  8.3 17.2 %collective-permute-start.1 = (bf16[24,4224]{1,0:T(8,128)(2,1)S(1)}, bf16[24,4224]{1,0:T(8,128)(2,1)S(1)}, u32[]{:S(2)}, u32[]{:S(2)}) collective-permute-start(bf16[24,4224]{1,0:T(8,128)(2,1)S(1)} %concatenate.24), channel_id=1, source_target_pairs={{0,16},{1,17},{2,18},{3,19},{4,20},{5,21},{6,22},{7,23},{8,24},{9,... | collective-permute-start | bytes 608264 | tf_op jit(solution)/shard_map/ppermute | solution.py:49
  8.3 17.2 %collective-permute-start = (bf16[24,4224]{1,0:T(8,128)(2,1)S(1)}, bf16[24,4224]{1,0:T(8,128)(2,1)S(1)}, u32[]{:S(2)}, u32[]{:S(2)}) collective-permute-start(bf16[24,4224]{1,0:T(8,128)(2,1)S(1)} %concatenate.24), channel_id=1, source_target_pairs={{0,8},{1,9},{2,10},{3,11},{4,12},{5,13},{6,14},{7,15},{8,0},{9,1},... | collective-permute-start | bytes 608264 | tf_op jit(solution)/shard_map/ppermute | solution.py:49
  25.6 21.0 %collective-permute-start.3 = (bf16[96,4224]{1,0:T(8,128)(2,1)S(1)}, bf16[96,4224]{1,0:T(8,128)(2,1)S(1)}, u32[]{:S(2)}, u32[]{:S(2)}) collective-permute-start(bf16[96,4224]{1,0:T(8,128)(2,1)S(1)} %pad_maximum_fusion.refs_0_), channel_id=1, source_target_pairs={{0,2},{1,3},{2,0},{3,1},{4,6},{5,7},{6,4},{7,5},{8,10},{9,11},{10,... | collective-permute-start | bytes 2433032 | tf_op jit(solution)/shard_map/ppermute | solution.py:49
  27.1 18.8 %collective-permute-start.4 = (bf16[96,4224]{1,0:T(8,128)(2,1)S(1)}, bf16[96,4224]{1,0:T(8,128)(2,1)S(1)}, u32[]{:S(2)}, u32[]{:S(2)}) collective-permute-start(bf16[96,4224]{1,0:T(8,128)(2,1)S(1)} %pad_maximum_fusion.refs_0_), channel_id=1, source_target_pairs={{0,4},{1,5},{2,6},{3,7},{4,0},{5,1},{6,2},{7,3},{8,12},{9,13},{10,... | collective-permute-start | bytes 2433032 | tf_op jit(solution)/shard_map/ppermute | solution.py:49
  28.7 27.9 %collective-permute-start.7 = (bf16[96,4224]{1,0:T(8,128)(2,1)S(1)}, bf16[96,4224]{1,0:T(8,128)(2,1)S(1)}, u32[]{:S(2)}, u32[]{:S(2)}) collective-permute-start(bf16[96,4224]{1,0:T(8,128)(2,1)S(1)} %pad_maximum_fusion.refs_0_), channel_id=1, source_target_pairs={{0,1},{1,0},{2,3},{3,2},{4,5},{5,4},{6,7},{7,6},{8,9},{9,8},{10,11... | collective-permute-start | bytes 2433032 | tf_op jit(solution)/shard_map/ppermute | solution.py:49
  28.7 9.9 %collective-permute-start.12 = (bf16[24,4096]{1,0:T(8,128)(2,1)}, bf16[24,4096]{1,0:T(8,128)(2,1)S(1)}, u32[]{:S(2)}, u32[]{:S(2)}) collective-permute-start(bf16[24,4096]{1,0:T(8,128)(2,1)} %param.8), channel_id=1, source_target_pairs={{0,8},{1,9},{2,10},{3,11},{4,12},{5,13},{6,14},{7,15},{8,0},{9,1},... | collective-permute-start | bytes 589832 | tf_op jit(solution)/shard_map/ppermute | solution.py:49
  30.3 17.9 %collective-permute-start.13 = (bf16[24,4096]{1,0:T(8,128)(2,1)}, bf16[24,4096]{1,0:T(8,128)(2,1)S(1)}, u32[]{:S(2)}, u32[]{:S(2)}) collective-permute-start(bf16[24,4096]{1,0:T(8,128)(2,1)} %param.8), channel_id=1, source_target_pairs={{0,16},{1,17},{2,18},{3,19},{4,20},{5,21},{6,22},{7,23},{8,24},{9,... | collective-permute-start | bytes 589832 | tf_op jit(solution)/shard_map/ppermute | solution.py:49
  38.5 9.7 %collective-permute-start.14 = (bf16[24,4096]{1,0:T(8,128)(2,1)}, bf16[24,4096]{1,0:T(8,128)(2,1)S(1)}, u32[]{:S(2)}, u32[]{:S(2)}) collective-permute-start(bf16[24,4096]{1,0:T(8,128)(2,1)} %param.8), channel_id=1, source_target_pairs={{0,24},{1,25},{2,26},{3,27},{4,28},{5,29},{6,30},{7,31},{8,16},{9,... | collective-permute-start | bytes 589832 | tf_op jit(solution)/shard_map/ppermute | solution.py:49
  46.0 9.3 %collective-permute-start.5 = (bf16[48,4224]{1,0:T(8,128)(2,1)S(1)}, bf16[48,4224]{1,0:T(8,128)(2,1)S(1)}, u32[]{:S(2)}, u32[]{:S(2)}) collective-permute-start(bf16[48,4224]{1,0:T(8,128)(2,1)S(1)} %slice.147), channel_id=1, source_target_pairs={{0,2},{1,3},{2,0},{3,1},{4,6},{5,7},{6,4},{7,5},{8,10},{9,11},{10,... | collective-permute-start | bytes 1216520 | tf_op jit(solution)/shard_map/ppermute | solution.py:49
  46.7 9.0 %collective-permute-start.6 = (bf16[48,4224]{1,0:T(8,128)(2,1)S(1)}, bf16[48,4224]{1,0:T(8,128)(2,1)S(1)}, u32[]{:S(2)}, u32[]{:S(2)}) collective-permute-start(bf16[48,4224]{1,0:T(8,128)(2,1)S(1)} %slice.148), channel_id=1, source_target_pairs={{0,4},{1,5},{2,6},{3,7},{4,0},{5,1},{6,2},{7,3},{8,12},{9,13},{10,... | collective-permute-start | bytes 1216520 | tf_op jit(solution)/shard_map/ppermute | solution.py:49
  48.2 8.7 %collective-permute-start.8 = (bf16[96,4224]{1,0:T(8,128)(2,1)S(1)}, bf16[96,4224]{1,0:T(8,128)(2,1)S(1)}, u32[]{:S(2)}, u32[]{:S(2)}) collective-permute-start(bf16[96,4224]{1,0:T(8,128)(2,1)S(1)} %collective-permute-done.3.refs_1_), channel_id=1, source_target_pairs={{0,1},{1,0},{2,3},{3,2},{4,5},{5,4},{6,7},{7,6},{8,9},{9,8},{10,11... | collective-permute-start | bytes 2433032 | tf_op jit(solution)/shard_map/ppermute | solution.py:49
  48.3 10.1 %collective-permute-start.9 = (bf16[96,4224]{1,0:T(8,128)(2,1)S(1)}, bf16[96,4224]{1,0:T(8,128)(2,1)S(1)}, u32[]{:S(2)}, u32[]{:S(2)}) collective-permute-start(bf16[96,4224]{1,0:T(8,128)(2,1)S(1)} %collective-permute-done.4.refs_2_), channel_id=1, source_target_pairs={{0,1},{1,0},{2,3},{3,2},{4,5},{5,4},{6,7},{7,6},{8,9},{9,8},{10,11... | collective-permute-start | bytes 2433032 | tf_op jit(solution)/shard_map/ppermute | solution.py:49
  56.5 36.5 %collective-permute-start.19 = (bf16[96,4096]{1,0:T(8,128)(2,1)}, bf16[96,4096]{1,0:T(8,128)(2,1)}, u32[]{:S(2)}, u32[]{:S(2)}) collective-permute-start(bf16[96,4096]{1,0:T(8,128)(2,1)} %constant_dynamic-update-slice_fusion.refs_0_), channel_id=1, source_target_pairs={{0,1},{1,0},{2,3},{3,2},{4,5},{5,4},{6,7},{7,6},{8,9},{9,8},{10,11... | collective-permute-start | bytes 2359304 | tf_op jit(solution)/shard_map/ppermute | solution.py:49
  56.9 20.1 %collective-permute-start.15 = (bf16[96,4096]{1,0:T(8,128)(2,1)}, bf16[96,4096]{1,0:T(8,128)(2,1)}, u32[]{:S(2)}, u32[]{:S(2)}) collective-permute-start(bf16[96,4096]{1,0:T(8,128)(2,1)} %constant_dynamic-update-slice_fusion.refs_0_), channel_id=1, source_target_pairs={{0,2},{1,3},{2,0},{3,1},{4,6},{5,7},{6,4},{7,5},{8,10},{9,11},{10,... | collective-permute-start | bytes 2359304 | tf_op jit(solution)/shard_map/ppermute | solution.py:49
  58.4 19.6 %collective-permute-start.16 = (bf16[96,4096]{1,0:T(8,128)(2,1)}, bf16[96,4096]{1,0:T(8,128)(2,1)}, u32[]{:S(2)}, u32[]{:S(2)}) collective-permute-start(bf16[96,4096]{1,0:T(8,128)(2,1)} %constant_dynamic-update-slice_fusion.refs_0_), channel_id=1, source_target_pairs={{0,4},{1,5},{2,6},{3,7},{4,0},{5,1},{6,2},{7,3},{8,12},{9,13},{10,... | collective-permute-start | bytes 2359304 | tf_op jit(solution)/shard_map/ppermute | solution.py:49
  79.0 12.5 %collective-permute-start.17 = (bf16[48,4096]{1,0:T(8,128)(2,1)S(1)}, bf16[48,4096]{1,0:T(8,128)(2,1)S(1)}, u32[]{:S(2)}, u32[]{:S(2)}) collective-permute-start(bf16[48,4096]{1,0:T(8,128)(2,1)S(1)} %slice.121), channel_id=1, source_target_pairs={{0,2},{1,3},{2,0},{3,1},{4,6},{5,7},{6,4},{7,5},{8,10},{9,11},{10,... | collective-permute-start | bytes 1179656 | tf_op jit(solution)/shard_map/ppermute | solution.py:49
  80.7 10.8 %collective-permute-start.18 = (bf16[48,4096]{1,0:T(8,128)(2,1)S(1)}, bf16[48,4096]{1,0:T(8,128)(2,1)S(1)}, u32[]{:S(2)}, u32[]{:S(2)}) collective-permute-start(bf16[48,4096]{1,0:T(8,128)(2,1)S(1)} %slice.122), channel_id=1, source_target_pairs={{0,4},{1,5},{2,6},{3,7},{4,0},{5,1},{6,2},{7,3},{8,12},{9,13},{10,... | collective-permute-start | bytes 1179656 | tf_op jit(solution)/shard_map/ppermute | solution.py:49
  82.3 10.7 %collective-permute-start.20 = (bf16[96,4096]{1,0:T(8,128)(2,1)}, bf16[96,4096]{1,0:T(8,128)(2,1)}, u32[]{:S(2)}, u32[]{:S(2)}) collective-permute-start(bf16[96,4096]{1,0:T(8,128)(2,1)} %collective-permute-done.15.refs_1_), channel_id=1, source_target_pairs={{0,1},{1,0},{2,3},{3,2},{4,5},{5,4},{6,7},{7,6},{8,9},{9,8},{10,11... | collective-permute-start | bytes 2359304 | tf_op jit(solution)/shard_map/ppermute | solution.py:49
  82.3 10.7 %collective-permute-start.21 = (bf16[96,4096]{1,0:T(8,128)(2,1)}, bf16[96,4096]{1,0:T(8,128)(2,1)}, u32[]{:S(2)}, u32[]{:S(2)}) collective-permute-start(bf16[96,4096]{1,0:T(8,128)(2,1)} %collective-permute-done.16.refs_2_), channel_id=1, source_target_pairs={{0,1},{1,0},{2,3},{3,2},{4,5},{5,4},{6,7},{7,6},{8,9},{9,8},{10,11... | collective-permute-start | bytes 2359304 | tf_op jit(solution)/shard_map/ppermute | solution.py:49
  129.6 9.0 %collective-permute-start.29 = (bf16[384,2176]{1,0:T(8,128)(2,1)}, bf16[384,2176]{1,0:T(8,128)(2,1)S(1)}, u32[]{:S(2)}, u32[]{:S(2)}) collective-permute-start(bf16[384,2176]{1,0:T(8,128)(2,1)} %get-tuple-element.58), channel_id=1, source_target_pairs={{0,1},{1,0},{2,3},{3,2},{4,5},{5,4},{6,7},{7,6},{8,9},{9,8},{10,11... | collective-permute-start | bytes 5013512 | tf_op jit(solution)/shard_map/ppermute | solution.py:49
  136.7 8.9 %collective-permute-start.27 = (bf16[48,2048]{1,0:T(8,128)(2,1)S(1)}, bf16[48,2048]{1,0:T(8,128)(2,1)S(1)}, u32[]{:S(2)}, u32[]{:S(2)}) collective-permute-start(bf16[48,2048]{1,0:T(8,128)(2,1)S(1)} %get-tuple-element.87), channel_id=1, source_target_pairs={{0,2},{1,3},{2,0},{3,1},{4,6},{5,7},{6,4},{7,5},{8,10},{9,11},{10,... | collective-permute-start | bytes 589832 | tf_op jit(solution)/shard_map/ppermute | solution.py:49
  139.1 10.7 %collective-permute-start.30 = (bf16[48,2176]{1,0:T(8,128)(2,1)S(1)}, bf16[48,2176]{1,0:T(8,128)(2,1)S(1)}, u32[]{:S(2)}, u32[]{:S(2)}) collective-permute-start(bf16[48,2176]{1,0:T(8,128)(2,1)S(1)} %get-tuple-element.82), channel_id=1, source_target_pairs={{0,4},{1,5},{2,6},{3,7},{4,0},{5,1},{6,2},{7,3},{8,12},{9,13},{10,... | collective-permute-start | bytes 626696 | tf_op jit(solution)/shard_map/ppermute | solution.py:49
  140.7 9.1 %collective-permute-start.32 = (bf16[48,2176]{1,0:T(8,128)(2,1)S(1)}, bf16[48,2176]{1,0:T(8,128)(2,1)S(1)}, u32[]{:S(2)}, u32[]{:S(2)}) collective-permute-start(bf16[48,2176]{1,0:T(8,128)(2,1)S(1)} %get-tuple-element.81), channel_id=1, source_target_pairs={{0,2},{1,3},{2,0},{3,1},{4,6},{5,7},{6,4},{7,5},{8,10},{9,11},{10,... | collective-permute-start | bytes 626696 | tf_op jit(solution)/shard_map/ppermute | solution.py:49
  146.1 12.1 %collective-permute-start.26 = (bf16[96,2048]{1,0:T(8,128)(2,1)S(1)}, bf16[96,2048]{1,0:T(8,128)(2,1)S(1)}, u32[]{:S(2)}, u32[]{:S(2)}) collective-permute-start(bf16[96,2048]{1,0:T(8,128)(2,1)S(1)} %pad_maximum_fusion.3), channel_id=1, source_target_pairs={{0,2},{1,3},{2,0},{3,1},{4,6},{5,7},{6,4},{7,5},{8,10},{9,11},{10,... | collective-permute-start | bytes 1179656 | tf_op jit(solution)/shard_map/ppermute | solution.py:49
  147.3 12.1 %collective-permute-start.28 = (bf16[96,2048]{1,0:T(8,128)(2,1)S(1)}, bf16[96,2048]{1,0:T(8,128)(2,1)S(1)}, u32[]{:S(2)}, u32[]{:S(2)}) collective-permute-start(bf16[96,2048]{1,0:T(8,128)(2,1)S(1)} %pad_maximum_fusion.4), channel_id=1, source_target_pairs={{0,4},{1,5},{2,6},{3,7},{4,0},{5,1},{6,2},{7,3},{8,12},{9,13},{10,... | collective-permute-start | bytes 1179656 | tf_op jit(solution)/shard_map/ppermute | solution.py:49
  150.0 16.7 %collective-permute-start.31 = (bf16[96,2176]{1,0:T(8,128)(2,1)S(1)}, bf16[96,2176]{1,0:T(8,128)(2,1)S(1)}, u32[]{:S(2)}, u32[]{:S(2)}) collective-permute-start(bf16[96,2176]{1,0:T(8,128)(2,1)S(1)} %pad_maximum_fusion.1), channel_id=1, source_target_pairs={{0,2},{1,3},{2,0},{3,1},{4,6},{5,7},{6,4},{7,5},{8,10},{9,11},{10,... | collective-permute-start | bytes 1253384 | tf_op jit(solution)/shard_map/ppermute | solution.py:49
  150.5 16.2 %collective-permute-start.33 = (bf16[96,2176]{1,0:T(8,128)(2,1)S(1)}, bf16[96,2176]{1,0:T(8,128)(2,1)S(1)}, u32[]{:S(2)}, u32[]{:S(2)}) collective-permute-start(bf16[96,2176]{1,0:T(8,128)(2,1)S(1)} %pad_maximum_fusion.2), channel_id=1, source_target_pairs={{0,4},{1,5},{2,6},{3,7},{4,0},{5,1},{6,2},{7,3},{8,12},{9,13},{10,... | collective-permute-start | bytes 1253384 | tf_op jit(solution)/shard_map/ppermute | solution.py:49
  159.6 9.5 %collective-permute-start.36 = (bf16[24,2048]{1,0:T(8,128)(2,1)S(1)}, bf16[24,2048]{1,0:T(8,128)(2,1)S(1)}, u32[]{:S(2)}, u32[]{:S(2)}) collective-permute-start(bf16[24,2048]{1,0:T(8,128)(2,1)S(1)} %get-tuple-element.95), channel_id=1, source_target_pairs={{0,24},{1,25},{2,26},{3,27},{4,28},{5,29},{6,30},{7,31},{8,16},{9,... | collective-permute-start | bytes 294920 | tf_op jit(solution)/shard_map/ppermute | solution.py:49
  161.8 9.6 %collective-permute-start.35 = (bf16[24,2048]{1,0:T(8,128)(2,1)S(1)}, bf16[24,2048]{1,0:T(8,128)(2,1)S(1)}, u32[]{:S(2)}, u32[]{:S(2)}) collective-permute-start(bf16[24,2048]{1,0:T(8,128)(2,1)S(1)} %get-tuple-element.96), channel_id=1, source_target_pairs={{0,16},{1,17},{2,18},{3,19},{4,20},{5,21},{6,22},{7,23},{8,24},{9,... | collective-permute-start | bytes 294920 | tf_op jit(solution)/shard_map/ppermute | solution.py:49
  161.8 9.6 %collective-permute-start.34 = (bf16[24,2048]{1,0:T(8,128)(2,1)S(1)}, bf16[24,2048]{1,0:T(8,128)(2,1)S(1)}, u32[]{:S(2)}, u32[]{:S(2)}) collective-permute-start(bf16[24,2048]{1,0:T(8,128)(2,1)S(1)} %get-tuple-element.97), channel_id=1, source_target_pairs={{0,8},{1,9},{2,10},{3,11},{4,12},{5,13},{6,14},{7,15},{8,0},{9,1},... | collective-permute-start | bytes 294920 | tf_op jit(solution)/shard_map/ppermute | solution.py:49
  166.9 8.8 %collective-permute-start.39 = (bf16[24,2176]{1,0:T(8,128)(2,1)S(1)}, bf16[24,2176]{1,0:T(8,128)(2,1)S(1)}, u32[]{:S(2)}, u32[]{:S(2)}) collective-permute-start(bf16[24,2176]{1,0:T(8,128)(2,1)S(1)} %get-tuple-element.92), channel_id=1, source_target_pairs={{0,24},{1,25},{2,26},{3,27},{4,28},{5,29},{6,30},{7,31},{8,16},{9,... | collective-permute-start | bytes 313352 | tf_op jit(solution)/shard_map/ppermute | solution.py:49
  (24 other events, 211.9 us)

commit v5 on v4

--- a/solution.py
+++ b/solution.py
@@ -387,7 +387,7 @@
     return x, ahead
 
 
-def pick_back_kernel(sizes, picks, blocks, ranges, tokens, slot_ref, slot_col, gain_ref, expert_ref, *refs):
+def pick_back_kernel(sizes, picks, blocks, ranges, tokens, half, slot_ref, slot_col, gain_ref, expert_ref, *refs):
     count = len(sizes)
     pieces, (down_any, gate_any, up_any), refs = refs[:count], refs[count : count + 3], refs[count + 3 :]
     *refs, held, place, rows_ref, piece_sems, x_sems, downs, gates, ups, d_gate, d_up, sems, token_sems = refs
@@ -451,11 +451,11 @@
         part = dot(d_gate[...], gates[to], ((1,), (1,)))
         part = (part + dot(d_up[...], ups[to], ((1,), (1,)))).astype(bf16)
 
-        @pl.when(at < tokens // 2)
+        @pl.when(at < half)
         def _():
             spread_rows(slot_col, part, (own_0, other_0))
 
-        @pl.when(at >= tokens // 2)
+        @pl.when(at >= half)
         def _():
             spread_rows(slot_col, part, (own_1, other_1))
 
@@ -479,7 +479,7 @@
     ranges = list(zip([0] + ends[:-1], ends))
     token_block = tile(cols, 512)
     tokens = cols // token_block
-    half = tokens // 2
+    half = tokens * 5 // 8
     base = picks + blocks
     dense_0 = pl.BlockSpec((total // 2, token_block), lambda i: (0, jnp.clip(i - base, 0, half - 1)))
     dense_1 = pl.BlockSpec((total // 2, token_block), lambda i: (0, jnp.maximum(i - base - half, 0)))
@@ -488,7 +488,7 @@
         return pl.BlockSpec((rows, block), lambda i: (0, jnp.clip(i - picks - part[0], 0, part[1] - part[0] - 1)))
 
     return call(
-        functools.partial(pick_back_kernel, sizes, picks, blocks, ranges, tokens),
+        functools.partial(pick_back_kernel, sizes, picks, blocks, ranges, tokens, half),
         2 * rows * (3 * cols * units + 2 * total * cols),
         6 * cols * units + 2 * (rows + 2 * total) * cols,
         grid=(base + tokens + 1,),
@@ -683,16 +683,21 @@
         (turned, g, row_gain), = ends
         out = down_grad(turned, g, row_gain, 0, 4, None)
         dense[0], out = lax.optimization_barrier((dense[0], out))
-        mine = [add(dense[k], flip(dense[k + 1], CORE)) for k in (0, 2)]
+        mine = [add(dense[0], flip(dense[1], CORE))]
+        mine.append(add(after(dense[2], mine[0]), flip(dense[3], CORE)))
         out = down_grad(turned, after(g, mine[1]), row_gain, 1, 4, out)
         sides = [scatter_far(rows_) for rows_ in mine]
+        sides[1] = lax.optimization_barrier((*sides[1], sides[0][1], sides[0][2]))[:3]
         sent = [send_sides(*side) for side in sides]
         out = down_grad(turned, after(g, sides[1][1]), row_gain, 2, 4, out)
         *sent[0], out = lax.optimization_barrier((*sent[0], out))
-        firsts = [add(*rows_) for rows_ in sent]
-        shares = [send_z(first_) for first_ in firsts]
-        shares[0] = [after(block, firsts[1]) for block in shares[0]]
+        firsts = [add(*sent[0])]
+        shares = [send_z(firsts[0])]
+        sent[1] = lax.optimization_barrier((*sent[1], shares[0][1]))[:3]
+        firsts.append(add(*sent[1]))
+        shares.append(send_z(firsts[1]))
         out = down_grad(turned, after(g, firsts[1]), row_gain, 3, 4, out)
+        *shares[0], out = lax.optimization_barrier((*shares[0], out))
         shares = [add(*share) for share in shares]
         grad_downs.append(out)
     else:

time: 179 us -> 180 us (level)
    unnamed x37 -> x39, local copies, waits for them, and re-layouts: 7 us -> 7 us
  transfers between devices with their start and end apart: 40 -> 40, of which waited for: 15 -> 16; matrix products, arithmetic and copies ran while one was open for 6% -> 6% of each run, Pallas kernels for 23% -> 23%
where the time goes in v5:
time: 180 us; the launch traced here: 179 us
  Pallas kernels  75.4 us (42%)
  waiting for transfers between devices  47.3 us (26%)
  starting transfers between devices  39.3 us (22%)
  local copies, waits for them, and re-layouts  12 us (7%)
  other arithmetic  4.39 us (2%)
    ppermute x40, waiting for transfers between devices, flip(): return lax.ppermute(value, 'wide', [(i, i ^ mask) for i in range(count)])  47.3 us
    ppermute x40, starting transfers between devices, flip(): return lax.ppermute(value, 'wide', [(i, i ^ mask) for i in range(count)])  39.3 us
    pallas_call x1, Pallas kernels, pick_back(): call(functools.partial(pick_back_kernel, sizes, picks, blocks, ranges, to...  34.8 us
    pallas_call x4, Pallas kernels, down_grad(): call(functools.partial(down_kernel, len(turned)), 2 * rows * width * unit...  17.3 us
    pallas_call x1, Pallas kernels, pick_forward(): call(functools.partial(pick_forward_kernel, sizes, picks, blocks), 4 * ro...  15.2 us
    pallas_call x1, Pallas kernels, forward(): call(forward_kernel, 4 * rows * width * units, 4 * width * units, grid=(u...  7.16 us
    unnamed x39, local copies, waits for them, and re-layouts  7 us
  transfers between devices with their start and end apart: 40, of which 16 were waited for; matrix products, arithmetic and copies ran while one was open for 6% of the time, Pallas kernels for 23%

profile of v5, /device:TPU:0, one launch (start us, length us, event | category | flops | bytes accessed | tf_op | source)
XLA Modules:
  0.0 179.5 jit_solution(10533434543259024452)
XLA Ops:
  3.2 5.1 %collective-permute-start.2 = (bf16[24,4224]{1,0:T(8,128)(2,1)S(1)}, bf16[24,4224]{1,0:T(8,128)(2,1)S(1)}, u32[]{:S(2)}, u32[]{:S(2)}) collective-permute-start(bf16[24,4224]{1,0:T(8,128)(2,1)S(1)} %concatenate.24), channel_id=1, source_target_pairs={{0,24},{1,25},{2,26},{3,27},{4,28},{5,29},{6,30},{7,31},{8,16},{9,... | collective-permute-start | bytes 608264 | tf_op jit(solution)/shard_map/ppermute | solution.py:49
  8.9 5.4 %collective-permute-done.2 = bf16[24,4224]{1,0:T(8,128)(2,1)S(1)} collective-permute-done((bf16[24,4224]{1,0:T(8,128)(2,1)S(1)}, bf16[24,4224]{1,0:T(8,128)(2,1)S(1)}, u32[]{:S(2)}, u32[]{:S(2)}) %collective-permute-start.2) | collective-permute-done | bytes 202784 | tf_op jit(solution)/shard_map/ppermute | solution.py:49
  14.3 11.2 %collective-permute-done.1 = bf16[24,4224]{1,0:T(8,128)(2,1)S(1)} collective-permute-done((bf16[24,4224]{1,0:T(8,128)(2,1)S(1)}, bf16[24,4224]{1,0:T(8,128)(2,1)S(1)}, u32[]{:S(2)}, u32[]{:S(2)}) %collective-permute-start.1) | collective-permute-done | bytes 202784 | tf_op jit(solution)/shard_map/ppermute | solution.py:49
  25.6 1.6 collective-permute-start.3
  27.1 1.5 collective-permute-start.4
  28.7 1.6 constant_dynamic-update-slice_fusion.3
  30.3 3.0 %collective-permute-start.13 = (bf16[24,4096]{1,0:T(8,128)(2,1)}, bf16[24,4096]{1,0:T(8,128)(2,1)S(1)}, u32[]{:S(2)}, u32[]{:S(2)}) collective-permute-start(bf16[24,4096]{1,0:T(8,128)(2,1)} %param.8), channel_id=1, source_target_pairs={{0,16},{1,17},{2,18},{3,19},{4,20},{5,21},{6,22},{7,23},{8,24},{9,... | collective-permute-start | bytes 589832 | tf_op jit(solution)/shard_map/ppermute | solution.py:49
  33.4 5.2 %collective-permute-done.12 = bf16[24,4096]{1,0:T(8,128)(2,1)S(1)} collective-permute-done((bf16[24,4096]{1,0:T(8,128)(2,1)}, bf16[24,4096]{1,0:T(8,128)(2,1)S(1)}, u32[]{:S(2)}, u32[]{:S(2)}) %collective-permute-start.12) | collective-permute-done | bytes 196640 | tf_op jit(solution)/shard_map/ppermute | solution.py:49
  38.5 1.5 collective-permute-start.14
  40.7 5.3 %collective-permute-done.4.refs_2_ = bf16[96,4224]{1,0:T(8,128)(2,1)S(1)} collective-permute-done((bf16[96,4224]{1,0:T(8,128)(2,1)S(1)}, bf16[96,4224]{1,0:T(8,128)(2,1)S(1)}, u32[]{:S(2)}, u32[]{:S(2)}) %collective-permute-start.4) | collective-permute-done | bytes 811040 | tf_op jit(solution)/shard_map/ppermute | solution.py:49
  46.7 1.6 collective-permute-start.6
  49.5 5.9 %collective-permute-done.5.refs_3_ = bf16[48,4224]{1,0:T(8,128)(2,1)S(1)} collective-permute-done((bf16[48,4224]{1,0:T(8,128)(2,1)S(1)}, bf16[48,4224]{1,0:T(8,128)(2,1)S(1)}, u32[]{:S(2)}, u32[]{:S(2)}) %collective-permute-start.5) | collective-permute-done | bytes 405536 | tf_op jit(solution)/shard_map/ppermute | solution.py:49
  56.9 1.5 collective-permute-start.15
  58.4 1.5 collective-permute-start.16
  61.7 15.2 %shard_map.95 = (bf16[384,4096]{1,0:T(8,128)(2,1)}, bf16[384,1024]{1,0:T(8,128)(2,1)}, bf16[1024,384]{1,0:T(8,128)(2,1)}, bf16[384,1024]{1,0:T(8,128)(2,1)}, bf16[384,1024]{1,0:T(8,128)(2,1)}) custom-call(s32[1,768]{1,0:T(1,128)S(1)} %get-tuple-element.93.slot_ref, bf16[96,4224]{1,0:T(8,128)(2,1)} %copy-done.6, bf16[96,4224]{1,0:T(8,128)(2,1)} %copy-done.8, ...), custom_call_target="tpu_custom_call" | custom-call | flops 8858370048 | bytes 26214400 | tf_op jit(solution)/shard_map/pallas_call | solution.py:369
  80.7 1.6 collective-permute-start.18
  82.9 7.2 %shard_map.96 = (bf16[384,512]{1,0:T(8,128)(2,1)S(1)}, bf16[512,384]{1,0:T(8,128)(2,1)S(1)}, bf16[384,512]{1,0:T(8,128)(2,1)S(1)}, bf16[384,512]{1,0:T(8,128)(2,1)S(1)}) custom-call(bf16[384,4096]{1,0:T(8,128)(2,1)} %get-tuple-element.51.x_ref, bf16[4096,1536]{1,0:T(8,128)(2,1)} %bitcast.22, bf16[4096,1536]{1,0:T(8,128)(2,1)} %bitcast.25), custom_call_target="tpu_custom_call" | custom-call | flops 3221225472 | bytes 8388608 | tf_op jit(solution)/shard_map/pallas_call | solution.py:203
  94.6 34.8 %shard_map.97 = (bf16[384,4096]{1,0:T(8,128)(2,1)}, f32[384,1]{1,0:T(8,128)}, bf16[384,2560]{1,0:T(8,128)(2,1)}, bf16[384,2560]{1,0:T(8,128)(2,1)}, bf16[384,166...) custom-call(s32[1,768]{1,0:T(1,128)S(1)} %get-tuple-element.93.slot_ref, s32[768,1]{1,0:T(8,128)S(1)} %bitcast_select_fusion.slot_col, ...), custom_call_target="tpu_custom_call" | custom-call | flops 19327352832 | bytes 53477376 | tf_op jit(solution)/shard_map/pallas_call | solution.py:490
  130.0 4.4 %shard_map.98.refs_2_ = bf16[1536,4096]{1,0:T(8,128)(2,1)} custom-call(bf16[384,4096]{1,0:T(8,128)(2,1)} %get-tuple-element.80.g_ref, f32[384,1]{1,0:T(8,128)S(1)} %broadcast_in_dim.49.gain_ref, bf16[1024,384]{1,0:T(8,128)(2,1)S(1)} %copy-done, bf16[512,384]{1,0:T(8,128)(2,1)S(1)} %get-tuple-element.62.refs_1_), custom_call_target="tpu_custom_call" | custom-call | flops 1207959552 | bytes 3145728 | tf_op jit(solution)/shard_map/pallas_call | solution.py:588
  135.0 1.5 collective-permute-start.27
  137.4 1.4 collective-permute-start.31
  139.5 4.3 %shard_map.99.refs_2_ = bf16[1536,4096]{1,0:T(8,128)(2,1)} custom-call(bf16[384,4096]{1,0:T(8,128)(2,1)} %get-tuple-element.80.g_ref, f32[384,1]{1,0:T(8,128)S(1)} %broadcast_in_dim.49.gain_ref, bf16[1024,384]{1,0:T(8,128)(2,1)S(1)} %copy-done, bf16[512,384]{1,0:T(8,128)(2,1)S(1)} %get-tuple-element.62.refs_1_, ...), custom_call_target="tpu_custom_call", output_to_operand_aliasing={{}: (4, {})} | custom-call | flops 1207959552 | bytes 3145728 | tf_op jit(solution)/shard_map/pallas_call | solution.py:588
  143.9 1.5 collective-permute-done.25
  146.9 1.4 collective-permute-done.30
  150.0 4.3 %shard_map.100.refs_2_ = bf16[1536,4096]{1,0:T(8,128)(2,1)} custom-call(bf16[384,4096]{1,0:T(8,128)(2,1)} %get-tuple-element.80.g_ref, f32[384,1]{1,0:T(8,128)S(1)} %broadcast_in_dim.49.gain_ref, bf16[1024,384]{1,0:T(8,128)(2,1)S(1)} %copy-done, bf16[512,384]{1,0:T(8,128)(2,1)S(1)} %get-tuple-element.62.refs_1_, ...), custom_call_target="tpu_custom_call", output_to_operand_aliasing={{}: (4, {})} | custom-call | flops 1207959552 | bytes 3145728 | tf_op jit(solution)/shard_map/pallas_call | solution.py:588
  154.3 5.5 %collective-permute-done.26 = bf16[96,2560]{1,0:T(8,128)(2,1)S(1)} collective-permute-done((bf16[96,2560]{1,0:T(8,128)(2,1)S(1)}, bf16[96,2560]{1,0:T(8,128)(2,1)S(1)}, u32[]{:S(2)}, u32[]{:S(2)}) %collective-permute-start.26) | collective-permute-done | bytes 491552 | tf_op jit(solution)/shard_map/ppermute | solution.py:49
  161.4 2.7 %collective-permute-start.33 = (bf16[24,2560]{1,0:T(8,128)(2,1)S(1)}, bf16[24,2560]{1,0:T(8,128)(2,1)S(1)}, u32[]{:S(2)}, u32[]{:S(2)}) collective-permute-start(bf16[24,2560]{1,0:T(8,128)(2,1)S(1)} %get-tuple-element.108), channel_id=1, source_target_pairs={{0,16},{1,17},{2,18},{3,19},{4,20},{5,21},{6,22},{7,23},{8,24},{9,... | collective-permute-start | bytes 368648 | tf_op jit(solution)/shard_map/ppermute | solution.py:49
  164.0 1.7 collective-permute-start.34
  167.0 2.2 %collective-permute-start.39 = (bf16[24,1664]{1,0:T(8,128)(2,1)S(1)}, bf16[24,1664]{1,0:T(8,128)(2,1)S(1)}, u32[]{:S(2)}, u32[]{:S(2)}) collective-permute-start(bf16[24,1664]{1,0:T(8,128)(2,1)S(1)} %get-tuple-element.112), channel_id=1, source_target_pairs={{0,24},{1,25},{2,26},{3,27},{4,28},{5,29},{6,30},{7,31},{8,16},{9,... | collective-permute-start | bytes 239624 | tf_op jit(solution)/shard_map/ppermute | solution.py:49
  169.2 2.3 %collective-permute-start.37 = (bf16[24,1664]{1,0:T(8,128)(2,1)S(1)}, bf16[24,1664]{1,0:T(8,128)(2,1)S(1)}, u32[]{:S(2)}, u32[]{:S(2)}) collective-permute-start(bf16[24,1664]{1,0:T(8,128)(2,1)S(1)} %get-tuple-element.111), channel_id=1, source_target_pairs={{0,8},{1,9},{2,10},{3,11},{4,12},{5,13},{6,14},{7,15},{8,0},{9,1},... | collective-permute-start | bytes 239624 | tf_op jit(solution)/shard_map/ppermute | solution.py:49
  171.5 4.3 %shard_map.101 = bf16[1536,4096]{1,0:T(8,128)(2,1)} custom-call(bf16[384,4096]{1,0:T(8,128)(2,1)} %get-tuple-element.80.g_ref, f32[384,1]{1,0:T(8,128)S(1)} %broadcast_in_dim.49.gain_ref, bf16[1024,384]{1,0:T(8,128)(2,1)S(1)} %copy-done, bf16[512,384]{1,0:T(8,128)(2,1)S(1)} %get-tuple-element.62.refs_1_, ...), custom_call_target="tpu_custom_call", output_to_operand_aliasing={{}: (4, {})} | custom-call | flops 1207959552 | bytes 3145728 | tf_op jit(solution)/shard_map/pallas_call | solution.py:588
  175.8 2.0 %collective-permute-done.38 = bf16[24,1664]{1,0:T(8,128)(2,1)S(1)} collective-permute-done((bf16[24,1664]{1,0:T(8,128)(2,1)S(1)}, bf16[24,1664]{1,0:T(8,128)(2,1)S(1)}, u32[]{:S(2)}, u32[]{:S(2)}) %collective-permute-start.38) | collective-permute-done | bytes 79904 | tf_op jit(solution)/shard_map/ppermute | solution.py:49
  (140 shorter events, 28.5 us)
Async XLA Ops:
  3.2 11.1 %collective-permute-start.2 = (bf16[24,4224]{1,0:T(8,128)(2,1)S(1)}, bf16[24,4224]{1,0:T(8,128)(2,1)S(1)}, u32[]{:S(2)}, u32[]{:S(2)}) collective-permute-start(bf16[24,4224]{1,0:T(8,128)(2,1)S(1)} %concatenate.24), channel_id=1, source_target_pairs={{0,24},{1,25},{2,26},{3,27},{4,28},{5,29},{6,30},{7,31},{8,16},{9,... | collective-permute-start | bytes 608264 | tf_op jit(solution)/shard_map/ppermute | solution.py:49
  8.3 17.2 %collective-permute-start.1 = (bf16[24,4224]{1,0:T(8,128)(2,1)S(1)}, bf16[24,4224]{1,0:T(8,128)(2,1)S(1)}, u32[]{:S(2)}, u32[]{:S(2)}) collective-permute-start(bf16[24,4224]{1,0:T(8,128)(2,1)S(1)} %concatenate.24), channel_id=1, source_target_pairs={{0,16},{1,17},{2,18},{3,19},{4,20},{5,21},{6,22},{7,23},{8,24},{9,... | collective-permute-start | bytes 608264 | tf_op jit(solution)/shard_map/ppermute | solution.py:49
  8.3 17.2 %collective-permute-start = (bf16[24,4224]{1,0:T(8,128)(2,1)S(1)}, bf16[24,4224]{1,0:T(8,128)(2,1)S(1)}, u32[]{:S(2)}, u32[]{:S(2)}) collective-permute-start(bf16[24,4224]{1,0:T(8,128)(2,1)S(1)} %concatenate.24), channel_id=1, source_target_pairs={{0,8},{1,9},{2,10},{3,11},{4,12},{5,13},{6,14},{7,15},{8,0},{9,1},... | collective-permute-start | bytes 608264 | tf_op jit(solution)/shard_map/ppermute | solution.py:49
  25.6 21.0 %collective-permute-start.3 = (bf16[96,4224]{1,0:T(8,128)(2,1)S(1)}, bf16[96,4224]{1,0:T(8,128)(2,1)S(1)}, u32[]{:S(2)}, u32[]{:S(2)}) collective-permute-start(bf16[96,4224]{1,0:T(8,128)(2,1)S(1)} %pad_maximum_fusion.refs_0_), channel_id=1, source_target_pairs={{0,2},{1,3},{2,0},{3,1},{4,6},{5,7},{6,4},{7,5},{8,10},{9,11},{10,... | collective-permute-start | bytes 2433032 | tf_op jit(solution)/shard_map/ppermute | solution.py:49
  27.1 18.8 %collective-permute-start.4 = (bf16[96,4224]{1,0:T(8,128)(2,1)S(1)}, bf16[96,4224]{1,0:T(8,128)(2,1)S(1)}, u32[]{:S(2)}, u32[]{:S(2)}) collective-permute-start(bf16[96,4224]{1,0:T(8,128)(2,1)S(1)} %pad_maximum_fusion.refs_0_), channel_id=1, source_target_pairs={{0,4},{1,5},{2,6},{3,7},{4,0},{5,1},{6,2},{7,3},{8,12},{9,13},{10,... | collective-permute-start | bytes 2433032 | tf_op jit(solution)/shard_map/ppermute | solution.py:49
  28.7 27.9 %collective-permute-start.7 = (bf16[96,4224]{1,0:T(8,128)(2,1)S(1)}, bf16[96,4224]{1,0:T(8,128)(2,1)S(1)}, u32[]{:S(2)}, u32[]{:S(2)}) collective-permute-start(bf16[96,4224]{1,0:T(8,128)(2,1)S(1)} %pad_maximum_fusion.refs_0_), channel_id=1, source_target_pairs={{0,1},{1,0},{2,3},{3,2},{4,5},{5,4},{6,7},{7,6},{8,9},{9,8},{10,11... | collective-permute-start | bytes 2433032 | tf_op jit(solution)/shard_map/ppermute | solution.py:49
  28.7 9.9 %collective-permute-start.12 = (bf16[24,4096]{1,0:T(8,128)(2,1)}, bf16[24,4096]{1,0:T(8,128)(2,1)S(1)}, u32[]{:S(2)}, u32[]{:S(2)}) collective-permute-start(bf16[24,4096]{1,0:T(8,128)(2,1)} %param.8), channel_id=1, source_target_pairs={{0,8},{1,9},{2,10},{3,11},{4,12},{5,13},{6,14},{7,15},{8,0},{9,1},... | collective-permute-start | bytes 589832 | tf_op jit(solution)/shard_map/ppermute | solution.py:49
  30.3 17.9 %collective-permute-start.13 = (bf16[24,4096]{1,0:T(8,128)(2,1)}, bf16[24,4096]{1,0:T(8,128)(2,1)S(1)}, u32[]{:S(2)}, u32[]{:S(2)}) collective-permute-start(bf16[24,4096]{1,0:T(8,128)(2,1)} %param.8), channel_id=1, source_target_pairs={{0,16},{1,17},{2,18},{3,19},{4,20},{5,21},{6,22},{7,23},{8,24},{9,... | collective-permute-start | bytes 589832 | tf_op jit(solution)/shard_map/ppermute | solution.py:49
  38.5 9.7 %collective-permute-start.14 = (bf16[24,4096]{1,0:T(8,128)(2,1)}, bf16[24,4096]{1,0:T(8,128)(2,1)S(1)}, u32[]{:S(2)}, u32[]{:S(2)}) collective-permute-start(bf16[24,4096]{1,0:T(8,128)(2,1)} %param.8), channel_id=1, source_target_pairs={{0,24},{1,25},{2,26},{3,27},{4,28},{5,29},{6,30},{7,31},{8,16},{9,... | collective-permute-start | bytes 589832 | tf_op jit(solution)/shard_map/ppermute | solution.py:49
  46.0 9.3 %collective-permute-start.5 = (bf16[48,4224]{1,0:T(8,128)(2,1)S(1)}, bf16[48,4224]{1,0:T(8,128)(2,1)S(1)}, u32[]{:S(2)}, u32[]{:S(2)}) collective-permute-start(bf16[48,4224]{1,0:T(8,128)(2,1)S(1)} %slice.147), channel_id=1, source_target_pairs={{0,2},{1,3},{2,0},{3,1},{4,6},{5,7},{6,4},{7,5},{8,10},{9,11},{10,... | collective-permute-start | bytes 1216520 | tf_op jit(solution)/shard_map/ppermute | solution.py:49
  46.7 9.0 %collective-permute-start.6 = (bf16[48,4224]{1,0:T(8,128)(2,1)S(1)}, bf16[48,4224]{1,0:T(8,128)(2,1)S(1)}, u32[]{:S(2)}, u32[]{:S(2)}) collective-permute-start(bf16[48,4224]{1,0:T(8,128)(2,1)S(1)} %slice.148), channel_id=1, source_target_pairs={{0,4},{1,5},{2,6},{3,7},{4,0},{5,1},{6,2},{7,3},{8,12},{9,13},{10,... | collective-permute-start | bytes 1216520 | tf_op jit(solution)/shard_map/ppermute | solution.py:49
  48.3 10.1 %collective-permute-start.9 = (bf16[96,4224]{1,0:T(8,128)(2,1)S(1)}, bf16[96,4224]{1,0:T(8,128)(2,1)S(1)}, u32[]{:S(2)}, u32[]{:S(2)}) collective-permute-start(bf16[96,4224]{1,0:T(8,128)(2,1)S(1)} %collective-permute-done.4.refs_2_), channel_id=1, source_target_pairs={{0,1},{1,0},{2,3},{3,2},{4,5},{5,4},{6,7},{7,6},{8,9},{9,8},{10,11... | collective-permute-start | bytes 2433032 | tf_op jit(solution)/shard_map/ppermute | solution.py:49
  56.5 36.5 %collective-permute-start.19 = (bf16[96,4096]{1,0:T(8,128)(2,1)}, bf16[96,4096]{1,0:T(8,128)(2,1)}, u32[]{:S(2)}, u32[]{:S(2)}) collective-permute-start(bf16[96,4096]{1,0:T(8,128)(2,1)} %constant_dynamic-update-slice_fusion.refs_0_), channel_id=1, source_target_pairs={{0,1},{1,0},{2,3},{3,2},{4,5},{5,4},{6,7},{7,6},{8,9},{9,8},{10,11... | collective-permute-start | bytes 2359304 | tf_op jit(solution)/shard_map/ppermute | solution.py:49
  56.9 20.1 %collective-permute-start.15 = (bf16[96,4096]{1,0:T(8,128)(2,1)}, bf16[96,4096]{1,0:T(8,128)(2,1)}, u32[]{:S(2)}, u32[]{:S(2)}) collective-permute-start(bf16[96,4096]{1,0:T(8,128)(2,1)} %constant_dynamic-update-slice_fusion.refs_0_), channel_id=1, source_target_pairs={{0,2},{1,3},{2,0},{3,1},{4,6},{5,7},{6,4},{7,5},{8,10},{9,11},{10,... | collective-permute-start | bytes 2359304 | tf_op jit(solution)/shard_map/ppermute | solution.py:49
  58.4 19.6 %collective-permute-start.16 = (bf16[96,4096]{1,0:T(8,128)(2,1)}, bf16[96,4096]{1,0:T(8,128)(2,1)}, u32[]{:S(2)}, u32[]{:S(2)}) collective-permute-start(bf16[96,4096]{1,0:T(8,128)(2,1)} %constant_dynamic-update-slice_fusion.refs_0_), channel_id=1, source_target_pairs={{0,4},{1,5},{2,6},{3,7},{4,0},{5,1},{6,2},{7,3},{8,12},{9,13},{10,... | collective-permute-start | bytes 2359304 | tf_op jit(solution)/shard_map/ppermute | solution.py:49
  79.0 12.5 %collective-permute-start.17 = (bf16[48,4096]{1,0:T(8,128)(2,1)S(1)}, bf16[48,4096]{1,0:T(8,128)(2,1)S(1)}, u32[]{:S(2)}, u32[]{:S(2)}) collective-permute-start(bf16[48,4096]{1,0:T(8,128)(2,1)S(1)} %slice.121), channel_id=1, source_target_pairs={{0,2},{1,3},{2,0},{3,1},{4,6},{5,7},{6,4},{7,5},{8,10},{9,11},{10,... | collective-permute-start | bytes 1179656 | tf_op jit(solution)/shard_map/ppermute | solution.py:49
  80.7 10.8 %collective-permute-start.18 = (bf16[48,4096]{1,0:T(8,128)(2,1)S(1)}, bf16[48,4096]{1,0:T(8,128)(2,1)S(1)}, u32[]{:S(2)}, u32[]{:S(2)}) collective-permute-start(bf16[48,4096]{1,0:T(8,128)(2,1)S(1)} %slice.122), channel_id=1, source_target_pairs={{0,4},{1,5},{2,6},{3,7},{4,0},{5,1},{6,2},{7,3},{8,12},{9,13},{10,... | collective-permute-start | bytes 1179656 | tf_op jit(solution)/shard_map/ppermute | solution.py:49
  82.3 10.7 %collective-permute-start.20 = (bf16[96,4096]{1,0:T(8,128)(2,1)}, bf16[96,4096]{1,0:T(8,128)(2,1)}, u32[]{:S(2)}, u32[]{:S(2)}) collective-permute-start(bf16[96,4096]{1,0:T(8,128)(2,1)} %collective-permute-done.15.refs_1_), channel_id=1, source_target_pairs={{0,1},{1,0},{2,3},{3,2},{4,5},{5,4},{6,7},{7,6},{8,9},{9,8},{10,11... | collective-permute-start | bytes 2359304 | tf_op jit(solution)/shard_map/ppermute | solution.py:49
  82.3 10.7 %collective-permute-start.21 = (bf16[96,4096]{1,0:T(8,128)(2,1)}, bf16[96,4096]{1,0:T(8,128)(2,1)}, u32[]{:S(2)}, u32[]{:S(2)}) collective-permute-start(bf16[96,4096]{1,0:T(8,128)(2,1)} %collective-permute-done.16.refs_2_), channel_id=1, source_target_pairs={{0,1},{1,0},{2,3},{3,2},{4,5},{5,4},{6,7},{7,6},{8,9},{9,8},{10,11... | collective-permute-start | bytes 2359304 | tf_op jit(solution)/shard_map/ppermute | solution.py:49
  135.0 8.9 %collective-permute-start.27 = (bf16[48,2560]{1,0:T(8,128)(2,1)S(1)}, bf16[48,2560]{1,0:T(8,128)(2,1)S(1)}, u32[]{:S(2)}, u32[]{:S(2)}) collective-permute-start(bf16[48,2560]{1,0:T(8,128)(2,1)S(1)} %get-tuple-element.97), channel_id=1, source_target_pairs={{0,2},{1,3},{2,0},{3,1},{4,6},{5,7},{6,4},{7,5},{8,10},{9,11},{10,... | collective-permute-start | bytes 737288 | tf_op jit(solution)/shard_map/ppermute | solution.py:49
  136.5 8.8 %collective-permute-start.25 = (bf16[48,2560]{1,0:T(8,128)(2,1)S(1)}, bf16[48,2560]{1,0:T(8,128)(2,1)S(1)}, u32[]{:S(2)}, u32[]{:S(2)}) collective-permute-start(bf16[48,2560]{1,0:T(8,128)(2,1)S(1)} %get-tuple-element.99), channel_id=1, source_target_pairs={{0,4},{1,5},{2,6},{3,7},{4,0},{5,1},{6,2},{7,3},{8,12},{9,13},{10,... | collective-permute-start | bytes 737288 | tf_op jit(solution)/shard_map/ppermute | solution.py:49
  137.4 9.5 %collective-permute-start.31 = (bf16[48,1664]{1,0:T(8,128)(2,1)S(1)}, bf16[48,1664]{1,0:T(8,128)(2,1)S(1)}, u32[]{:S(2)}, u32[]{:S(2)}) collective-permute-start(bf16[48,1664]{1,0:T(8,128)(2,1)S(1)} %get-tuple-element.103), channel_id=1, source_target_pairs={{0,2},{1,3},{2,0},{3,1},{4,6},{5,7},{6,4},{7,5},{8,10},{9,11},{10,... | collective-permute-start | bytes 479240 | tf_op jit(solution)/shard_map/ppermute | solution.py:49
  138.8 9.5 %collective-permute-start.30 = (bf16[48,1664]{1,0:T(8,128)(2,1)S(1)}, bf16[48,1664]{1,0:T(8,128)(2,1)S(1)}, u32[]{:S(2)}, u32[]{:S(2)}) collective-permute-start(bf16[48,1664]{1,0:T(8,128)(2,1)S(1)} %get-tuple-element.105), channel_id=1, source_target_pairs={{0,4},{1,5},{2,6},{3,7},{4,0},{5,1},{6,2},{7,3},{8,12},{9,13},{10,... | collective-permute-start | bytes 479240 | tf_op jit(solution)/shard_map/ppermute | solution.py:49
  145.5 14.2 %collective-permute-start.26 = (bf16[96,2560]{1,0:T(8,128)(2,1)S(1)}, bf16[96,2560]{1,0:T(8,128)(2,1)S(1)}, u32[]{:S(2)}, u32[]{:S(2)}) collective-permute-start(bf16[96,2560]{1,0:T(8,128)(2,1)S(1)} %pad_maximum_fusion.1), channel_id=1, source_target_pairs={{0,2},{1,3},{2,0},{3,1},{4,6},{5,7},{6,4},{7,5},{8,10},{9,11},{10,... | collective-permute-start | bytes 1474568 | tf_op jit(solution)/shard_map/ppermute | solution.py:49
  146.2 14.2 %collective-permute-start.28 = (bf16[96,2560]{1,0:T(8,128)(2,1)S(1)}, bf16[96,2560]{1,0:T(8,128)(2,1)S(1)}, u32[]{:S(2)}, u32[]{:S(2)}) collective-permute-start(bf16[96,2560]{1,0:T(8,128)(2,1)S(1)} %pad_maximum_fusion.2), channel_id=1, source_target_pairs={{0,4},{1,5},{2,6},{3,7},{4,0},{5,1},{6,2},{7,3},{8,12},{9,13},{10,... | collective-permute-start | bytes 1474568 | tf_op jit(solution)/shard_map/ppermute | solution.py:49
  148.4 17.4 %collective-permute-start.35 = (bf16[96,1664]{1,0:T(8,128)(2,1)S(1)}, bf16[96,1664]{1,0:T(8,128)(2,1)S(1)}, u32[]{:S(2)}, u32[]{:S(2)}) collective-permute-start(bf16[96,1664]{1,0:T(8,128)(2,1)S(1)} %get-tuple-element.68), channel_id=1, source_target_pairs={{0,2},{1,3},{2,0},{3,1},{4,6},{5,7},{6,4},{7,5},{8,10},{9,11},{10,... | collective-permute-start | bytes 958472 | tf_op jit(solution)/shard_map/ppermute | solution.py:49
  148.8 16.9 %collective-permute-start.36 = (bf16[96,1664]{1,0:T(8,128)(2,1)S(1)}, bf16[96,1664]{1,0:T(8,128)(2,1)S(1)}, u32[]{:S(2)}, u32[]{:S(2)}) collective-permute-start(bf16[96,1664]{1,0:T(8,128)(2,1)S(1)} %get-tuple-element.76), channel_id=1, source_target_pairs={{0,4},{1,5},{2,6},{3,7},{4,0},{5,1},{6,2},{7,3},{8,12},{9,13},{10,... | collective-permute-start | bytes 958472 | tf_op jit(solution)/shard_map/ppermute | solution.py:49
  161.4 14.4 %collective-permute-start.33 = (bf16[24,2560]{1,0:T(8,128)(2,1)S(1)}, bf16[24,2560]{1,0:T(8,128)(2,1)S(1)}, u32[]{:S(2)}, u32[]{:S(2)}) collective-permute-start(bf16[24,2560]{1,0:T(8,128)(2,1)S(1)} %get-tuple-element.108), channel_id=1, source_target_pairs={{0,16},{1,17},{2,18},{3,19},{4,20},{5,21},{6,22},{7,23},{8,24},{9,... | collective-permute-start | bytes 368648 | tf_op jit(solution)/shard_map/ppermute | solution.py:49
  164.0 11.7 %collective-permute-start.34 = (bf16[24,2560]{1,0:T(8,128)(2,1)S(1)}, bf16[24,2560]{1,0:T(8,128)(2,1)S(1)}, u32[]{:S(2)}, u32[]{:S(2)}) collective-permute-start(bf16[24,2560]{1,0:T(8,128)(2,1)S(1)} %get-tuple-element.107), channel_id=1, source_target_pairs={{0,24},{1,25},{2,26},{3,27},{4,28},{5,29},{6,30},{7,31},{8,16},{9,... | collective-permute-start | bytes 368648 | tf_op jit(solution)/shard_map/ppermute | solution.py:49
  167.0 8.8 %collective-permute-start.39 = (bf16[24,1664]{1,0:T(8,128)(2,1)S(1)}, bf16[24,1664]{1,0:T(8,128)(2,1)S(1)}, u32[]{:S(2)}, u32[]{:S(2)}) collective-permute-start(bf16[24,1664]{1,0:T(8,128)(2,1)S(1)} %get-tuple-element.112), channel_id=1, source_target_pairs={{0,24},{1,25},{2,26},{3,27},{4,28},{5,29},{6,30},{7,31},{8,16},{9,... | collective-permute-start | bytes 239624 | tf_op jit(solution)/shard_map/ppermute | solution.py:49
  169.2 8.7 %collective-permute-start.38 = (bf16[24,1664]{1,0:T(8,128)(2,1)S(1)}, bf16[24,1664]{1,0:T(8,128)(2,1)S(1)}, u32[]{:S(2)}, u32[]{:S(2)}) collective-permute-start(bf16[24,1664]{1,0:T(8,128)(2,1)S(1)} %get-tuple-element.113), channel_id=1, source_target_pairs={{0,16},{1,17},{2,18},{3,19},{4,20},{5,21},{6,22},{7,23},{8,24},{9,... | collective-permute-start | bytes 239624 | tf_op jit(solution)/shard_map/ppermute | solution.py:49
  169.2 8.7 %collective-permute-start.37 = (bf16[24,1664]{1,0:T(8,128)(2,1)S(1)}, bf16[24,1664]{1,0:T(8,128)(2,1)S(1)}, u32[]{:S(2)}, u32[]{:S(2)}) collective-permute-start(bf16[24,1664]{1,0:T(8,128)(2,1)S(1)} %get-tuple-element.111), channel_id=1, source_target_pairs={{0,8},{1,9},{2,10},{3,11},{4,12},{5,13},{6,14},{7,15},{8,0},{9,1},... | collective-permute-start | bytes 239624 | tf_op jit(solution)/shard_map/ppermute | solution.py:49
  (26 other events, 208.7 us)
